TPU v7x, 512 devices: a whole 4x8x8 slice. The times are simulated.
512 devices in a mesh: gx: 32 (over x_lo, y, core), row: 16 (over x_hi, z).
Axes of the slice: x: 4 (x_hi: 2, x_lo: 2; x = x_hi * 2 + x_lo), y: 8, z: 8, core: 2. Of those that a mesh axis runs over, the one named last changes fastest.
Arguments:
- test_vectors: float32 [2, 5, 64, 256, 128], P(None, None, 'gx', 'row')
- base_coeffs: float32 [101, 64, 256], P(None, 'gx', 'row'), as said below
- panel_set: float32 [512, 10, 10], P(('gx', 'row')), as said below
- owner_index: int32 [1], replicated, may hold values from 0 to 511
Outputs:
- basis: float32 [2, 5, 64, 128, 256], P(None, None, 'gx', 'row')
Inputs may be any that keep to these rules, and one draw needn't show every extreme that they name: `owner_index`: the index, with gx slowest, of the device whose panel this window uses. `panel_set`: panels are nonsingular. `base_coeffs`: viscosities are positive.
All inputs are finite; a program needn't handle non-finite values.
Results may differ from a plain program's by a relative error of at most 0.0003.
Values sent between devices are 32-bit elements; how exact they have to be, the bound alone decides.
No kernel may reach another device: no remote copies, remote signals or barrier semaphores. Data moves between devices by JAX's collectives and lax.ppermute only.
A program may use at most 64 MiB of HBM per device.

v0:
```python
import math

import jax
import jax.numpy as jnp
from jax import lax
from jax.sharding import PartitionSpec as P

STEPS = 2


def spread(value, axis, source):
    kept = jnp.where(lax.axis_index(axis) == source, value, 0).astype(value.dtype)
    return lax.psum(kept, axis)


def with_halo(block, sides, width):
    for axis, dim in sides:
        count = lax.axis_size(axis)
        forward = [(i, i + 1) for i in range(count - 1)]
        backward = [(target, source) for source, target in forward]
        low = lax.ppermute(
            lax.slice_in_dim(block, block.shape[dim] - width, None, axis=dim), axis, forward
        )
        high = lax.ppermute(lax.slice_in_dim(block, 0, width, axis=dim), axis, backward)
        block = jnp.concatenate([low, block, high], axis=dim)
    return block


def advance(padded, coeffs):
    n_var = padded.shape[1]
    n_pair = n_var * n_var
    advect = coeffs[: 3 * n_pair].reshape((3, n_var, n_var) + coeffs.shape[1:])
    reaction = coeffs[3 * n_pair : 4 * n_pair].reshape((n_var, n_var) + coeffs.shape[1:])
    viscous = coeffs[4 * n_pair]
    fluxes = jnp.einsum("djixr,kjxrt->dkixrt", advect, padded, precision=lax.Precision.HIGHEST)
    centre = padded[:, :, 1:-1, 1:-1]
    stream = fluxes[0, :, :, 2:, 1:-1] - fluxes[0, :, :, :-2, 1:-1]
    radial = fluxes[1, :, :, 1:-1, 2:] - fluxes[1, :, :, 1:-1, :-2]
    beside_all = fluxes[2, :, :, 1:-1, 1:-1]
    azimuth = jnp.roll(beside_all, -1, axis=4) - jnp.roll(beside_all, 1, axis=4)
    neighbours = (
        padded[:, :, 2:, 1:-1]
        + padded[:, :, :-2, 1:-1]
        + padded[:, :, 1:-1, 2:]
        + padded[:, :, 1:-1, :-2]
    )
    neighbours = neighbours + jnp.roll(centre, -1, axis=4) + jnp.roll(centre, 1, axis=4)
    source = jnp.einsum(
        "jixr,kjxrt->kixrt", reaction[:, :, 1:-1, 1:-1], centre, precision=lax.Precision.HIGHEST
    )
    return (
        centre
        + stream
        + radial
        + azimuth
        + viscous[1:-1, 1:-1, None] * (neighbours - 6.0 * centre)
        + source
    )


def body(test_vectors, base_coeffs, panel_set, owner_index):
    panel_now = spread(panel_set[0], ("gx", "row"), owner_index[0])
    field = test_vectors
    count_x = lax.axis_size("gx")
    count_r = lax.axis_size("row")
    wide_x = field.shape[2]
    wide_r = field.shape[3]
    n_theta = field.shape[4]
    n_var = field.shape[1]
    n_vec = field.shape[0]
    coeff_rim = with_halo(base_coeffs, (("gx", 1), ("row", 2)), 1)
    for repeat in range(STEPS):
        padded = with_halo(field, (("gx", 2), ("row", 3)), 1)
        field = advance(padded, coeff_rim)
    sketch = jnp.dot(panel_now, field.reshape(n_vec * n_var, -1), precision=lax.Precision.HIGHEST)
    first = sketch[:n_var]
    second = sketch[n_var:]
    norm_one = lax.psum(jnp.sum(first * first), ("gx", "row"))
    inv_one = 1.0 / jnp.sqrt(norm_one)
    unit_one = first * inv_one
    projection = lax.psum(jnp.sum(unit_one * second), ("gx", "row"))
    remainder = second - projection * unit_one
    norm_two = lax.psum(jnp.sum(remainder * remainder), ("gx", "row"))
    inv_two = 1.0 / jnp.sqrt(norm_two)
    scale = math.sqrt(n_var * wide_x * count_x * wide_r * count_r * n_theta)
    weight_one = scale * inv_one
    weight_two = scale * inv_two
    weight_mix = -scale * inv_two * projection * inv_one
    block_shape = (n_var, wide_x, wide_r, n_theta)
    column_one = first.reshape(block_shape)
    column_two = second.reshape(block_shape)
    basis_local = jnp.stack(
        [weight_one * column_one, weight_two * column_two + weight_mix * column_one]
    )
    return lax.all_to_all(
        basis_local.transpose(0, 1, 2, 4, 3), "row", split_axis=3, concat_axis=4, tiled=True
    )


def solution(mesh):
    placed = (
        P(None, None, "gx", "row", None),
        P(None, "gx", "row"),
        P(("gx", "row"), None, None),
        P(),
    )
    return jax.shard_map(
        body,
        mesh=mesh,
        in_specs=placed,
        out_specs=P(None, None, "gx", "row", None),
        check_vma=False,
    )
```

profile of v0, /device:TPU:1, one launch (start us, length us, event | category | flops | bytes accessed | tf_op | source)
XLA Modules:
  0.0 480.5 jit_solution(10872169300837984554)
XLA Ops:
  1.1 4.6 collective-permute-start
  5.7 5.5 %collective-permute-start.1 = (f32[2,5,1,16,128]{4,1,0,3,2:T(8,128)S(1)}, f32[2,5,1,16,128]{4,1,0,3,2:T(8,128)S(1)}, u32[]{:S(2)}, u32[]{:S(2)}) collective-permute-start(f32[2,5,1,16,128]{4,1,0,3,2:T(8,128)S(1)} %get-tuple-element.29), channel_id=1, source_target_pairs={{16,0},{32,16},{48,32},{64,48},{80,64},{96,80},{112,96},{128,112},... | collective-permute-start | bytes 245768 | tf_op jit(solution)/shard_map/ppermute | solution.py:24
  11.9 1.9 collective-permute-start.4
  13.9 2.4 collective-permute-start.5
  17.2 1.6 collective-permute-done.5
  18.8 2.1 collective-permute-start.6
  22.3 107.3 %psum.28 = f32[10,10]{1,0:T(8,128)S(1)} all-reduce(f32[10,10]{1,0:T(8,128)S(1)} %fusion.42), channel_id=1, replica_groups=mesh['gx'=32,'row'=16] {'gx','row'}, use_global_device_ids=true, to_apply=%region_0.1 | all-reduce | flops 100 | bytes 800 | tf_op jit(solution)/shard_map/psum | solution.py:13
  129.8 2.5 collective-permute-start.2
  132.3 1.3 collective-permute-start.3
  135.2 1.8 collective-permute-done.3
  137.0 1.5 convolution_bitcast_fusion.1
  139.5 4.4 collective-permute-start.8
  143.9 1.9 collective-permute-start.9
  146.0 4.2 collective-permute-done.9
  150.2 3.4 collective-permute-start.10
  155.0 3.2 collective-permute-done.11
  158.2 1.5 convolution_bitcast_fusion
  161.8 105.5 %psum.29 = f32[]{:T(128)} all-reduce(f32[]{:T(128)} %multiply_reduce_fusion.2), channel_id=1, replica_groups=mesh['gx'=32,'row'=16] {'gx','row'}, use_global_device_ids=true, to_apply=%region_2.3 | all-reduce | flops 1 | bytes 8 | tf_op jit(solution)/shard_map/psum | solution.py:78
  268.7 94.1 %psum.30 = f32[]{:T(128)} all-reduce(f32[]{:T(128)} %multiply_reduce_fusion.1), channel_id=1, replica_groups=mesh['gx'=32,'row'=16] {'gx','row'}, use_global_device_ids=true, to_apply=%region_4.5 | all-reduce | flops 1 | bytes 8 | tf_op jit(solution)/shard_map/psum | solution.py:81
  362.7 1.3 multiply_bitcast_fusion
  364.1 94.3 %psum.31 = f32[]{:T(128)} all-reduce(f32[]{:T(128)} %get-tuple-element.10), channel_id=1, replica_groups=mesh['gx'=32,'row'=16] {'gx','row'}, use_global_device_ids=true, to_apply=%region_6.7 | all-reduce | flops 1 | bytes 8 | tf_op jit(solution)/shard_map/psum | solution.py:83
  461.1 1.8 reshape.70
  462.9 12.8 %all_to_all.18 = f32[16,1,2560]{2,1,0:T(1,128)S(1)} all-to-all(f32[16,1,2560]{2,1,0:T(1,128)S(1)} %reshape.70), channel_id=1, replica_groups=mesh['gx'=32,'row'=16] {'row'}, dimensions={0} | all-to-all | bytes 327680 | tf_op jit(solution)/shard_map/all_to_all | solution.py:95
  477.3 1.7 reshape.71
  (67 shorter events, 14.6 us)
Async XLA Ops:
  0.0 129.7 %copy-start = (f32[2,5,2,16,128]{4,3,2,1,0:T(8,128)S(1)}, f32[2,5,2,16,128]{4,3,2,1,0:T(8,128)}, u32[]{:S(2)}) copy-start(f32[2,5,2,16,128]{4,3,2,1,0:T(8,128)} %param.4) | copy-start | bytes 491524
  0.0 17.2 %copy-start.1 = (f32[101,2,16]{0,2,1:T(8,128)S(1)}, f32[101,2,16]{0,2,1:T(8,128)}, u32[]{:S(2)}) copy-start(f32[101,2,16]{0,2,1:T(8,128)} %param.5) | copy-start | bytes 38788
  0.0 22.3 %copy-start.2 = (f32[1,10,10]{2,0,1:T(1,128)S(1)}, f32[1,10,10]{2,0,1:T(1,128)}, u32[]{:S(2)}) copy-start(f32[1,10,10]{2,0,1:T(1,128)} %param.6) | copy-start | bytes 1204
  1.1 128.5 %collective-permute-start = (f32[2,5,1,16,128]{4,1,0,3,2:T(8,128)S(1)}, f32[2,5,1,16,128]{4,1,0,3,2:T(8,128)S(1)}, u32[]{:S(2)}, u32[]{:S(2)}) collective-permute-start(f32[2,5,1,16,128]{4,1,0,3,2:T(8,128)S(1)} %get-tuple-element.30), channel_id=1, source_target_pairs={{0,16},{16,32},{32,48},{48,64},{64,80},{80,96},{96,112},{112,128},... | collective-permute-start | bytes 245768 | tf_op jit(solution)/shard_map/ppermute | solution.py:21
  5.7 124.1 %collective-permute-start.1 = (f32[2,5,1,16,128]{4,1,0,3,2:T(8,128)S(1)}, f32[2,5,1,16,128]{4,1,0,3,2:T(8,128)S(1)}, u32[]{:S(2)}, u32[]{:S(2)}) collective-permute-start(f32[2,5,1,16,128]{4,1,0,3,2:T(8,128)S(1)} %get-tuple-element.29), channel_id=1, source_target_pairs={{16,0},{32,16},{48,32},{64,48},{80,64},{96,80},{112,96},{128,112},... | collective-permute-start | bytes 245768 | tf_op jit(solution)/shard_map/ppermute | solution.py:24
  11.9 5.3 %collective-permute-start.4 = (f32[101,1,16]{0,2,1:T(8,128)S(1)}, f32[101,1,16]{0,2,1:T(8,128)S(1)}, u32[]{:S(2)}, u32[]{:S(2)}) collective-permute-start(f32[101,1,16]{0,2,1:T(8,128)S(1)} %get-tuple-element.34), channel_id=1, source_target_pairs={{0,16},{16,32},{32,48},{48,64},{64,80},{80,96},{96,112},{112,128},... | collective-permute-start | bytes 19400 | tf_op jit(solution)/shard_map/ppermute | solution.py:21
  13.9 5.0 %collective-permute-start.5 = (f32[101,1,16]{0,2,1:T(8,128)S(1)}, f32[101,1,16]{0,2,1:T(8,128)S(1)}, u32[]{:S(2)}, u32[]{:S(2)}) collective-permute-start(f32[101,1,16]{0,2,1:T(8,128)S(1)} %get-tuple-element.33), channel_id=1, source_target_pairs={{16,0},{32,16},{48,32},{64,48},{80,64},{96,80},{112,96},{128,112},... | collective-permute-start | bytes 19400 | tf_op jit(solution)/shard_map/ppermute | solution.py:24
  18.8 110.8 %collective-permute-start.6 = (f32[101,4,1]{0,2,1:T(1,128)S(1)}, f32[101,4,1]{0,2,1:T(1,128)S(1)}, u32[]{:S(2)}, u32[]{:S(2)}) collective-permute-start(f32[101,4,1]{0,2,1:T(1,128)S(1)} %get-tuple-element.31), channel_id=1, source_target_pairs={{0,1},{1,2},{2,3},{3,4},{4,5},{5,6},{6,7},{7,8},{8,9},{9,10},{10,1... | collective-permute-start | bytes 4856 | tf_op jit(solution)/shard_map/ppermute | solution.py:21
  21.0 108.6 %collective-permute-start.7 = (f32[101,4,1]{0,2,1:T(1,128)S(1)}, f32[101,4,1]{0,2,1:T(1,128)S(1)}, u32[]{:S(2)}, u32[]{:S(2)}) collective-permute-start(f32[101,4,1]{0,2,1:T(1,128)S(1)} %get-tuple-element.32), channel_id=1, source_target_pairs={{1,0},{2,1},{3,2},{4,3},{5,4},{6,5},{7,6},{8,7},{9,8},{10,9},{11,1... | collective-permute-start | bytes 4856 | tf_op jit(solution)/shard_map/ppermute | solution.py:24
  129.8 5.3 %collective-permute-start.2 = (f32[2,5,4,1,128]{4,1,0,3,2:T(8,128)S(1)}, f32[2,5,4,1,128]{4,1,0,3,2:T(8,128)S(1)}, u32[]{:S(2)}, u32[]{:S(2)}) collective-permute-start(f32[2,5,4,1,128]{4,1,0,3,2:T(8,128)S(1)} %get-tuple-element.8), channel_id=1, source_target_pairs={{0,1},{1,2},{2,3},{3,4},{4,5},{5,6},{6,7},{7,8},{8,9},{9,10},{10,1... | collective-permute-start | bytes 61448 | tf_op jit(solution)/shard_map/ppermute | solution.py:21
  132.3 4.7 collective-permute-start.3
  139.5 6.5 %collective-permute-start.8 = (f32[2,5,1,16,128]{4,1,0,3,2:T(8,128)S(1)}, f32[2,5,1,16,128]{4,1,0,3,2:T(8,128)S(1)}, u32[]{:S(2)}, u32[]{:S(2)}) collective-permute-start(f32[2,5,1,16,128]{4,1,0,3,2:T(8,128)S(1)} %get-tuple-element.19), channel_id=1, source_target_pairs={{0,16},{16,32},{32,48},{48,64},{64,80},{80,96},{96,112},{112,128},... | collective-permute-start | bytes 245768 | tf_op jit(solution)/shard_map/ppermute | solution.py:21
  143.9 6.3 %collective-permute-start.9 = (f32[2,5,1,16,128]{4,1,0,3,2:T(8,128)S(1)}, f32[2,5,1,16,128]{4,1,0,3,2:T(8,128)S(1)}, u32[]{:S(2)}, u32[]{:S(2)}) collective-permute-start(f32[2,5,1,16,128]{4,1,0,3,2:T(8,128)S(1)} %get-tuple-element.20), channel_id=1, source_target_pairs={{16,0},{32,16},{48,32},{64,48},{80,64},{96,80},{112,96},{128,112},... | collective-permute-start | bytes 245768 | tf_op jit(solution)/shard_map/ppermute | solution.py:24
  150.2 4.8 %collective-permute-start.10 = (f32[2,5,4,1,128]{4,1,0,3,2:T(8,128)S(1)}, f32[2,5,4,1,128]{4,1,0,3,2:T(8,128)S(1)}, u32[]{:S(2)}, u32[]{:S(2)}) collective-permute-start(f32[2,5,4,1,128]{4,1,0,3,2:T(8,128)S(1)} %get-tuple-element.6), channel_id=1, source_target_pairs={{0,1},{1,2},{2,3},{3,4},{4,5},{5,6},{6,7},{7,8},{8,9},{9,10},{10,1... | collective-permute-start | bytes 61448 | tf_op jit(solution)/shard_map/ppermute | solution.py:21
  153.6 4.7 collective-permute-start.11
where the time goes:
time: 483 us; the launch traced here: 481 us
  blocking collectives  414 us (86%)
  starting transfers between devices  32.6 us (7%)
  local copies, waits for them, and re-layouts  11.6 us (2%)
  waiting for transfers between devices  10.9 us (2%)
    psum x1, blocking collectives, spread(): return lax.psum(kept, axis)  107 us
    psum x1, blocking collectives, body(): norm_one = lax.psum(jnp.sum(first * first), ('gx', 'row'))  106 us
    psum x1, blocking collectives, body(): norm_two = lax.psum(jnp.sum(remainder * remainder), ('gx', 'row'))  94.3 us
    psum x1, blocking collectives, body(): projection = lax.psum(jnp.sum(unit_one * second), ('gx', 'row'))  94.1 us
    ppermute x6, starting transfers between devices, with_halo(): lax.ppermute(lax.slice_in_dim(block, block.shape[dim] - width, None, axis...  18.9 us
    ppermute x6, starting transfers between devices, with_halo(): lax.ppermute(lax.slice_in_dim(block, 0, width, axis=dim), axis, backward)  13.7 us
    all_to_all x1, blocking collectives, body(): lax.all_to_all(basis_local.transpose(0, 1, 2, 4, 3), 'row', split_axis=3,...  12.8 us
    ppermute x6, waiting for transfers between devices, with_halo(): lax.ppermute(lax.slice_in_dim(block, 0, width, axis=dim), axis, backward)  10.8 us
  transfers between devices with their start and end apart: 12, of which 4 were waited for; matrix products, arithmetic and copies ran while one was open for 1% of the time, Pallas kernels for 0%

commit v1 on v0

v1 whole, which is shorter than its diff:
```python
import math

import jax
import jax.numpy as jnp
from jax import lax
from jax.sharding import PartitionSpec as P

STEPS = 2


def everyone(value, axis):
    count = lax.axis_size(axis)
    flat = value.reshape(1, 1, -1)
    sent = jnp.broadcast_to(flat, (count,) + flat.shape[1:])
    got = lax.all_to_all(sent, axis, 0, 0, tiled=True)
    return got.reshape((count,) + value.shape)


def with_halo(block, axis, dim, width):
    count = lax.axis_size(axis)
    forward = [(i, i + 1) for i in range(count - 1)]
    backward = [(target, source) for source, target in forward]
    low = lax.ppermute(
        lax.slice_in_dim(block, block.shape[dim] - width, None, axis=dim), axis, forward
    )
    high = lax.ppermute(lax.slice_in_dim(block, 0, width, axis=dim), axis, backward)
    return jnp.concatenate([low, block, high], axis=dim)


def advance(padded, coeffs):
    n_var = padded.shape[1]
    n_pair = n_var * n_var
    advect = coeffs[: 3 * n_pair].reshape((3, n_var, n_var) + coeffs.shape[1:])
    reaction = coeffs[3 * n_pair : 4 * n_pair].reshape((n_var, n_var) + coeffs.shape[1:])
    viscous = coeffs[4 * n_pair]
    fluxes = jnp.einsum("djixr,kjxrt->dkixrt", advect, padded, precision=lax.Precision.HIGHEST)
    centre = padded[:, :, 1:-1, 1:-1]
    stream = fluxes[0, :, :, 2:, 1:-1] - fluxes[0, :, :, :-2, 1:-1]
    radial = fluxes[1, :, :, 1:-1, 2:] - fluxes[1, :, :, 1:-1, :-2]
    beside_all = fluxes[2, :, :, 1:-1, 1:-1]
    azimuth = jnp.roll(beside_all, -1, axis=4) - jnp.roll(beside_all, 1, axis=4)
    neighbours = (
        padded[:, :, 2:, 1:-1]
        + padded[:, :, :-2, 1:-1]
        + padded[:, :, 1:-1, 2:]
        + padded[:, :, 1:-1, :-2]
    )
    neighbours = neighbours + jnp.roll(centre, -1, axis=4) + jnp.roll(centre, 1, axis=4)
    source = jnp.einsum(
        "jixr,kjxrt->kixrt", reaction[:, :, 1:-1, 1:-1], centre, precision=lax.Precision.HIGHEST
    )
    return (
        centre
        + stream
        + radial
        + azimuth
        + viscous[1:-1, 1:-1, None] * (neighbours - 6.0 * centre)
        + source
    )


def safe_ratio(cross, square):
    positive = square > 0
    return jnp.where(positive, cross / jnp.where(positive, square, 1.0), 0.0)


def merged(parts):
    square, cross, rest = parts[:, 0], parts[:, 1], parts[:, 2]
    square_all = jnp.sum(square)
    cross_all = jnp.sum(cross)
    shift = safe_ratio(cross, square) - safe_ratio(cross_all, square_all)
    return jnp.stack([square_all, cross_all, jnp.sum(rest + square * shift * shift)])


def body(test_vectors, base_coeffs, panel_set, owner_index):
    count_x = lax.axis_size("gx")
    count_r = lax.axis_size("row")
    n_vec, n_var, wide_x, wide_r, n_theta = test_vectors.shape
    here = lax.axis_index("gx") * count_r + lax.axis_index("row")
    panel = jnp.where(here == owner_index[0], panel_set[0], 0.0)
    panel = jnp.sum(everyone(panel, "row"), axis=0)
    panel = jnp.sum(everyone(panel, "gx"), axis=0)

    n_coeff = base_coeffs.shape[0]
    n_pair = n_vec * n_var
    field = test_vectors.reshape((n_pair, wide_x, wide_r, n_theta))
    turned = base_coeffs.transpose(1, 2, 0)
    turned = jnp.pad(turned, ((0, 0), (0, 0), (0, n_theta - n_coeff)))
    both = jnp.concatenate([field, turned[None]], axis=0)
    both = with_halo(both, "row", 2, 2)
    both = with_halo(both, "gx", 1, 2)
    coeffs = both[n_pair, :, :, :n_coeff].transpose(2, 0, 1)
    field = both[:n_pair].reshape((n_vec, n_var) + both.shape[1:])
    place_x = lax.axis_index("gx") * wide_x + jnp.arange(-1, wide_x + 1)
    place_r = lax.axis_index("row") * wide_r + jnp.arange(-1, wide_r + 1)
    inside = ((place_x >= 0) & (place_x < wide_x * count_x))[:, None, None] & (
        (place_r >= 0) & (place_r < wide_r * count_r)
    )[None, :, None]
    field = jnp.where(inside, advance(field, coeffs), 0.0)
    field = advance(field, coeffs[:, 1:-1, 1:-1])

    sketch = jnp.dot(panel, field.reshape(n_pair, -1), precision=lax.Precision.HIGHEST)
    first = sketch[:n_var]
    second = sketch[n_var:]
    square = jnp.sum(first * first)
    cross = jnp.sum(first * second)
    rest = second - safe_ratio(cross, square) * first
    triple = jnp.stack([square, cross, jnp.sum(rest * rest)])
    triple = merged(everyone(triple, "gx"))
    triple = merged(everyone(triple, "row"))
    inv_one = 1.0 / jnp.sqrt(triple[0])
    inv_two = 1.0 / jnp.sqrt(triple[2])
    projection = triple[1] * inv_one
    scale = math.sqrt(n_var * wide_x * count_x * wide_r * count_r * n_theta)

    turned = sketch.reshape(n_vec, n_var, wide_x, wide_r, n_theta).transpose(0, 1, 2, 4, 3)
    turned = lax.all_to_all(turned, "row", split_axis=3, concat_axis=4, tiled=True)
    one = (scale * inv_one) * turned[0]
    two = (scale * inv_two) * turned[1] - (scale * inv_two * projection * inv_one) * turned[0]
    return jnp.stack([one, two])


def solution(mesh):
    placed = (
        P(None, None, "gx", "row", None),
        P(None, "gx", "row"),
        P(("gx", "row"), None, None),
        P(),
    )
    return jax.shard_map(
        body,
        mesh=mesh,
        in_specs=placed,
        out_specs=P(None, None, "gx", "row", None),
        check_vma=False,
    )
```

time: 483 us -> 145 us (0.30)
  blocking collectives: 414 us -> 0 us
  local copies, waits for them, and re-layouts: 11.6 us -> 31.7 us
  starting transfers between devices: 32.6 us -> 52 us
  waiting for transfers between devices: 10.9 us -> 25.4 us
  matrix products: 4.67 us -> 13.1 us
  other arithmetic: 3.68 us -> 12 us
  between operations: 3.15 us -> 8.96 us
    psum x4 -> x0, blocking collectives: 401 us -> none  [the longest x1 107 us: spread(): return lax.psum(kept, axis)]
    all_to_all x0 -> x5, starting transfers between devices: none -> 39.4 us  [the longest x4 35.9 us: everyone(): got = lax.all_to_all(sent, axis, 0, 0, tiled=True)]
    all_to_all x0 -> x5, waiting for transfers between devices: none -> 25.4 us  [the longest x4 21.7 us: everyone(): got = lax.all_to_all(sent, axis, 0, 0, tiled=True)]
    all_to_all x1 -> x0, blocking collectives: 12.8 us -> none  [body(): lax.all_to_all(basis_local.transpose(0, 1, 2, 4, 3), 'row', split_axis=3,...]
    ppermute x6 -> x2, waiting for transfers between devices: 10.8 us -> 0.01 us  [with_halo(): lax.ppermute(lax.slice_in_dim(block, 0, width, axis=dim), axis, backward)]
    ppermute x6 -> x2, starting transfers between devices: 13.7 us -> 3.21 us  [with_halo(): lax.ppermute(lax.slice_in_dim(block, 0, width, axis=dim), axis, backward)]
    ppermute x6 -> x2, starting transfers between devices: 18.9 us -> 9.43 us  [with_halo(): lax.ppermute(lax.slice_in_dim(block, block.shape[dim] - width, None, axis...]
    unnamed x17 -> x19, local copies, waits for them, and re-layouts: 5.37 us -> 13.3 us
  transfers between devices with their start and end apart: 12 -> 9, of which waited for: 4 -> 5; matrix products, arithmetic and copies ran while one was open for 1% -> 5% of each run, Pallas kernels for 0% -> 0%
where the time goes in v1:
time: 145 us; the launch traced here: 143 us
  starting transfers between devices  52 us (36%)
  local copies, waits for them, and re-layouts  31.7 us (22%)
  waiting for transfers between devices  25.4 us (18%)
  matrix products  13.1 us (9%)
  other arithmetic  12 us (8%)
  between operations  8.96 us (6%)
    all_to_all x4, starting transfers between devices, everyone(): got = lax.all_to_all(sent, axis, 0, 0, tiled=True)  35.9 us
    all_to_all x4, waiting for transfers between devices, everyone(): got = lax.all_to_all(sent, axis, 0, 0, tiled=True)  21.7 us
    unnamed x19, local copies, waits for them, and re-layouts  13.3 us
    ppermute x2, starting transfers between devices, with_halo(): lax.ppermute(lax.slice_in_dim(block, block.shape[dim] - width, None, axis...  9.43 us
    dot_general x2, matrix products, advance(): jnp.einsum('jixr,kjxrt->kixrt', reaction[:, :, 1:-1, 1:-1], centre, preci...  8.21 us
    dot_general x2, matrix products, advance(): jnp.einsum('djixr,kjxrt->dkixrt', advect, padded, precision=lax.Precision...  4.3 us
    all_to_all x1, waiting for transfers between devices, body(): lax.all_to_all(turned, 'row', split_axis=3, concat_axis=4, tiled=True)  3.69 us
    all_to_all x1, starting transfers between devices, body(): lax.all_to_all(turned, 'row', split_axis=3, concat_axis=4, tiled=True)  3.52 us
  transfers between devices with their start and end apart: 9, of which 5 were waited for; matrix products, arithmetic and copies ran while one was open for 5% of the time, Pallas kernels for 0%

profile of v1, /device:TPU:1, one launch (start us, length us, event | category | flops | bytes accessed | tf_op | source)
XLA Modules:
  0.0 143.2 jit_solution(9297083442493135772)
XLA Ops:
  1.7 4.8 %collective-permute-start = (f32[11,2,2,128]{3,2,1,0:T(2,128)S(1)}, f32[11,2,2,128]{3,2,1,0:T(2,128)S(1)}, u32[]{:S(2)}, u32[]{:S(2)}) collective-permute-start(f32[11,2,2,128]{3,2,1,0:T(2,128)S(1)} %get-tuple-element.34), channel_id=1, source_target_pairs={{0,1},{1,2},{2,3},{3,4},{4,5},{5,6},{6,7},{7,8},{8,9},{9,10},{10,1... | collective-permute-start | bytes 67592 | tf_op jit(solution)/shard_map/ppermute | solution.py:23
  9.2 13.8 %all-to-all-start = ((f32[16,1,100]{2,1,0:T(1,128)}), f32[16,1,100]{2,1,0:T(1,128)S(1)}, u32[]{:S(2)}, u32[]{:S(2)}) async-start(f32[16,1,100]{2,1,0:T(1,128)} %broadcast_in_dim.52), calls=%async_computation | async-start | bytes 16384 | tf_op jit(solution)/shard_map/all_to_all | solution.py:15
  24.0 4.6 %collective-permute-start.2 = (f32[11,2,20,128]{3,2,1,0:T(8,128)S(1)}, f32[11,2,20,128]{3,2,1,0:T(8,128)S(1)}, u32[]{:S(2)}, u32[]{:S(2)}) collective-permute-start(f32[11,2,20,128]{3,2,1,0:T(8,128)S(1)} %pad_maximum_fusion.1), channel_id=1, source_target_pairs={{0,16},{16,32},{32,48},{48,64},{64,80},{80,96},{96,112},{112,128},... | collective-permute-start | bytes 675848 | tf_op jit(solution)/shard_map/ppermute | solution.py:23
  28.6 1.9 %collective-permute-start.3 = (f32[11,2,20,128]{3,2,1,0:T(8,128)S(1)}, f32[11,2,20,128]{3,2,1,0:T(8,128)S(1)}, u32[]{:S(2)}, u32[]{:S(2)}) collective-permute-start(f32[11,2,20,128]{3,2,1,0:T(8,128)S(1)} %pad_maximum_fusion.1), channel_id=1, source_target_pairs={{16,0},{32,16},{48,32},{64,48},{80,64},{96,80},{112,96},{128,112},... | collective-permute-start | bytes 675848 | tf_op jit(solution)/shard_map/ppermute | solution.py:26
  32.3 9.9 %all-to-all-start.1 = ((f32[32,1,100]{2,1,0:T(1,128)}), f32[32,1,100]{2,1,0:T(1,128)S(1)}, u32[]{:S(2)}, u32[]{:S(2)}) async-start(f32[32,1,100]{2,1,0:T(1,128)} %broadcast_in_dim.53), calls=%async_computation.1 | async-start | bytes 32768 | tf_op jit(solution)/shard_map/all_to_all | solution.py:15
  42.4 7.7 %all-to-all-done.1 = f32[32,1,100]{2,1,0:T(1,128)S(1)} async-done(((f32[32,1,100]{2,1,0:T(1,128)}), f32[32,1,100]{2,1,0:T(1,128)S(1)}, u32[]{:S(2)}, u32[]{:S(2)}) %all-to-all-start.1) | async-done | bytes 12832 | tf_op jit(solution)/shard_map/all_to_all | solution.py:15
  51.6 2.8 %convolution_bitcast_fusion = f32[3,2,5,6,20,128]{5,2,0,1,4,3:T(8,128)S(1)} fusion(f32[3,5,5,6,20,1]{1,2,0,5,4,3:T(8,128)S(1)} %copy.156, f32[2,5,6,20,128,1]{4,3,2,1,0,5:T(8,128)S(1)} %bitcast.168), kind=kOutput, calls=%fused_computation | convolution fusion | flops 27648000 | bytes 2493600 | tf_op jit(solution)/shard_map/djixr,kjxrt->dkixrt/dot_general | solution.py:36
  61.2 1.6 %copy.141 = f32[25,6,20]{2,1,0:T(8,128)} copy(f32[25,6,20]{0,2,1:T(8,128)} %slice.284) | data formatting | bytes 24000 | tf_op jit(solution)/shard_map/slice | solution.py:34
  62.8 1.6 %slice.285 = f32[5,5,4,18]{3,2,1,0:T(4,128)} slice(f32[5,5,6,20]{3,2,1,0:T(8,128)} %bitcast.184), slice={[0:5], [0:5], [1:5], [1:19]} | slice | bytes 14400 | tf_op jit(solution)/shard_map/slice | solution.py:50
  64.4 1.9 %copy.180 = f32[5,5,4,18]{0,1,3,2:T(8,128)} copy(f32[5,5,4,18]{3,2,1,0:T(4,128)} %slice.285) | data formatting | bytes 14400
  67.4 2.1 %copy.177 = f32[2,5,4,18,1]{4,1,0,3,2:T(8,128)} copy(f32[2,5,4,18,1]{4,3,2,1,0:T(8,128)} %get-tuple-element.19) | data formatting | bytes 5760
  72.4 6.2 %fusion.1 = f32[2,5,4,18,128]{4,1,0,3,2:T(8,128)S(1)} fusion(f32[2,5,4,18,128]{4,3,2,1,0:T(8,128)} %get-tuple-element.17, f32[3,2,5,6,20,128]{5,2,0,1,4,3:T(8,128)} %copy-done, f32[2,5,4,18,1]{4,1,0,3,2:T(8,128)} %get-tuple-element.27, f32[2,5,4,18,127]{4,1,0,3,2:T(8,128)} %get-tuple-element.29, f32[2,5,4,18,127]{4,1,0,3,2:T(8,128)} %get-tuple-element.28, ...), kind=kOutput, calls=%fused_computation.5 | convolution fusion | flops 7464960 | bytes 10199400 | tf_op jit(solution)/shard_map/jixr,kjxrt->kixrt/dot_general | solution.py:49
  78.7 1.5 %convolution_bitcast_fusion.1 = f32[3,2,5,4,18,128]{5,2,1,4,3,0:T(8,128)S(1)} fusion(f32[3,5,5,4,18,1]{1,2,5,4,3,0:T(8,128)S(1)} %copy.158, f32[2,5,4,18,128]{4,1,0,3,2:T(8,128)S(1)} %fusion.1), kind=kOutput, calls=%fused_computation.1 | convolution fusion | flops 16588800 | bytes 1496160 | tf_op jit(solution)/shard_map/djixr,kjxrt->dkixrt/dot_general | solution.py:36
  82.1 2.0 %fusion.2 = f32[2,5,2,16,128]{4,1,0,3,2:T(8,128)S(1)} fusion(f32[2,5,4,18,128]{4,1,0,3,2:T(8,128)S(1)} %fusion.1, f32[3,2,5,4,18,128]{5,2,1,4,3,0:T(8,128)} %copy-done.2, f32[2,5,2,16,1]{4,1,0,3,2:T(8,128)S(1)} %get-tuple-element.36, f32[2,5,2,16,127]{4,1,0,3,2:T(8,128)S(1)} %get-tuple-element.38, f32[2,5,2,16,127]{4,1,0,3,2:T(8,128)S(1)} %get-tuple-element.39, ...), kind=kOutput, calls=%fused_computation.7 | convolution fusion | flops 3276800 | bytes 4948992 | tf_op jit(solution)/shard_map/jixr,kjxrt->kixrt/dot_general | solution.py:49
  88.2 2.0 %pad_maximum_fusion.5 = f32[3]{0:T(128)S(1)} fusion(f32[1]{0:T(128)} %bitcast.34, f32[1]{0:T(128)} %bitcast.33, f32[1]{0:T(128)} %bitcast.32), kind=kLoop, calls=%fused_computation.82 | loop fusion | flops 6 | bytes 24 | tf_op jit(solution)/shard_map/stack | solution.py:108
  90.7 4.3 %all-to-all-start.2 = ((f32[32,1,3]{2,1,0:T(1,128)}), f32[32,1,3]{2,1,0:T(1,128)S(1)}, u32[]{:S(2)}, u32[]{:S(2)}) async-start(f32[32,1,3]{2,1,0:T(1,128)} %broadcast_in_dim.57), calls=%async_computation.2 | async-start | bytes 32768 | tf_op jit(solution)/shard_map/all_to_all | solution.py:15
  95.9 7.0 %all-to-all-done.2 = f32[32,1,3]{2,1,0:T(1,128)S(1)} async-done(((f32[32,1,3]{2,1,0:T(1,128)}), f32[32,1,3]{2,1,0:T(1,128)S(1)}, u32[]{:S(2)}, u32[]{:S(2)}) %all-to-all-start.2) | async-done | bytes 416 | tf_op jit(solution)/shard_map/all_to_all | solution.py:15
  106.3 2.0 %pad_maximum_fusion.6 = f32[3]{0:T(128)S(1)} fusion(f32[1]{0:T(128)} %bitcast.41, f32[1]{0:T(128)} %bitcast.37, f32[1]{0:T(128)} %bitcast.36), kind=kLoop, calls=%fused_computation.83 | loop fusion | flops 6 | bytes 24 | tf_op jit(solution)/shard_map/stack | solution.py:72
  108.9 7.9 %all-to-all-start.3 = ((f32[16,1,3]{2,1,0:T(1,128)}), f32[16,1,3]{2,1,0:T(1,128)S(1)}, u32[]{:S(2)}, u32[]{:S(2)}) async-start(f32[16,1,3]{2,1,0:T(1,128)} %broadcast_in_dim.59), calls=%async_computation.3 | async-start | bytes 16384 | tf_op jit(solution)/shard_map/all_to_all | solution.py:15
  117.2 2.5 %reshape.166 = f32[16,1,2560]{2,1,0:T(1,128)} reshape(f32[128,2,5,2,16]{4,3,2,1,0:T(2,128)S(1)} %bitcast_bitcast_fusion) | data formatting | bytes 327680
  119.7 5.9 %all-to-all-done.3 = f32[16,1,3]{2,1,0:T(1,128)S(1)} async-done(((f32[16,1,3]{2,1,0:T(1,128)}), f32[16,1,3]{2,1,0:T(1,128)S(1)}, u32[]{:S(2)}, u32[]{:S(2)}) %all-to-all-start.3) | async-done | bytes 224 | tf_op jit(solution)/shard_map/all_to_all | solution.py:15
  125.6 3.5 %all-to-all-start.4 = ((f32[16,1,2560]{2,1,0:T(1,128)}), f32[16,1,2560]{2,1,0:T(1,128)S(1)}, u32[]{:S(2)}, u32[]{:S(2)}) async-start(f32[16,1,2560]{2,1,0:T(1,128)} %reshape.166), calls=%async_computation.4 | async-start | bytes 327680 | tf_op jit(solution)/shard_map/all_to_all | solution.py:117
  134.4 3.7 %all-to-all-done.4 = f32[16,1,2560]{2,1,0:T(1,128)S(1)} async-done(((f32[16,1,2560]{2,1,0:T(1,128)}), f32[16,1,2560]{2,1,0:T(1,128)S(1)}, u32[]{:S(2)}, u32[]{:S(2)}) %all-to-all-start.4) | async-done | bytes 163872 | tf_op jit(solution)/shard_map/all_to_all | solution.py:117
  139.7 1.7 %reshape.167 = f32[128,2,5,2,16]{4,3,2,1,0:T(2,128)S(1)} reshape(f32[16,2560]{1,0:T(8,128)S(1)} %reduce.12) | data formatting | bytes 327680
  (82 shorter events, 31.4 us)
Async XLA Ops:
  1.7 21.3 %collective-permute-start = (f32[11,2,2,128]{3,2,1,0:T(2,128)S(1)}, f32[11,2,2,128]{3,2,1,0:T(2,128)S(1)}, u32[]{:S(2)}, u32[]{:S(2)}) collective-permute-start(f32[11,2,2,128]{3,2,1,0:T(2,128)S(1)} %get-tuple-element.34), channel_id=1, source_target_pairs={{0,1},{1,2},{2,3},{3,4},{4,5},{5,6},{6,7},{7,8},{8,9},{9,10},{10,1... | collective-permute-start | bytes 67592 | tf_op jit(solution)/shard_map/ppermute | solution.py:23
  6.5 16.5 %collective-permute-start.1 = (f32[11,2,2,128]{3,2,1,0:T(2,128)S(1)}, f32[11,2,2,128]{3,2,1,0:T(2,128)S(1)}, u32[]{:S(2)}, u32[]{:S(2)}) collective-permute-start(f32[11,2,2,128]{3,2,1,0:T(2,128)S(1)} %get-tuple-element.35), channel_id=1, source_target_pairs={{1,0},{2,1},{3,2},{4,3},{5,4},{6,5},{7,6},{8,7},{9,8},{10,9},{11,1... | collective-permute-start | bytes 67592 | tf_op jit(solution)/shard_map/ppermute | solution.py:26
  9.2 22.5 %all-to-all-start = ((f32[16,1,100]{2,1,0:T(1,128)}), f32[16,1,100]{2,1,0:T(1,128)S(1)}, u32[]{:S(2)}, u32[]{:S(2)}) async-start(f32[16,1,100]{2,1,0:T(1,128)} %broadcast_in_dim.52), calls=%async_computation | async-start | bytes 16384 | tf_op jit(solution)/shard_map/all_to_all | solution.py:15
  24.0 26.2 %collective-permute-start.2 = (f32[11,2,20,128]{3,2,1,0:T(8,128)S(1)}, f32[11,2,20,128]{3,2,1,0:T(8,128)S(1)}, u32[]{:S(2)}, u32[]{:S(2)}) collective-permute-start(f32[11,2,20,128]{3,2,1,0:T(8,128)S(1)} %pad_maximum_fusion.1), channel_id=1, source_target_pairs={{0,16},{16,32},{32,48},{48,64},{64,80},{80,96},{96,112},{112,128},... | collective-permute-start | bytes 675848 | tf_op jit(solution)/shard_map/ppermute | solution.py:23
  28.6 21.6 %collective-permute-start.3 = (f32[11,2,20,128]{3,2,1,0:T(8,128)S(1)}, f32[11,2,20,128]{3,2,1,0:T(8,128)S(1)}, u32[]{:S(2)}, u32[]{:S(2)}) collective-permute-start(f32[11,2,20,128]{3,2,1,0:T(8,128)S(1)} %pad_maximum_fusion.1), channel_id=1, source_target_pairs={{16,0},{32,16},{48,32},{64,48},{80,64},{96,80},{112,96},{128,112},... | collective-permute-start | bytes 675848 | tf_op jit(solution)/shard_map/ppermute | solution.py:26
  32.3 17.7 %all-to-all-start.1 = ((f32[32,1,100]{2,1,0:T(1,128)}), f32[32,1,100]{2,1,0:T(1,128)S(1)}, u32[]{:S(2)}, u32[]{:S(2)}) async-start(f32[32,1,100]{2,1,0:T(1,128)} %broadcast_in_dim.53), calls=%async_computation.1 | async-start | bytes 32768 | tf_op jit(solution)/shard_map/all_to_all | solution.py:15
  50.2 1.3 copy-start.1
  54.4 1.9 %copy-start = (f32[3,2,5,6,20,128]{5,2,0,1,4,3:T(8,128)}, f32[3,2,5,6,20,128]{5,2,0,1,4,3:T(8,128)S(1)}, u32[]{:S(2)}) copy-start(f32[3,2,5,6,20,128]{5,2,0,1,4,3:T(8,128)S(1)} %convolution_bitcast_fusion) | copy-start | bytes 5529604
  67.4 4.2 %copy-start.3 = (f32[75,4,18]{0,2,1:T(8,128)S(1)}, f32[75,4,18]{0,2,1:T(8,128)}, u32[]{:S(2)}) copy-start(f32[75,4,18]{0,2,1:T(8,128)} %slice.287) | copy-start | bytes 64804
  80.2 1.2 copy-start.2
  90.7 12.2 %all-to-all-start.2 = ((f32[32,1,3]{2,1,0:T(1,128)}), f32[32,1,3]{2,1,0:T(1,128)S(1)}, u32[]{:S(2)}, u32[]{:S(2)}) async-start(f32[32,1,3]{2,1,0:T(1,128)} %broadcast_in_dim.57), calls=%async_computation.2 | async-start | bytes 32768 | tf_op jit(solution)/shard_map/all_to_all | solution.py:15
  108.9 16.7 %all-to-all-start.3 = ((f32[16,1,3]{2,1,0:T(1,128)}), f32[16,1,3]{2,1,0:T(1,128)S(1)}, u32[]{:S(2)}, u32[]{:S(2)}) async-start(f32[16,1,3]{2,1,0:T(1,128)} %broadcast_in_dim.59), calls=%async_computation.3 | async-start | bytes 16384 | tf_op jit(solution)/shard_map/all_to_all | solution.py:15
  125.6 12.5 %all-to-all-start.4 = ((f32[16,1,2560]{2,1,0:T(1,128)}), f32[16,1,2560]{2,1,0:T(1,128)S(1)}, u32[]{:S(2)}, u32[]{:S(2)}) async-start(f32[16,1,2560]{2,1,0:T(1,128)} %reshape.166), calls=%async_computation.4 | async-start | bytes 327680 | tf_op jit(solution)/shard_map/all_to_all | solution.py:117

commit v2 on v1

v2 whole, which is shorter than its diff:
```python
import math

import jax
import jax.numpy as jnp
from jax import lax
from jax.experimental import pallas as pl
from jax.experimental.pallas import tpu as pltpu
from jax.sharding import PartitionSpec as P

STEPS = 2
RIM = 2
LANES = 128
ROWS = 8
RING = 12
HIGH, LOW, SIZE, PANEL = 64, 76, 88, 100


def two_sum(a, b):
    total = a + b
    part = total - a
    return total, (a - (total - part)) + (b - part)


def quick_two_sum(a, b):
    total = a + b
    return total, b - (total - a)


def split(a):
    wide = a * 4097.0
    high = wide - (wide - a)
    return high, a - high


def two_prod(a, b):
    product = a * b
    a_high, a_low = split(a)
    b_high, b_low = split(b)
    return product, ((a_high * b_high - product) + a_high * b_low + a_low * b_high) + a_low * b_low


def pair_add(a, b):
    high, low = two_sum(a[0], b[0])
    return quick_two_sum(high, low + (a[1] + b[1]))


def pair_mul(a, b):
    high, low = two_prod(a[0], b[0])
    return quick_two_sum(high, low + (a[0] * b[1] + a[1] * b[0]))


def pair_scale(a, factor):
    high, low = two_prod(a[0], factor)
    return quick_two_sum(high, low + a[1] * factor)


def pair_roll(a, shift, axis):
    size = a[0].shape[axis]
    return tuple(pltpu.roll(part, shift % size, axis) for part in a)


def pair_tree(pairs):
    while len(pairs) > 1:
        rest = [pairs[-1]] if len(pairs) % 2 else []
        pairs = [pair_add(pairs[i], pairs[i + 1]) for i in range(0, len(pairs) - 1, 2)] + rest
    return pairs[0]


def tree(parts, join):
    while len(parts) > 1:
        rest = [parts[-1]] if len(parts) % 2 else []
        parts = [join(parts[i], parts[i + 1]) for i in range(0, len(parts) - 1, 2)] + rest
    return parts[0]


def lanes_of(shape):
    return lax.broadcasted_iota(jnp.int32, shape, 1)


def roll_lanes(value, shift):
    return pltpu.roll(value, shift % LANES, 1)


def safe_inverse(value):
    positive = value > 0
    return jnp.where(positive, 1.0 / jnp.where(positive, value, 1.0), 0.0)


def merge(tiles):
    size = tree(tiles, jnp.maximum)
    inverse = safe_inverse(size)
    scaled = []
    for tile in tiles:
        ratio = tile * inverse
        ratio = roll_lanes(ratio * ratio, HIGH - SIZE)
        scaled.append(pair_scale((tile, roll_lanes(tile, HIGH - LOW)), ratio))
    return pair_tree(scaled), size, tree(tiles, jnp.add)


def placed_at(lane, start, width, value, other):
    return jnp.where((lane >= start) & (lane < start + width), value, other)


def pack_stats(pair, size, panel):
    lane = lanes_of(size.shape)
    tile = placed_at(lane, HIGH, RING, pair[0], 0.0)
    tile = placed_at(lane, LOW, RING, roll_lanes(pair[1], LOW - HIGH), tile)
    tile = placed_at(lane, SIZE, RING, size, tile)
    return jnp.where(lane >= PANEL, panel, tile)


def march_kernel(
    n_var, wide_x, wide_r, count_x, count_r,
    place_ref, low_ref, mid_ref, high_ref, panel_ref,
    out_ref, rows_ref, now_ref, next_ref, coeff_ref, packed_ref, parts_ref,
):
    n_plane = low_ref.shape[0] - 1
    n_theta = low_ref.shape[-1]
    n_tile = n_theta // ROWS
    deep = wide_r + 2 * RIM
    n_pair = n_var * n_var
    used = (wide_x + 2 * RIM) * deep

    for plane in range(n_plane + 1):
        blocks = [low_ref[plane, x] for x in range(RIM)]
        blocks += [mid_ref[plane, x] for x in range(wide_x)]
        blocks += [high_ref[plane, x] for x in range(RIM)]
        for x, block in enumerate(blocks):
            rows_ref[plane, x * deep : (x + 1) * deep, :] = block
        rows_ref[plane, used:LANES, :] = jnp.zeros((LANES - used, n_theta), jnp.float32)
    for plane in range(n_plane):
        turned = rows_ref[plane].T
        now_ref[plane, ROWS : ROWS + n_theta, :] = turned
        now_ref[plane, ROWS - 1 : ROWS, :] = turned[n_theta - 1 :]
        now_ref[plane, ROWS + n_theta : ROWS + n_theta + 1, :] = turned[:1]
    coeff_ref[: n_theta, :] = rows_ref[n_plane].T
    viscous = coeff_ref[4 * n_pair : 4 * n_pair + 1, :]
    for i in range(n_var):
        own = 3 * n_pair + i * n_var + i
        coeff_ref[own : own + 1, :] = coeff_ref[own : own + 1, :] + (1.0 - 6.0 * viscous)
    for n, shift in enumerate((deep, -deep, 1, -1)):
        coeff_ref[n_theta + n : n_theta + n + 1, :] = roll_lanes(viscous, shift)

    lane = lanes_of((ROWS, LANES))
    at_x = lane // deep - RIM + place_ref[0] * wide_x
    at_r = lane % deep - RIM + place_ref[1] * wide_r
    inside = (at_x >= 0) & (at_x < wide_x * count_x) & (at_r >= 0) & (at_r < wide_r * count_r)
    inside = inside & (lane < used)

    def coeff(index):
        return coeff_ref[index : index + 1, :]

    def advance(source_ref, tile):
        start = ROWS + tile * ROWS
        centre = [source_ref[b, pl.ds(start, ROWS), :] for b in range(n_plane)]
        before = [source_ref[b, pl.ds(start - 1, ROWS), :] for b in range(n_plane)]
        after = [source_ref[b, pl.ds(start + 1, ROWS), :] for b in range(n_plane)]
        differ = [a - b for a, b in zip(after, before)]
        both = [a + b for a, b in zip(after, before)]
        result = [None] * n_plane
        for i in range(n_var):
            for k in range(0, n_plane, n_var):
                stream = radial = local = 0.0
                for j in range(n_var):
                    at = j * n_var + i
                    stream = stream + coeff(at) * centre[k + j]
                    radial = radial + coeff(n_pair + at) * centre[k + j]
                    local = local + coeff(2 * n_pair + at) * differ[k + j]
                    local = local + coeff(3 * n_pair + at) * centre[k + j]
                own = centre[k + i]
                local = local + coeff(4 * n_pair) * both[k + i]
                local = local + roll_lanes(coeff(n_theta) * own + stream, -deep)
                local = local + roll_lanes(coeff(n_theta + 1) * own - stream, deep)
                local = local + roll_lanes(coeff(n_theta + 2) * own + radial, -1)
                local = local + roll_lanes(coeff(n_theta + 3) * own - radial, 1)
                result[k + i] = local
        return result

    def first_step(tile, carry):
        result = advance(now_ref, tile)
        for b in range(n_plane):
            next_ref[b, pl.ds(ROWS + tile * ROWS, ROWS), :] = jnp.where(inside, result[b], 0.0)
        return carry

    lax.fori_loop(0, n_tile, first_step, 0)
    for b in range(n_plane):
        next_ref[b, ROWS - 1 : ROWS, :] = next_ref[b, ROWS + n_theta - 1 : ROWS + n_theta, :]
        next_ref[b, ROWS + n_theta : ROWS + n_theta + 1, :] = next_ref[b, ROWS : ROWS + 1, :]

    group = wide_x * wide_r
    per_vreg = LANES // group
    n_wide = packed_ref.shape[-1] // LANES

    def second_step(tile, largest):
        result = advance(next_ref, tile)
        for v in range(n_wide):
            packed = jnp.zeros((ROWS, LANES), jnp.float32)
            for b in range(v * per_vreg, min((v + 1) * per_vreg, n_plane)):
                for x in range(wide_x):
                    target = (b % per_vreg) * group + x * wide_r
                    shift = target - ((x + RIM) * deep + RIM)
                    packed = placed_at(lane, target, wide_r, roll_lanes(result[b], shift), packed)
            packed_ref[tile, :, v * LANES : (v + 1) * LANES] = packed
            largest = jnp.maximum(largest, jnp.abs(packed))
        return largest

    largest = lax.fori_loop(0, n_tile, second_step, jnp.zeros((ROWS, LANES), jnp.float32))
    largest = jnp.max(largest, axis=1, keepdims=True)
    largest = jnp.max(largest, axis=0, keepdims=True)
    inverse = safe_inverse(jnp.broadcast_to(largest, (ROWS, LANES)))
    largest = jnp.broadcast_to(largest, (ROWS, LANES))

    for tile in range(n_tile):
        for v in range(n_wide):
            high, low = split(packed_ref[tile, :, v * LANES : (v + 1) * LANES] * inverse)
            parts_ref[0, tile, v] = high
            parts_ref[1, tile, v] = low

    def shifted(part, tile, v, s):
        whole, rest = divmod(s, per_vreg)
        value = parts_ref[part, tile, (v + whole) % n_wide]
        if not rest:
            return value
        other = parts_ref[part, tile, (v + whole + 1) % n_wide]
        keep = lane < LANES - rest * group
        return jnp.where(keep, roll_lanes(value, -rest * group), roll_lanes(other, -rest * group))

    pairs = [[None] * n_wide for _ in range(ROWS)]
    zero = jnp.zeros((ROWS, LANES), jnp.float32)
    for s in range(RING // 2 + 1):
        for v in range(n_wide):
            total, error = zero, zero
            for tile in range(n_tile):
                a_high, a_low = parts_ref[0, tile, v], parts_ref[1, tile, v]
                if s:
                    b_high, b_low = shifted(0, tile, v, s), shifted(1, tile, v, s)
                    minor = a_high * b_low + a_low * b_high
                else:
                    b_high, b_low = a_high, a_low
                    minor = 2.0 * a_high * a_low
                total, lost = two_sum(total, a_high * b_high)
                error = error + (lost + (minor + a_low * b_low))
            pairs[s][v] = quick_two_sum(total, error)
    row = lax.broadcasted_iota(jnp.int32, (ROWS, LANES), 0)
    sums = []
    for v in range(n_wide):
        level = [pairs[s][v] if s <= RING // 2 else (zero, zero) for s in range(ROWS)]
        half = ROWS // 2
        while half:
            joined = []
            for s in range(half):
                a, b = level[s], level[s + half]
                front = (row // half) % 2 == 0
                a_turned, b_turned = pair_roll(a, -half, 0), pair_roll(b, half, 0)
                one = tuple(jnp.where(front, p, q) for p, q in zip(a, b_turned))
                two = tuple(jnp.where(front, p, q) for p, q in zip(a_turned, b))
                joined.append(pair_add(one, two))
            level = joined
            half //= 2
        sums.append(level[0])
    step = group // 2
    while step:
        sums = [pair_add(a, pair_roll(a, -step, 1)) for a in sums]
        step //= 2
    gathered = (zero, zero)
    for b in range(RING):
        turned = pair_roll(sums[b // per_vreg], HIGH + b - (b % per_vreg) * group, 1)
        gathered = tuple(jnp.where(lane == HIGH + b, p, q) for p, q in zip(turned, gathered))
    stats = pack_stats(gathered, largest, panel_ref[...])
    last = (n_wide - 1) * LANES
    for tile in range(n_tile):
        out_ref[tile, :, :last] = packed_ref[tile, :, :last]
        out_ref[tile, :, last:] = jnp.where(lane < HIGH, packed_ref[tile, :, last:], stats)


def reduce_kernel(got_ref, out_ref):
    count, _, wide = got_ref.shape
    pair, size, panel = merge([got_ref[n, :, wide - LANES :] for n in range(count)])
    tile = pack_stats(pair, size, panel)
    for n in range(out_ref.shape[0]):
        out_ref[n] = tile


def relay_kernel(n_plane, wide_x, wide_r, got_ref, out_ref):
    count = got_ref.shape[0]
    per_vreg = LANES // wide_r
    lane = lanes_of((ROWS, LANES))
    for g in range(n_plane * wide_x):
        v, slot = divmod(g, per_vreg)
        for half in range(count // per_vreg):
            value = jnp.zeros((ROWS, LANES), jnp.float32)
            for n in range(per_vreg):
                source = got_ref[half * per_vreg + n, :, v * LANES : (v + 1) * LANES]
                turned = roll_lanes(source, (n - slot) * wide_r)
                value = placed_at(lane, n * wide_r, wide_r, turned, value)
            out_ref[g, :, half * LANES : (half + 1) * LANES] = value


def final_kernel(n_var, wide_x, scale, got_ref, cells_ref, out_ref, weight_ref):
    n_plane = 2 * n_var
    tiles = [got_ref[n] for n in range(got_ref.shape[0])]
    pair, size, tile = merge(tiles)
    lane = lanes_of((ROWS, LANES))
    row = lax.broadcasted_iota(jnp.int32, (ROWS, LANES), 0)
    live = row < n_var
    one = jnp.where(live & (lane < n_plane), roll_lanes(tile, -PANEL), 0.0)
    two = jnp.where(live & (lane < n_plane), roll_lanes(tile, -PANEL - n_plane), 0.0)
    left = one + roll_lanes(one, RING) + roll_lanes(two, 2 * RING)
    right = one + roll_lanes(two, RING) + roll_lanes(two, 2 * RING)
    inner = []
    for part in pair:
        at = jnp.where(lane < RING, roll_lanes(part, -HIGH), 0.0)
        inner.append(at + roll_lanes(at, RING) + roll_lanes(at, 2 * RING))
    place = lane % RING

    def turned(value, s):
        if not s:
            return value
        return jnp.where(place < RING - s, roll_lanes(value, -s), roll_lanes(value, RING - s))

    terms = []
    for s in range(RING // 2 + 1):
        left_s, right_s = turned(left, s), turned(right, s)
        term = pair_add(two_prod(left, right_s), two_prod(left_s, right))
        share = 1.0 if s % (RING // 2) else 0.5
        row_s = tuple(share * part[s : s + 1, :] for part in inner)
        terms.append(pair_mul(term, row_s))
    total = pair_tree(terms)
    for shift in (4, 2, 1):
        total = pair_add(total, pair_roll(total, shift, 0))
    total = pair_add(total, pair_roll(total, -RING // 2, 1))
    total = pair_add(total, pair_roll(total, -RING // 4, 1))
    total = pair_tree([total, pair_roll(total, -1, 1), pair_roll(total, -2, 1)])

    def everywhere(part, at):
        return jnp.broadcast_to(part[:, at : at + 1], (ROWS, LANES))

    square, cross, other = (
        tuple(everywhere(part, g * RING) for part in total) for g in range(3)
    )
    ratio = cross[0] / square[0]
    left_over = pair_add(cross, tuple(-p for p in pair_scale(square, ratio)))
    ratio = quick_two_sum(ratio, left_over[0] / square[0])
    rest = pair_add(other, tuple(-p for p in pair_mul(cross, ratio)))
    largest = everywhere(size, SIZE)
    inv_one = scale / jnp.sqrt(square[0]) / largest
    inv_two = scale / jnp.sqrt(rest[0]) / largest
    weight_ref[:ROWS, :] = inv_one * one
    weight_ref[ROWS:, :] = inv_two * two - (inv_two * ratio[0]) * one

    for a in range(n_plane):
        at = (a // n_var) * ROWS + a % n_var
        weights = jnp.broadcast_to(weight_ref[at : at + 1, :], (ROWS, LANES))
        spread = [everywhere(weights, b) for b in range(n_plane)]
        for x in range(wide_x):
            for h in range(cells_ref.shape[-1] // LANES):
                cut = slice(h * LANES, (h + 1) * LANES)
                value = spread[0] * cells_ref[x, :, cut]
                for b in range(1, n_plane):
                    value = value + spread[b] * cells_ref[b * wide_x + x, :, cut]
                out_ref[a * wide_x + x, :, cut] = value


VMEM = pl.BlockSpec(memory_space=pltpu.VMEM)
PARAMS = pltpu.CompilerParams(vmem_limit_bytes=32 * 1024 * 1024)


def with_halo(block, axis, dim, width):
    count = lax.axis_size(axis)
    forward = [(i, i + 1) for i in range(count - 1)]
    backward = [(target, source) for source, target in forward]
    low = lax.ppermute(
        lax.slice_in_dim(block, block.shape[dim] - width, None, axis=dim), axis, forward
    )
    high = lax.ppermute(lax.slice_in_dim(block, 0, width, axis=dim), axis, backward)
    return low, high


def body(test_vectors, base_coeffs, panel_set, owner_index):
    count_x = lax.axis_size("gx")
    count_r = lax.axis_size("row")
    n_vec, n_var, wide_x, wide_r, n_theta = test_vectors.shape
    n_coeff = base_coeffs.shape[0]
    n_plane = n_vec * n_var
    at_x, at_r = lax.axis_index("gx"), lax.axis_index("row")

    panel = panel_set[0] / jnp.max(jnp.abs(panel_set[0]))
    panel = jnp.where(at_x * count_r + at_r == owner_index[0], panel, 0.0)
    panel = jnp.concatenate([panel[:n_var], panel[n_var:]], axis=1)
    panel = jnp.pad(panel, ((0, ROWS - n_var), (PANEL, LANES - PANEL - 2 * n_plane)))

    field = test_vectors.reshape((n_plane, wide_x, wide_r, n_theta))
    turned = base_coeffs.transpose(1, 2, 0)
    turned = jnp.pad(turned, ((0, 0), (0, 0), (0, n_theta - n_coeff)))
    both = jnp.concatenate([field, turned[None]], axis=0)
    low, high = with_halo(both, "row", 2, RIM)
    both = jnp.concatenate([low, both, high], axis=2)
    low, high = with_halo(both, "gx", 1, RIM)

    n_wide = 3
    n_tile = n_theta // ROWS
    sent = pl.pallas_call(
        lambda *refs: march_kernel(n_var, wide_x, wide_r, count_x, count_r, *refs),
        out_shape=jax.ShapeDtypeStruct((n_tile, ROWS, n_wide * LANES), jnp.float32),
        in_specs=[pl.BlockSpec(memory_space=pltpu.SMEM)] + [VMEM] * 4,
        out_specs=VMEM,
        scratch_shapes=[
            pltpu.VMEM((n_plane + 1, LANES, n_theta), jnp.float32),
            pltpu.VMEM((n_plane, n_theta + 2 * ROWS, LANES), jnp.float32),
            pltpu.VMEM((n_plane, n_theta + 2 * ROWS, LANES), jnp.float32),
            pltpu.VMEM((n_theta + ROWS, LANES), jnp.float32),
            pltpu.VMEM((n_tile, ROWS, n_wide * LANES), jnp.float32),
            pltpu.VMEM((2, n_tile, n_wide, ROWS, LANES), jnp.float32),
        ],
        compiler_params=PARAMS,
        name="march",
    )(jnp.stack([at_x, at_r]), low, both, high, panel)
    got = lax.all_to_all(sent, "row", 0, 0, tiled=True)
    stats = pl.pallas_call(
        reduce_kernel,
        out_shape=jax.ShapeDtypeStruct((count_x, ROWS, LANES), jnp.float32),
        in_specs=[VMEM],
        out_specs=VMEM,
        compiler_params=PARAMS,
        name="reduce",
    )(got)
    stats = lax.all_to_all(stats, "gx", 0, 0, tiled=True)
    cells = pl.pallas_call(
        lambda *refs: relay_kernel(n_plane, wide_x, wide_r, *refs),
        out_shape=jax.ShapeDtypeStruct((n_plane * wide_x, ROWS, count_r * wide_r), jnp.float32),
        in_specs=[VMEM],
        out_specs=VMEM,
        compiler_params=PARAMS,
        name="relay",
    )(got)
    scale = math.sqrt(n_var * wide_x * count_x * wide_r * count_r * n_theta)
    basis = pl.pallas_call(
        lambda *refs: final_kernel(n_var, wide_x, scale, *refs),
        out_shape=jax.ShapeDtypeStruct(cells.shape, jnp.float32),
        in_specs=[VMEM, VMEM],
        out_specs=VMEM,
        scratch_shapes=[pltpu.VMEM((2 * ROWS, LANES), jnp.float32)],
        compiler_params=PARAMS,
        name="final",
    )(stats, cells)
    return basis.reshape((n_vec, n_var, wide_x, n_theta // count_r, count_r * wide_r))


def solution(mesh):
    placed = (
        P(None, None, "gx", "row", None),
        P(None, "gx", "row"),
        P(("gx", "row"), None, None),
        P(),
    )
    return jax.shard_map(
        body,
        mesh=mesh,
        in_specs=placed,
        out_specs=P(None, None, "gx", "row", None),
        check_vma=False,
    )
```

time: 145 us -> 73.5 us (0.51)
  local copies, waits for them, and re-layouts: 31.7 us -> 0.79 us
  starting transfers between devices: 52 us -> 25.1 us
  blocking collectives: 0 us -> 19.8 us
  matrix products: 13.1 us -> 0 us
  waiting for transfers between devices: 25.4 us -> 13.7 us
  Pallas kernels: 0 us -> 10.4 us
  other arithmetic: 12 us -> 2.5 us
  between operations: 8.96 us -> 0.75 us
    all_to_all x5 -> x1, starting transfers between devices: 39.4 us -> 11.3 us  [body(): stats = lax.all_to_all(stats, 'gx', 0, 0, tiled=True)]
    all_to_all x0 -> x1, blocking collectives: none -> 19.8 us  [body(): got = lax.all_to_all(sent, 'row', 0, 0, tiled=True)]
    all_to_all x5 -> x1, waiting for transfers between devices: 25.4 us -> 8.7 us  [body(): stats = lax.all_to_all(stats, 'gx', 0, 0, tiled=True)]
    unnamed x19 -> x4, local copies, waits for them, and re-layouts: 13.3 us -> 0.03 us
    dot_general x5 -> x0, matrix products: 13.1 us -> none  [the longest x2 8.21 us: advance(): jnp.einsum('jixr,kjxrt->kixrt', reaction[:, :, 1:-1, 1:-1], centre, preci...]
    slice x21 -> x1, local copies, waits for them, and re-layouts: 10.8 us -> 0.01 us  [body(): panel = jnp.concatenate([panel[:n_var], panel[n_var:]], axis=1)]
    pallas_call x0 -> x4, Pallas kernels: none -> 10.4 us  [the longest x1 7.43 us: body(): pl.pallas_call(lambda *refs: march_kernel(n_var, wide_x, wide_r, count_x,...]
    another operation x3 -> x1, other arithmetic: 4.61 us -> 0.08 us  [body(): jnp.stack([at_x, at_r])]
  transfers between devices with their start and end apart: 9 -> 5, of which waited for: 5 -> 4; matrix products, arithmetic and copies ran while one was open for 5% -> 2% of each run, Pallas kernels for 0% -> 0%
where the time goes in v2:
time: 73.5 us; the launch traced here: 73 us
  starting transfers between devices  25.1 us (34%)
  blocking collectives  19.8 us (27%)
  waiting for transfers between devices  13.7 us (19%)
  Pallas kernels  10.4 us (14%)
  other arithmetic  2.5 us (3%)
  local copies, waits for them, and re-layouts  0.79 us (1%)
  between operations  0.75 us (1%)
    all_to_all x1, blocking collectives, body(): got = lax.all_to_all(sent, 'row', 0, 0, tiled=True)  19.8 us
    all_to_all x1, starting transfers between devices, body(): stats = lax.all_to_all(stats, 'gx', 0, 0, tiled=True)  11.3 us
    all_to_all x1, waiting for transfers between devices, body(): stats = lax.all_to_all(stats, 'gx', 0, 0, tiled=True)  8.7 us
    pallas_call x1, Pallas kernels, body(): pl.pallas_call(lambda *refs: march_kernel(n_var, wide_x, wide_r, count_x,...  7.43 us
    ppermute x2, starting transfers between devices, with_halo(): lax.ppermute(lax.slice_in_dim(block, 0, width, axis=dim), axis, backward)  7.05 us
    ppermute x2, starting transfers between devices, with_halo(): lax.ppermute(lax.slice_in_dim(block, block.shape[dim] - width, None, axis...  6.75 us
    ppermute x2, waiting for transfers between devices, with_halo(): lax.ppermute(lax.slice_in_dim(block, 0, width, axis=dim), axis, backward)  3 us
    ppermute x2, waiting for transfers between devices, with_halo(): lax.ppermute(lax.slice_in_dim(block, block.shape[dim] - width, None, axis...  2.03 us
  transfers between devices with their start and end apart: 5, of which 4 were waited for; matrix products, arithmetic and copies ran while one was open for 2% of the time, Pallas kernels for 0%

profile of v2, /device:TPU:1, one launch (start us, length us, event | category | flops | bytes accessed | tf_op | source)
XLA Modules:
  0.0 73.0 jit_solution(12330686656334083497)
XLA Ops:
  0.0 0.8 %pad_bitcast_fusion = f32[1,2,16,128]{3,2,1,0:T(8,128)S(1)} fusion(f32[2,16,101]{2,1,0:T(8,128)} %bitcast.15), kind=kLoop, calls=%fused_computation.3 | loop fusion | bytes 29312 | tf_op jit(solution)/shard_map/broadcast_in_dim | solution.py:395
  0.8 0.9 %pad_maximum_fusion.2 = (f32[11,2,2,128]{3,2,1,0:T(2,128)S(1)}, f32[11,2,2,128]{3,2,1,0:T(2,128)S(1)}) fusion(f32[1,2,16,128]{3,2,1,0:T(8,128)S(1)} %pad_bitcast_fusion, f32[10,2,16,128]{3,2,1,0:T(8,128)} %bitcast.13), kind=kLoop, calls=%fused_computation.2 | loop fusion | flops 11264 | bytes 225280 | tf_op jit(solution)/shard_map/slice | solution.py:373
  1.7 4.8 %collective-permute-start = (f32[11,2,2,128]{3,2,1,0:T(2,128)S(1)}, f32[11,2,2,128]{3,2,1,0:T(2,128)S(1)}, u32[]{:S(2)}, u32[]{:S(2)}) collective-permute-start(f32[11,2,2,128]{3,2,1,0:T(2,128)S(1)} %get-tuple-element.5), channel_id=1, source_target_pairs={{0,1},{1,2},{2,3},{3,4},{4,5},{5,6},{6,7},{7,8},{8,9},{9,10},{10,1... | collective-permute-start | bytes 67592 | tf_op jit(solution)/shard_map/ppermute | solution.py:372
  6.5 1.3 %collective-permute-start.1 = (f32[11,2,2,128]{3,2,1,0:T(2,128)S(1)}, f32[11,2,2,128]{3,2,1,0:T(2,128)S(1)}, u32[]{:S(2)}, u32[]{:S(2)}) collective-permute-start(f32[11,2,2,128]{3,2,1,0:T(2,128)S(1)} %get-tuple-element.6), channel_id=1, source_target_pairs={{1,0},{2,1},{3,2},{4,3},{5,4},{6,5},{7,6},{8,7},{9,8},{10,9},{11,1... | collective-permute-start | bytes 67592 | tf_op jit(solution)/shard_map/ppermute | solution.py:375
  7.8 0.0 copy-start.1
  8.5 0.0 copy-done.1
  8.5 0.7 abs_reduce_fusion
  9.2 0.7 fusion
  9.9 0.0 collective-permute-done
  9.9 1.8 %collective-permute-done.1 = f32[11,2,2,128]{3,2,1,0:T(2,128)S(1)} collective-permute-done((f32[11,2,2,128]{3,2,1,0:T(2,128)S(1)}, f32[11,2,2,128]{3,2,1,0:T(2,128)S(1)}, u32[]{:S(2)}, u32[]{:S(2)}) %collective-permute-start.1) | collective-permute-done | bytes 22560 | tf_op jit(solution)/shard_map/ppermute | solution.py:375
  11.7 0.0 copy-done
  11.8 5.8 %collective-permute-start.3 = (f32[11,2,20,128]{3,2,1,0:T(8,128)S(1)}, f32[11,2,20,128]{3,2,1,0:T(8,128)S(1)}, u32[]{:S(2)}, u32[]{:S(2)}) collective-permute-start(f32[11,2,20,128]{3,2,1,0:T(8,128)S(1)} %pad_maximum_fusion.refs_2_), channel_id=1, source_target_pairs={{16,0},{32,16},{48,32},{64,48},{80,64},{96,80},{112,96},{128,112},... | collective-permute-start | bytes 675848 | tf_op jit(solution)/shard_map/ppermute | solution.py:375
  17.5 1.9 %collective-permute-start.2 = (f32[11,2,20,128]{3,2,1,0:T(8,128)S(1)}, f32[11,2,20,128]{3,2,1,0:T(8,128)S(1)}, u32[]{:S(2)}, u32[]{:S(2)}) collective-permute-start(f32[11,2,20,128]{3,2,1,0:T(8,128)S(1)} %pad_maximum_fusion.refs_2_), channel_id=1, source_target_pairs={{0,16},{16,32},{32,48},{48,64},{64,80},{80,96},{96,112},{112,128},... | collective-permute-start | bytes 675848 | tf_op jit(solution)/shard_map/ppermute | solution.py:372
  19.5 0.1 pad_add_fusion.refs_0_
  19.6 0.1 select_maximum_fusion.refs_4_
  19.6 1.2 %collective-permute-done.3.refs_3_ = f32[11,2,20,128]{3,2,1,0:T(8,128)S(1)} collective-permute-done((f32[11,2,20,128]{3,2,1,0:T(8,128)S(1)}, f32[11,2,20,128]{3,2,1,0:T(8,128)S(1)}, u32[]{:S(2)}, u32[]{:S(2)}) %collective-permute-start.3) | collective-permute-done | bytes 225312 | tf_op jit(solution)/shard_map/ppermute | solution.py:375
  20.8 2.0 %collective-permute-done.2.refs_1_ = f32[11,2,20,128]{3,2,1,0:T(8,128)S(1)} collective-permute-done((f32[11,2,20,128]{3,2,1,0:T(8,128)S(1)}, f32[11,2,20,128]{3,2,1,0:T(8,128)S(1)}, u32[]{:S(2)}, u32[]{:S(2)}) %collective-permute-start.2) | collective-permute-done | bytes 225312 | tf_op jit(solution)/shard_map/ppermute | solution.py:372
  22.9 7.4 %march.1 = f32[16,8,384]{2,1,0:T(8,128)S(1)} custom-call(s32[2]{0:T(128)S(1)} %pad_add_fusion.refs_0_, f32[11,2,20,128]{3,2,1,0:T(8,128)S(1)} %collective-permute-done.2.refs_1_, f32[11,2,20,128]{3,2,1,0:T(8,128)S(1)} %pad_maximum_fusion.refs_2_, f32[11,2,20,128]{3,2,1,0:T(8,128)S(1)} %collective-permute-done.3.refs_3_, f32[8,128]{1,0:T(8,128)S(1)} %select_maximum_fusion.refs_4_), custom_call_target="tpu_custom_call" | custom-call | tf_op jit(solution)/shard_map/march/pallas_call | solution.py:402
  30.3 19.8 %all_to_all.10.got_ref.refs_0_ = f32[16,8,384]{2,1,0:T(8,128)S(1)} all-to-all(f32[16,8,384]{2,1,0:T(8,128)S(1)} %march.1), channel_id=1, replica_groups=mesh['gx'=32,'row'=16] {'row'}, dimensions={0} | all-to-all | bytes 393216 | tf_op jit(solution)/shard_map/all_to_all | solution.py:418
  50.1 0.9 %reduce.2 = f32[32,8,128]{2,1,0:T(8,128)} custom-call(f32[16,8,384]{2,1,0:T(8,128)S(1)} %all_to_all.10.got_ref.refs_0_), custom_call_target="tpu_custom_call" | custom-call | tf_op jit(solution)/shard_map/reduce/pallas_call | solution.py:419
  51.0 11.3 %all-to-all-start.1 = ((f32[32,8,128]{2,1,0:T(8,128)}), f32[32,8,128]{2,1,0:T(8,128)S(1)}, u32[]{:S(2)}, u32[]{:S(2)}) async-start(f32[32,8,128]{2,1,0:T(8,128)} %reduce.2), calls=%async_computation.1 | async-start | bytes 262144 | tf_op jit(solution)/shard_map/all_to_all | solution.py:427
  62.3 0.4 relay.1.refs_1_
  62.6 8.7 %all-to-all-done.1.refs_0_ = f32[32,8,128]{2,1,0:T(8,128)S(1)} async-done(((f32[32,8,128]{2,1,0:T(8,128)}), f32[32,8,128]{2,1,0:T(8,128)S(1)}, u32[]{:S(2)}, u32[]{:S(2)}) %all-to-all-start.1) | async-done | bytes 131104 | tf_op jit(solution)/shard_map/all_to_all | solution.py:427
  71.3 1.7 %final.1 = f32[20,8,256]{2,1,0:T(8,128)} custom-call(f32[32,8,128]{2,1,0:T(8,128)S(1)} %all-to-all-done.1.refs_0_, f32[20,8,256]{2,1,0:T(8,128)S(1)} %relay.1.refs_1_), custom_call_target="tpu_custom_call" | custom-call | tf_op jit(solution)/shard_map/final/pallas_call | solution.py:437
  (3 shorter events, 0.0 us)
Async XLA Ops:
  0.0 11.7 %copy-start = (f32[2,5,2,16,128]{4,3,2,1,0:T(8,128)S(1)}, f32[2,5,2,16,128]{4,3,2,1,0:T(8,128)}, u32[]{:S(2)}) copy-start(f32[2,5,2,16,128]{4,3,2,1,0:T(8,128)} %param.4) | copy-start | bytes 491524
  1.7 8.2 %collective-permute-start = (f32[11,2,2,128]{3,2,1,0:T(2,128)S(1)}, f32[11,2,2,128]{3,2,1,0:T(2,128)S(1)}, u32[]{:S(2)}, u32[]{:S(2)}) collective-permute-start(f32[11,2,2,128]{3,2,1,0:T(2,128)S(1)} %get-tuple-element.5), channel_id=1, source_target_pairs={{0,1},{1,2},{2,3},{3,4},{4,5},{5,6},{6,7},{7,8},{8,9},{9,10},{10,1... | collective-permute-start | bytes 67592 | tf_op jit(solution)/shard_map/ppermute | solution.py:372
  6.5 5.2 %collective-permute-start.1 = (f32[11,2,2,128]{3,2,1,0:T(2,128)S(1)}, f32[11,2,2,128]{3,2,1,0:T(2,128)S(1)}, u32[]{:S(2)}, u32[]{:S(2)}) collective-permute-start(f32[11,2,2,128]{3,2,1,0:T(2,128)S(1)} %get-tuple-element.6), channel_id=1, source_target_pairs={{1,0},{2,1},{3,2},{4,3},{5,4},{6,5},{7,6},{8,7},{9,8},{10,9},{11,1... | collective-permute-start | bytes 67592 | tf_op jit(solution)/shard_map/ppermute | solution.py:375
  7.8 0.7 copy-start.1
  11.8 9.1 %collective-permute-start.3 = (f32[11,2,20,128]{3,2,1,0:T(8,128)S(1)}, f32[11,2,20,128]{3,2,1,0:T(8,128)S(1)}, u32[]{:S(2)}, u32[]{:S(2)}) collective-permute-start(f32[11,2,20,128]{3,2,1,0:T(8,128)S(1)} %pad_maximum_fusion.refs_2_), channel_id=1, source_target_pairs={{16,0},{32,16},{48,32},{64,48},{80,64},{96,80},{112,96},{128,112},... | collective-permute-start | bytes 675848 | tf_op jit(solution)/shard_map/ppermute | solution.py:375
  17.5 5.3 %collective-permute-start.2 = (f32[11,2,20,128]{3,2,1,0:T(8,128)S(1)}, f32[11,2,20,128]{3,2,1,0:T(8,128)S(1)}, u32[]{:S(2)}, u32[]{:S(2)}) collective-permute-start(f32[11,2,20,128]{3,2,1,0:T(8,128)S(1)} %pad_maximum_fusion.refs_2_), channel_id=1, source_target_pairs={{0,16},{16,32},{32,48},{48,64},{64,80},{80,96},{96,112},{112,128},... | collective-permute-start | bytes 675848 | tf_op jit(solution)/shard_map/ppermute | solution.py:372
  51.0 20.4 %all-to-all-start.1 = ((f32[32,8,128]{2,1,0:T(8,128)}), f32[32,8,128]{2,1,0:T(8,128)S(1)}, u32[]{:S(2)}, u32[]{:S(2)}) async-start(f32[32,8,128]{2,1,0:T(8,128)} %reduce.2), calls=%async_computation.1 | async-start | bytes 262144 | tf_op jit(solution)/shard_map/all_to_all | solution.py:427

commit v3 on v2

--- a/solution.py
+++ b/solution.py
@@ -8,6 +8,7 @@
 from jax.sharding import PartitionSpec as P
 
 STEPS = 2
+UNROLL = 2
 RIM = 2
 LANES = 128
 ROWS = 8
@@ -110,30 +111,32 @@
 
 
 def march_kernel(
-    n_var, wide_x, wide_r, count_x, count_r,
-    place_ref, low_ref, mid_ref, high_ref, panel_ref,
-    out_ref, rows_ref, now_ref, next_ref, coeff_ref, packed_ref, parts_ref,
+    n_var, wide_x, wide_r, count_x,
+    place_ref, mid_ref, mate_ref, far_ref, panel_ref,
+    out_ref, now_ref, next_ref, coeff_ref, packed_ref, parts_ref,
 ):
-    n_plane = low_ref.shape[0] - 1
-    n_theta = low_ref.shape[-1]
+    n_plane = mid_ref.shape[0] - 1
+    n_theta = mid_ref.shape[-1]
     n_tile = n_theta // ROWS
     deep = wide_r + 2 * RIM
     n_pair = n_var * n_var
     used = (wide_x + 2 * RIM) * deep
 
-    for plane in range(n_plane + 1):
-        blocks = [low_ref[plane, x] for x in range(RIM)]
-        blocks += [mid_ref[plane, x] for x in range(wide_x)]
-        blocks += [high_ref[plane, x] for x in range(RIM)]
-        for x, block in enumerate(blocks):
-            rows_ref[plane, x * deep : (x + 1) * deep, :] = block
-        rows_ref[plane, used:LANES, :] = jnp.zeros((LANES - used, n_theta), jnp.float32)
+    mate_is_low = jnp.full((RIM * deep, n_theta), place_ref[0] % 2, jnp.int32) == 1
+
+    def turn(plane):
+        mate, far = mate_ref[plane], far_ref[plane]
+        low = jnp.where(mate_is_low, mate, far)
+        high = jnp.where(mate_is_low, far, mate)
+        blank = jnp.zeros((LANES - used, n_theta), jnp.float32)
+        return jnp.concatenate([low, mid_ref[plane], high, blank], axis=0).T
+
     for plane in range(n_plane):
-        turned = rows_ref[plane].T
+        turned = turn(plane)
         now_ref[plane, ROWS : ROWS + n_theta, :] = turned
         now_ref[plane, ROWS - 1 : ROWS, :] = turned[n_theta - 1 :]
         now_ref[plane, ROWS + n_theta : ROWS + n_theta + 1, :] = turned[:1]
-    coeff_ref[: n_theta, :] = rows_ref[n_plane].T
+    coeff_ref[:n_theta, :] = turn(n_plane)
     viscous = coeff_ref[4 * n_pair : 4 * n_pair + 1, :]
     for i in range(n_var):
         own = 3 * n_pair + i * n_var + i
@@ -143,9 +146,10 @@
 
     lane = lanes_of((ROWS, LANES))
     at_x = lane // deep - RIM + place_ref[0] * wide_x
-    at_r = lane % deep - RIM + place_ref[1] * wide_r
-    inside = (at_x >= 0) & (at_x < wide_x * count_x) & (at_r >= 0) & (at_r < wide_r * count_r)
-    inside = inside & (lane < used)
+    inside = (at_x >= 0) & (at_x < wide_x * count_x) & (lane < used)
+    first = place_ref[1] == 0
+    from_above = ~((lane % deep == 2 * RIM - 1) & first)
+    from_below = ~((lane % deep == 2 * RIM) & first)
 
     def coeff(index):
         return coeff_ref[index : index + 1, :]
@@ -160,19 +164,19 @@
         result = [None] * n_plane
         for i in range(n_var):
             for k in range(0, n_plane, n_var):
-                stream = radial = local = 0.0
-                for j in range(n_var):
-                    at = j * n_var + i
-                    stream = stream + coeff(at) * centre[k + j]
-                    radial = radial + coeff(n_pair + at) * centre[k + j]
-                    local = local + coeff(2 * n_pair + at) * differ[k + j]
-                    local = local + coeff(3 * n_pair + at) * centre[k + j]
+                def flux(start, values):
+                    return tree([coeff(start + j * n_var + i) * values[k + j] for j in range(n_var)], jnp.add)
+
                 own = centre[k + i]
+                stream = flux(0, centre)
+                radial = flux(n_pair, centre)
+                local = flux(2 * n_pair, differ) + flux(3 * n_pair, centre)
                 local = local + coeff(4 * n_pair) * both[k + i]
+                above = roll_lanes(coeff(n_theta + 2) * own + radial, -1)
+                below = roll_lanes(coeff(n_theta + 3) * own - radial, 1)
                 local = local + roll_lanes(coeff(n_theta) * own + stream, -deep)
                 local = local + roll_lanes(coeff(n_theta + 1) * own - stream, deep)
-                local = local + roll_lanes(coeff(n_theta + 2) * own + radial, -1)
-                local = local + roll_lanes(coeff(n_theta + 3) * own - radial, 1)
+                local = local + jnp.where(from_above, above, 0.0) + jnp.where(from_below, below, 0.0)
                 result[k + i] = local
         return result
 
@@ -182,7 +186,7 @@
             next_ref[b, pl.ds(ROWS + tile * ROWS, ROWS), :] = jnp.where(inside, result[b], 0.0)
         return carry
 
-    lax.fori_loop(0, n_tile, first_step, 0)
+    lax.fori_loop(0, n_tile, first_step, 0, unroll=UNROLL)
     for b in range(n_plane):
         next_ref[b, ROWS - 1 : ROWS, :] = next_ref[b, ROWS + n_theta - 1 : ROWS + n_theta, :]
         next_ref[b, ROWS + n_theta : ROWS + n_theta + 1, :] = next_ref[b, ROWS : ROWS + 1, :]
@@ -204,7 +208,7 @@
             largest = jnp.maximum(largest, jnp.abs(packed))
         return largest
 
-    largest = lax.fori_loop(0, n_tile, second_step, jnp.zeros((ROWS, LANES), jnp.float32))
+    largest = lax.fori_loop(0, n_tile, second_step, jnp.zeros((ROWS, LANES), jnp.float32), unroll=UNROLL)
     largest = jnp.max(largest, axis=1, keepdims=True)
     largest = jnp.max(largest, axis=0, keepdims=True)
     inverse = safe_inverse(jnp.broadcast_to(largest, (ROWS, LANES)))
@@ -287,13 +291,16 @@
     lane = lanes_of((ROWS, LANES))
     for g in range(n_plane * wide_x):
         v, slot = divmod(g, per_vreg)
+        halves = []
         for half in range(count // per_vreg):
             value = jnp.zeros((ROWS, LANES), jnp.float32)
             for n in range(per_vreg):
                 source = got_ref[half * per_vreg + n, :, v * LANES : (v + 1) * LANES]
                 turned = roll_lanes(source, (n - slot) * wide_r)
                 value = placed_at(lane, n * wide_r, wide_r, turned, value)
-            out_ref[g, :, half * LANES : (half + 1) * LANES] = value
+            halves.append(value)
+        whole = jnp.concatenate(halves, axis=1)
+        out_ref[g] = pltpu.roll(whole, whole.shape[1] - RIM, 1)
 
 
 def final_kernel(n_var, wide_x, scale, got_ref, cells_ref, out_ref, weight_ref):
@@ -365,17 +372,6 @@
 PARAMS = pltpu.CompilerParams(vmem_limit_bytes=32 * 1024 * 1024)
 
 
-def with_halo(block, axis, dim, width):
-    count = lax.axis_size(axis)
-    forward = [(i, i + 1) for i in range(count - 1)]
-    backward = [(target, source) for source, target in forward]
-    low = lax.ppermute(
-        lax.slice_in_dim(block, block.shape[dim] - width, None, axis=dim), axis, forward
-    )
-    high = lax.ppermute(lax.slice_in_dim(block, 0, width, axis=dim), axis, backward)
-    return low, high
-
-
 def body(test_vectors, base_coeffs, panel_set, owner_index):
     count_x = lax.axis_size("gx")
     count_r = lax.axis_size("row")
@@ -392,20 +388,24 @@
     field = test_vectors.reshape((n_plane, wide_x, wide_r, n_theta))
     turned = base_coeffs.transpose(1, 2, 0)
     turned = jnp.pad(turned, ((0, 0), (0, 0), (0, n_theta - n_coeff)))
+    ring = [(i, (i + 1) % count_r) for i in range(count_r)]
+    edge = jnp.concatenate([field[:, :, -2 * RIM :], turned[None, :, -2 * RIM :]], axis=0)
+    edge = lax.ppermute(edge, "row", ring)
     both = jnp.concatenate([field, turned[None]], axis=0)
-    low, high = with_halo(both, "row", 2, RIM)
-    both = jnp.concatenate([low, both, high], axis=2)
-    low, high = with_halo(both, "gx", 1, RIM)
+    both = jnp.concatenate([edge, both], axis=2)
+    both = both.reshape((n_plane + 1, wide_x * (wide_r + 2 * RIM), n_theta))
+    outer = [(i, i + 1 if i % 2 else i - 1) for i in range(1, count_x - 1)]
+    far = lax.ppermute(both, "gx", outer)
+    mate = lax.ppermute(both, "gx", [(i, i ^ 1) for i in range(count_x)])
 
     n_wide = 3
     n_tile = n_theta // ROWS
     sent = pl.pallas_call(
-        lambda *refs: march_kernel(n_var, wide_x, wide_r, count_x, count_r, *refs),
+        lambda *refs: march_kernel(n_var, wide_x, wide_r, count_x, *refs),
         out_shape=jax.ShapeDtypeStruct((n_tile, ROWS, n_wide * LANES), jnp.float32),
         in_specs=[pl.BlockSpec(memory_space=pltpu.SMEM)] + [VMEM] * 4,
         out_specs=VMEM,
         scratch_shapes=[
-            pltpu.VMEM((n_plane + 1, LANES, n_theta), jnp.float32),
             pltpu.VMEM((n_plane, n_theta + 2 * ROWS, LANES), jnp.float32),
             pltpu.VMEM((n_plane, n_theta + 2 * ROWS, LANES), jnp.float32),
             pltpu.VMEM((n_theta + ROWS, LANES), jnp.float32),
@@ -414,7 +414,7 @@
         ],
         compiler_params=PARAMS,
         name="march",
-    )(jnp.stack([at_x, at_r]), low, both, high, panel)
+    )(jnp.stack([at_x, at_r]), both, mate, far, panel)
     got = lax.all_to_all(sent, "row", 0, 0, tiled=True)
     stats = pl.pallas_call(
         reduce_kernel,

time: 73.5 us -> 66.8 us (0.909)
  blocking collectives: 19.8 us -> 13.7 us
  waiting for transfers between devices: 13.7 us -> 18 us
  starting transfers between devices: 25.1 us -> 21.3 us
  other arithmetic: 2.5 us -> 1.36 us
  local copies, waits for them, and re-layouts: 0.79 us -> 1.69 us
  Pallas kernels: 10.4 us -> 9.52 us
    all_to_all x1, blocking collectives: 19.8 us -> 13.7 us  [body(): got = lax.all_to_all(sent, 'row', 0, 0, tiled=True)]
    ppermute x4 -> x3, waiting for transfers between devices: 5.03 us -> 10.2 us  [the longest x1 8.65 us: body(): edge = lax.ppermute(edge, 'row', ring)]
    ppermute x4 -> x3, starting transfers between devices: 13.8 us -> 11.4 us  [the longest x1 4.83 us: body(): edge = lax.ppermute(edge, 'row', ring)]
    pallas_call x1, Pallas kernels: 7.43 us -> 5.7 us  [body(): pl.pallas_call(lambda *refs: march_kernel(n_var, wide_x, wide_r, count_x,...]
    all_to_all x1, starting transfers between devices: 11.3 us -> 9.92 us  [body(): stats = lax.all_to_all(stats, 'gx', 0, 0, tiled=True)]
    slice x1 -> x0, other arithmetic: 0.94 us -> none  [with_halo(): lax.slice_in_dim(block, block.shape[dim] - width, None, axis=dim)]
    slice x0 -> x1, local copies, waits for them, and re-layouts: none -> 0.9 us  [body(): field[:, :, -2 * RIM:]]
    all_to_all x1, waiting for transfers between devices: 8.7 us -> 7.83 us  [body(): stats = lax.all_to_all(stats, 'gx', 0, 0, tiled=True)]
  transfers between devices with their start and end apart: 5 -> 4, of which waited for: 4 -> 3; matrix products, arithmetic and copies ran while one was open for 2% -> 2% of each run, Pallas kernels for 0% -> 2%
where the time goes in v3:
time: 66.8 us; the launch traced here: 66.4 us
  starting transfers between devices  21.3 us (32%)
  waiting for transfers between devices  18 us (27%)
  blocking collectives  13.7 us (21%)
  Pallas kernels  9.52 us (14%)
  local copies, waits for them, and re-layouts  1.69 us (3%)
  other arithmetic  1.36 us (2%)
  between operations  0.78 us (1%)
    all_to_all x1, blocking collectives, body(): got = lax.all_to_all(sent, 'row', 0, 0, tiled=True)  13.7 us
    all_to_all x1, starting transfers between devices, body(): stats = lax.all_to_all(stats, 'gx', 0, 0, tiled=True)  9.92 us
    ppermute x1, waiting for transfers between devices, body(): edge = lax.ppermute(edge, 'row', ring)  8.65 us
    all_to_all x1, waiting for transfers between devices, body(): stats = lax.all_to_all(stats, 'gx', 0, 0, tiled=True)  7.83 us
    pallas_call x1, Pallas kernels, body(): pl.pallas_call(lambda *refs: march_kernel(n_var, wide_x, wide_r, count_x,...  5.7 us
    ppermute x1, starting transfers between devices, body(): edge = lax.ppermute(edge, 'row', ring)  4.83 us
    ppermute x1, starting transfers between devices, body(): far = lax.ppermute(both, 'gx', outer)  4.63 us
    ppermute x1, starting transfers between devices, body(): mate = lax.ppermute(both, 'gx', [(i, i ^ 1) for i in range(count_x)])  1.92 us
  transfers between devices with their start and end apart: 4, of which 3 were waited for; matrix products, arithmetic and copies ran while one was open for 2% of the time, Pallas kernels for 2%

profile of v3, /device:TPU:1, one launch (start us, length us, event | category | flops | bytes accessed | tf_op | source)
XLA Modules:
  0.0 66.4 jit_solution(2422237070272537970)
XLA Ops:
  0.0 0.7 %fusion.1 = f32[1,2,4,128]{3,2,1,0:T(4,128)S(1)} fusion(f32[2,16,101]{2,1,0:T(8,128)} %bitcast.17), kind=kLoop, calls=%fused_computation.9 | loop fusion | bytes 17024 | tf_op jit(solution)/shard_map/broadcast_in_dim | solution.py:392
  0.7 0.9 %slice.24 = f32[10,2,4,128]{3,2,1,0:T(4,128)S(1)} slice(f32[10,2,16,128]{3,2,1,0:T(8,128)} %bitcast.15), slice={[0:10], [0:2], [12:16], [0:128]} | slice | bytes 81920 | tf_op jit(solution)/shard_map/slice | solution.py:392
  1.7 4.8 %collective-permute-start = (f32[11,2,4,128]{3,2,1,0:T(4,128)S(1)}, f32[11,2,4,128]{3,2,1,0:T(4,128)S(1)}, u32[]{:S(2)}, u32[]{:S(2)}) collective-permute-start(f32[11,2,4,128]{3,2,1,0:T(4,128)S(1)} %pad_maximum_fusion), channel_id=1, source_target_pairs={{0,1},{1,2},{2,3},{3,4},{4,5},{5,6},{6,7},{7,8},{8,9},{9,10},{10,1... | collective-permute-start | bytes 135176 | tf_op jit(solution)/shard_map/ppermute | solution.py:393
  6.5 0.0 copy-start.2
  6.5 0.0 copy-start.1
  7.2 0.0 copy-done.2
  7.2 0.6 abs_reduce_fusion
  7.8 0.6 fusion
  8.4 0.0 copy-done.1
  8.4 8.7 %collective-permute-done = f32[11,2,4,128]{3,2,1,0:T(4,128)S(1)} collective-permute-done((f32[11,2,4,128]{3,2,1,0:T(4,128)S(1)}, f32[11,2,4,128]{3,2,1,0:T(4,128)S(1)}, u32[]{:S(2)}, u32[]{:S(2)}) %collective-permute-start) | collective-permute-done | bytes 45088 | tf_op jit(solution)/shard_map/ppermute | solution.py:393
  17.0 0.0 copy-done
  17.1 4.6 %collective-permute-start.2 = (f32[11,40,128]{2,1,0:T(8,128)S(1)}, f32[11,40,128]{2,1,0:T(8,128)S(1)}, u32[]{:S(2)}, u32[]{:S(2)}) collective-permute-start(f32[11,40,128]{2,1,0:T(8,128)S(1)} %reshape.18.refs_1_), channel_id=1, source_target_pairs={{16,32},{32,16},{48,64},{64,48},{80,96},{96,80},{112,128},{128,112... | collective-permute-start | bytes 675848 | tf_op jit(solution)/shard_map/ppermute | solution.py:398
  21.8 1.9 %collective-permute-start.1 = (f32[11,40,128]{2,1,0:T(8,128)S(1)}, f32[11,40,128]{2,1,0:T(8,128)S(1)}, u32[]{:S(2)}, u32[]{:S(2)}) collective-permute-start(f32[11,40,128]{2,1,0:T(8,128)S(1)} %reshape.18.refs_1_), channel_id=1, source_target_pairs={{0,16},{16,0},{32,48},{48,32},{64,80},{80,64},{96,112},{112,96},{1... | collective-permute-start | bytes 675848 | tf_op jit(solution)/shard_map/ppermute | solution.py:399
  23.7 0.1 pad_add_fusion.refs_0_
  23.8 0.1 select_maximum_fusion.refs_4_
  23.9 1.6 %collective-permute-done.2.refs_3_ = f32[11,40,128]{2,1,0:T(8,128)S(1)} collective-permute-done((f32[11,40,128]{2,1,0:T(8,128)S(1)}, f32[11,40,128]{2,1,0:T(8,128)S(1)}, u32[]{:S(2)}, u32[]{:S(2)}) %collective-permute-start.2) | collective-permute-done | bytes 225312 | tf_op jit(solution)/shard_map/ppermute | solution.py:398
  25.4 0.0 collective-permute-done.1.refs_2_
  25.4 5.7 %march.1 = f32[16,8,384]{2,1,0:T(8,128)S(1)} custom-call(s32[2]{0:T(128)S(1)} %pad_add_fusion.refs_0_, f32[11,40,128]{2,1,0:T(8,128)S(1)} %reshape.18.refs_1_, f32[11,40,128]{2,1,0:T(8,128)S(1)} %collective-permute-done.1.refs_2_, f32[11,40,128]{2,1,0:T(8,128)S(1)} %collective-permute-done.2.refs_3_, f32[8,128]{1,0:T(8,128)S(1)} %select_maximum_fusion.refs_4_), custom_call_target="tpu_custom_call" | custom-call | tf_op jit(solution)/shard_map/march/pallas_call | solution.py:403
  31.1 13.7 %all_to_all.10.got_ref.refs_0_ = f32[16,8,384]{2,1,0:T(8,128)S(1)} all-to-all(f32[16,8,384]{2,1,0:T(8,128)S(1)} %march.1), channel_id=1, replica_groups=mesh['gx'=32,'row'=16] {'row'}, dimensions={0} | all-to-all | bytes 393216 | tf_op jit(solution)/shard_map/all_to_all | solution.py:418
  44.9 0.9 %reduce.2 = f32[32,8,128]{2,1,0:T(8,128)} custom-call(f32[16,8,384]{2,1,0:T(8,128)S(1)} %all_to_all.10.got_ref.refs_0_), custom_call_target="tpu_custom_call" | custom-call | tf_op jit(solution)/shard_map/reduce/pallas_call | solution.py:419
  45.8 9.9 %all-to-all-start.1 = ((f32[32,8,128]{2,1,0:T(8,128)}), f32[32,8,128]{2,1,0:T(8,128)S(1)}, u32[]{:S(2)}, u32[]{:S(2)}) async-start(f32[32,8,128]{2,1,0:T(8,128)} %reduce.2), calls=%async_computation.1 | async-start | bytes 262144 | tf_op jit(solution)/shard_map/all_to_all | solution.py:427
  55.7 1.2 %relay.1.refs_1_ = f32[20,8,256]{2,1,0:T(8,128)S(1)} custom-call(f32[16,8,384]{2,1,0:T(8,128)S(1)} %all_to_all.10.got_ref.refs_0_), custom_call_target="tpu_custom_call" | custom-call | tf_op jit(solution)/shard_map/relay/pallas_call | solution.py:428
  56.9 7.8 %all-to-all-done.1.refs_0_ = f32[32,8,128]{2,1,0:T(8,128)S(1)} async-done(((f32[32,8,128]{2,1,0:T(8,128)}), f32[32,8,128]{2,1,0:T(8,128)S(1)}, u32[]{:S(2)}, u32[]{:S(2)}) %all-to-all-start.1) | async-done | bytes 131104 | tf_op jit(solution)/shard_map/all_to_all | solution.py:427
  64.8 1.7 %final.1 = f32[20,8,256]{2,1,0:T(8,128)} custom-call(f32[32,8,128]{2,1,0:T(8,128)S(1)} %all-to-all-done.1.refs_0_, f32[20,8,256]{2,1,0:T(8,128)S(1)} %relay.1.refs_1_), custom_call_target="tpu_custom_call" | custom-call | tf_op jit(solution)/shard_map/final/pallas_call | solution.py:437
  (6 shorter events, 0.1 us)
Async XLA Ops:
  0.0 17.1 %copy-start = (f32[2,5,2,16,128]{4,3,2,1,0:T(8,128)S(1)}, f32[2,5,2,16,128]{4,3,2,1,0:T(8,128)}, u32[]{:S(2)}) copy-start(f32[2,5,2,16,128]{4,3,2,1,0:T(8,128)} %param.4) | copy-start | bytes 491524
  1.7 15.4 %collective-permute-start = (f32[11,2,4,128]{3,2,1,0:T(4,128)S(1)}, f32[11,2,4,128]{3,2,1,0:T(4,128)S(1)}, u32[]{:S(2)}, u32[]{:S(2)}) collective-permute-start(f32[11,2,4,128]{3,2,1,0:T(4,128)S(1)} %pad_maximum_fusion), channel_id=1, source_target_pairs={{0,1},{1,2},{2,3},{3,4},{4,5},{5,6},{6,7},{7,8},{8,9},{9,10},{10,1... | collective-permute-start | bytes 135176 | tf_op jit(solution)/shard_map/ppermute | solution.py:393
  6.5 0.7 %copy-start.2 = (f32[1,10,10]{2,0,1:T(1,128)S(1)}, f32[1,10,10]{2,0,1:T(1,128)}, u32[]{:S(2)}) copy-start(f32[1,10,10]{2,0,1:T(1,128)} %param.6) | copy-start | bytes 1204
  6.5 1.9 %copy-start.1 = (f32[101,2,16]{0,2,1:T(8,128)S(1)}, f32[101,2,16]{0,2,1:T(8,128)}, u32[]{:S(2)}) copy-start(f32[101,2,16]{0,2,1:T(8,128)} %param.5) | copy-start | bytes 38788
  17.1 8.3 %collective-permute-start.2 = (f32[11,40,128]{2,1,0:T(8,128)S(1)}, f32[11,40,128]{2,1,0:T(8,128)S(1)}, u32[]{:S(2)}, u32[]{:S(2)}) collective-permute-start(f32[11,40,128]{2,1,0:T(8,128)S(1)} %reshape.18.refs_1_), channel_id=1, source_target_pairs={{16,32},{32,16},{48,64},{64,48},{80,96},{96,80},{112,128},{128,112... | collective-permute-start | bytes 675848 | tf_op jit(solution)/shard_map/ppermute | solution.py:398
  21.8 3.6 %collective-permute-start.1 = (f32[11,40,128]{2,1,0:T(8,128)S(1)}, f32[11,40,128]{2,1,0:T(8,128)S(1)}, u32[]{:S(2)}, u32[]{:S(2)}) collective-permute-start(f32[11,40,128]{2,1,0:T(8,128)S(1)} %reshape.18.refs_1_), channel_id=1, source_target_pairs={{0,16},{16,0},{32,48},{48,32},{64,80},{80,64},{96,112},{112,96},{1... | collective-permute-start | bytes 675848 | tf_op jit(solution)/shard_map/ppermute | solution.py:399
  45.8 19.0 %all-to-all-start.1 = ((f32[32,8,128]{2,1,0:T(8,128)}), f32[32,8,128]{2,1,0:T(8,128)S(1)}, u32[]{:S(2)}, u32[]{:S(2)}) async-start(f32[32,8,128]{2,1,0:T(8,128)} %reduce.2), calls=%async_computation.1 | async-start | bytes 262144 | tf_op jit(solution)/shard_map/all_to_all | solution.py:427

commit v4 on v3

--- a/solution.py
+++ b/solution.py
@@ -194,16 +194,20 @@
     group = wide_x * wide_r
     per_vreg = LANES // group
     n_wide = packed_ref.shape[-1] // LANES
+    mine = []
+    for x in range(wide_x):
+        start = (x + RIM) * deep + RIM
+        mine.append((lane >= start) & (lane < start + wide_r))
 
     def second_step(tile, largest):
         result = advance(next_ref, tile)
         for v in range(n_wide):
-            packed = jnp.zeros((ROWS, LANES), jnp.float32)
+            pieces = []
             for b in range(v * per_vreg, min((v + 1) * per_vreg, n_plane)):
                 for x in range(wide_x):
-                    target = (b % per_vreg) * group + x * wide_r
-                    shift = target - ((x + RIM) * deep + RIM)
-                    packed = placed_at(lane, target, wide_r, roll_lanes(result[b], shift), packed)
+                    shift = (b % per_vreg) * group + x * wide_r - ((x + RIM) * deep + RIM)
+                    pieces.append(roll_lanes(jnp.where(mine[x], result[b], 0.0), shift))
+            packed = tree(pieces, jnp.add)
             packed_ref[tile, :, v * LANES : (v + 1) * LANES] = packed
             largest = jnp.maximum(largest, jnp.abs(packed))
         return largest
@@ -229,10 +233,12 @@
         keep = lane < LANES - rest * group
         return jnp.where(keep, roll_lanes(value, -rest * group), roll_lanes(other, -rest * group))
 
-    pairs = [[None] * n_wide for _ in range(ROWS)]
     zero = jnp.zeros((ROWS, LANES), jnp.float32)
+    pairs = [[(zero, zero)] * n_wide for _ in range(ROWS)]
     for s in range(RING // 2 + 1):
         for v in range(n_wide):
+            if 2 * s == RING and v * per_vreg + s >= n_plane:
+                continue
             total, error = zero, zero
             for tile in range(n_tile):
                 a_high, a_low = parts_ref[0, tile, v], parts_ref[1, tile, v]
@@ -248,7 +254,7 @@
     row = lax.broadcasted_iota(jnp.int32, (ROWS, LANES), 0)
     sums = []
     for v in range(n_wide):
-        level = [pairs[s][v] if s <= RING // 2 else (zero, zero) for s in range(ROWS)]
+        level = [pairs[s][v] for s in range(ROWS)]
         half = ROWS // 2
         while half:
             joined = []
@@ -277,6 +283,16 @@
         out_ref[tile, :, last:] = jnp.where(lane < HIGH, packed_ref[tile, :, last:], stats)
 
 
+def prepare_kernel(field_ref, coeff_ref, edge_ref, turned_ref):
+    n_plane, _, wide_r, _ = field_ref.shape
+    n_coeff = coeff_ref.shape[-1]
+    start = wide_r - edge_ref.shape[2]
+    edge_ref[:n_plane] = field_ref[:, :, start:, :]
+    turned_ref[...] = jnp.zeros_like(turned_ref)
+    turned_ref[:, :, :n_coeff] = coeff_ref[...]
+    edge_ref[n_plane] = turned_ref[:, start:, :]
+
+
 def reduce_kernel(got_ref, out_ref):
     count, _, wide = got_ref.shape
     pair, size, panel = merge([got_ref[n, :, wide - LANES :] for n in range(count)])
@@ -329,15 +345,13 @@
     for s in range(RING // 2 + 1):
         left_s, right_s = turned(left, s), turned(right, s)
         term = pair_add(two_prod(left, right_s), two_prod(left_s, right))
-        share = 1.0 if s % (RING // 2) else 0.5
+        share = 1.0 if s else 0.5
         row_s = tuple(share * part[s : s + 1, :] for part in inner)
         terms.append(pair_mul(term, row_s))
     total = pair_tree(terms)
+    total = pair_tree([pair_roll(total, -b, 1) for b in range(n_plane)])
     for shift in (4, 2, 1):
         total = pair_add(total, pair_roll(total, shift, 0))
-    total = pair_add(total, pair_roll(total, -RING // 2, 1))
-    total = pair_add(total, pair_roll(total, -RING // 4, 1))
-    total = pair_tree([total, pair_roll(total, -1, 1), pair_roll(total, -2, 1)])
 
     def everywhere(part, at):
         return jnp.broadcast_to(part[:, at : at + 1], (ROWS, LANES))
@@ -376,7 +390,6 @@
     count_x = lax.axis_size("gx")
     count_r = lax.axis_size("row")
     n_vec, n_var, wide_x, wide_r, n_theta = test_vectors.shape
-    n_coeff = base_coeffs.shape[0]
     n_plane = n_vec * n_var
     at_x, at_r = lax.axis_index("gx"), lax.axis_index("row")
 
@@ -386,10 +399,18 @@
     panel = jnp.pad(panel, ((0, ROWS - n_var), (PANEL, LANES - PANEL - 2 * n_plane)))
 
     field = test_vectors.reshape((n_plane, wide_x, wide_r, n_theta))
-    turned = base_coeffs.transpose(1, 2, 0)
-    turned = jnp.pad(turned, ((0, 0), (0, 0), (0, n_theta - n_coeff)))
+    edge, turned = pl.pallas_call(
+        prepare_kernel,
+        out_shape=(
+            jax.ShapeDtypeStruct((n_plane + 1, wide_x, 2 * RIM, n_theta), jnp.float32),
+            jax.ShapeDtypeStruct((wide_x, wide_r, n_theta), jnp.float32),
+        ),
+        in_specs=[VMEM, VMEM],
+        out_specs=(VMEM, VMEM),
+        compiler_params=PARAMS,
+        name="prepare",
+    )(field, base_coeffs.transpose(1, 2, 0))
     ring = [(i, (i + 1) % count_r) for i in range(count_r)]
-    edge = jnp.concatenate([field[:, :, -2 * RIM :], turned[None, :, -2 * RIM :]], axis=0)
     edge = lax.ppermute(edge, "row", ring)
     both = jnp.concatenate([field, turned[None]], axis=0)
     both = jnp.concatenate([edge, both], axis=2)

time: 66.8 us -> 66.9 us (level)
    unnamed x6 -> x8, local copies, waits for them, and re-layouts: 0.02 us -> 1.66 us
    slice x1 -> x0, local copies, waits for them, and re-layouts: 0.9 us -> none  [body(): field[:, :, -2 * RIM:]]
    broadcast_in_dim x2 -> x0, local copies, waits for them, and re-layouts: 0.74 us -> none  [the longest x1 0.74 us: body(): turned[None, :, -2 * RIM:]]
where the time goes in v4:
time: 66.9 us; the launch traced here: 66.5 us
  starting transfers between devices  21.4 us (32%)
  waiting for transfers between devices  17.9 us (27%)
  blocking collectives  13.7 us (20%)
  Pallas kernels  9.45 us (14%)
  local copies, waits for them, and re-layouts  1.69 us (3%)
  other arithmetic  1.47 us (2%)
  between operations  0.74 us (1%)
    all_to_all x1, blocking collectives, body(): got = lax.all_to_all(sent, 'row', 0, 0, tiled=True)  13.7 us
    all_to_all x1, starting transfers between devices, body(): stats = lax.all_to_all(stats, 'gx', 0, 0, tiled=True)  9.92 us
    ppermute x1, waiting for transfers between devices, body(): edge = lax.ppermute(edge, 'row', ring)  8.55 us
    all_to_all x1, waiting for transfers between devices, body(): stats = lax.all_to_all(stats, 'gx', 0, 0, tiled=True)  7.83 us
    pallas_call x1, Pallas kernels, body(): pl.pallas_call(lambda *refs: march_kernel(n_var, wide_x, wide_r, count_x,...  5.74 us
    ppermute x1, starting transfers between devices, body(): edge = lax.ppermute(edge, 'row', ring)  4.96 us
    ppermute x1, starting transfers between devices, body(): far = lax.ppermute(both, 'gx', outer)  4.63 us
    ppermute x1, starting transfers between devices, body(): mate = lax.ppermute(both, 'gx', [(i, i ^ 1) for i in range(count_x)])  1.92 us
  transfers between devices with their start and end apart: 4, of which 3 were waited for; matrix products, arithmetic and copies ran while one was open for 2% of the time, Pallas kernels for 2%

profile of v4, /device:TPU:1, one launch (start us, length us, event | category | flops | bytes accessed | tf_op | source)
XLA Modules:
  0.0 66.5 jit_solution(8826750547609959)
XLA Ops:
  0.0 0.0 copy-start
  0.0 0.9 %copy-done = f32[2,5,2,16,128]{4,3,2,1,0:T(8,128)S(1)} copy-done((f32[2,5,2,16,128]{4,3,2,1,0:T(8,128)S(1)}, f32[2,5,2,16,128]{4,3,2,1,0:T(8,128)}, u32[]{:S(2)}) %copy-start) | copy-done | bytes 163864
  0.9 0.0 copy-start.2
  0.9 0.7 %copy-done.2 = f32[101,2,16]{0,2,1:T(8,128)S(1)} copy-done((f32[101,2,16]{0,2,1:T(8,128)S(1)}, f32[101,2,16]{0,2,1:T(8,128)}, u32[]{:S(2)}) %copy-start.2) | copy-done | bytes 12952
  1.7 5.0 %collective-permute-start = (f32[11,2,4,128]{3,2,1,0:T(4,128)S(1)}, f32[11,2,4,128]{3,2,1,0:T(4,128)S(1)}, u32[]{:S(2)}, u32[]{:S(2)}) collective-permute-start(f32[11,2,4,128]{3,2,1,0:T(4,128)S(1)} %get-tuple-element.7), channel_id=1, source_target_pairs={{0,1},{1,2},{2,3},{3,4},{4,5},{5,6},{6,7},{7,8},{8,9},{9,10},{10,1... | collective-permute-start | bytes 135176 | tf_op jit(solution)/shard_map/ppermute | solution.py:414
  6.6 0.0 copy-start.3
  7.3 0.0 copy-done.3
  7.3 0.7 abs_reduce_fusion
  8.0 0.6 fusion
  8.6 8.6 %collective-permute-done = f32[11,2,4,128]{3,2,1,0:T(4,128)S(1)} collective-permute-done((f32[11,2,4,128]{3,2,1,0:T(4,128)S(1)}, f32[11,2,4,128]{3,2,1,0:T(4,128)S(1)}, u32[]{:S(2)}, u32[]{:S(2)}) %collective-permute-start) | collective-permute-done | bytes 45088 | tf_op jit(solution)/shard_map/ppermute | solution.py:414
  17.2 0.0 copy-done.1
  17.2 4.6 %collective-permute-start.2 = (f32[11,40,128]{2,1,0:T(8,128)S(1)}, f32[11,40,128]{2,1,0:T(8,128)S(1)}, u32[]{:S(2)}, u32[]{:S(2)}) collective-permute-start(f32[11,40,128]{2,1,0:T(8,128)S(1)} %reshape.18.refs_1_), channel_id=1, source_target_pairs={{16,32},{32,16},{48,64},{64,48},{80,96},{96,80},{112,128},{128,112... | collective-permute-start | bytes 675848 | tf_op jit(solution)/shard_map/ppermute | solution.py:419
  21.9 1.9 %collective-permute-start.1 = (f32[11,40,128]{2,1,0:T(8,128)S(1)}, f32[11,40,128]{2,1,0:T(8,128)S(1)}, u32[]{:S(2)}, u32[]{:S(2)}) collective-permute-start(f32[11,40,128]{2,1,0:T(8,128)S(1)} %reshape.18.refs_1_), channel_id=1, source_target_pairs={{0,16},{16,0},{32,48},{48,32},{64,80},{80,64},{96,112},{112,96},{1... | collective-permute-start | bytes 675848 | tf_op jit(solution)/shard_map/ppermute | solution.py:420
  23.8 0.1 pad_add_fusion.refs_0_
  23.9 0.1 select_maximum_fusion.refs_4_
  24.0 1.6 %collective-permute-done.2.refs_3_ = f32[11,40,128]{2,1,0:T(8,128)S(1)} collective-permute-done((f32[11,40,128]{2,1,0:T(8,128)S(1)}, f32[11,40,128]{2,1,0:T(8,128)S(1)}, u32[]{:S(2)}, u32[]{:S(2)}) %collective-permute-start.2) | collective-permute-done | bytes 225312 | tf_op jit(solution)/shard_map/ppermute | solution.py:419
  25.5 0.0 collective-permute-done.1.refs_2_
  25.5 5.7 %march.1 = f32[16,8,384]{2,1,0:T(8,128)S(1)} custom-call(s32[2]{0:T(128)S(1)} %pad_add_fusion.refs_0_, f32[11,40,128]{2,1,0:T(8,128)S(1)} %reshape.18.refs_1_, f32[11,40,128]{2,1,0:T(8,128)S(1)} %collective-permute-done.1.refs_2_, f32[11,40,128]{2,1,0:T(8,128)S(1)} %collective-permute-done.2.refs_3_, f32[8,128]{1,0:T(8,128)S(1)} %select_maximum_fusion.refs_4_), custom_call_target="tpu_custom_call" | custom-call | tf_op jit(solution)/shard_map/march/pallas_call | solution.py:424
  31.3 13.7 %all_to_all.10.got_ref.refs_0_ = f32[16,8,384]{2,1,0:T(8,128)S(1)} all-to-all(f32[16,8,384]{2,1,0:T(8,128)S(1)} %march.1), channel_id=1, replica_groups=mesh['gx'=32,'row'=16] {'row'}, dimensions={0} | all-to-all | bytes 393216 | tf_op jit(solution)/shard_map/all_to_all | solution.py:439
  45.0 0.9 %reduce.2 = f32[32,8,128]{2,1,0:T(8,128)} custom-call(f32[16,8,384]{2,1,0:T(8,128)S(1)} %all_to_all.10.got_ref.refs_0_), custom_call_target="tpu_custom_call" | custom-call | tf_op jit(solution)/shard_map/reduce/pallas_call | solution.py:440
  45.9 9.9 %all-to-all-start.1 = ((f32[32,8,128]{2,1,0:T(8,128)}), f32[32,8,128]{2,1,0:T(8,128)S(1)}, u32[]{:S(2)}, u32[]{:S(2)}) async-start(f32[32,8,128]{2,1,0:T(8,128)} %reduce.2), calls=%async_computation.1 | async-start | bytes 262144 | tf_op jit(solution)/shard_map/all_to_all | solution.py:448
  55.8 1.2 %relay.1.refs_1_ = f32[20,8,256]{2,1,0:T(8,128)S(1)} custom-call(f32[16,8,384]{2,1,0:T(8,128)S(1)} %all_to_all.10.got_ref.refs_0_), custom_call_target="tpu_custom_call" | custom-call | tf_op jit(solution)/shard_map/relay/pallas_call | solution.py:449
  57.1 7.8 %all-to-all-done.1.refs_0_ = f32[32,8,128]{2,1,0:T(8,128)S(1)} async-done(((f32[32,8,128]{2,1,0:T(8,128)}), f32[32,8,128]{2,1,0:T(8,128)S(1)}, u32[]{:S(2)}, u32[]{:S(2)}) %all-to-all-start.1) | async-done | bytes 131104 | tf_op jit(solution)/shard_map/all_to_all | solution.py:448
  64.9 1.6 %final.1 = f32[20,8,256]{2,1,0:T(8,128)} custom-call(f32[32,8,128]{2,1,0:T(8,128)S(1)} %all-to-all-done.1.refs_0_, f32[20,8,256]{2,1,0:T(8,128)S(1)} %relay.1.refs_1_), custom_call_target="tpu_custom_call" | custom-call | tf_op jit(solution)/shard_map/final/pallas_call | solution.py:458
  (5 shorter events, 0.1 us)
Async XLA Ops:
  0.0 0.9 %copy-start = (f32[2,5,2,16,128]{4,3,2,1,0:T(8,128)S(1)}, f32[2,5,2,16,128]{4,3,2,1,0:T(8,128)}, u32[]{:S(2)}) copy-start(f32[2,5,2,16,128]{4,3,2,1,0:T(8,128)} %param.4) | copy-start | bytes 491524
  0.9 0.7 %copy-start.2 = (f32[101,2,16]{0,2,1:T(8,128)S(1)}, f32[101,2,16]{0,2,1:T(8,128)}, u32[]{:S(2)}) copy-start(f32[101,2,16]{0,2,1:T(8,128)} %param.5) | copy-start | bytes 38788
  1.6 15.5 %copy-start.1 = (f32[2,5,2,16,128]{4,3,2,1,0:T(8,128)S(1)}, f32[2,5,2,16,128]{4,3,2,1,0:T(8,128)}, u32[]{:S(2)}) copy-start(f32[2,5,2,16,128]{4,3,2,1,0:T(8,128)} %param.4) | copy-start | bytes 491524
  1.7 15.5 %collective-permute-start = (f32[11,2,4,128]{3,2,1,0:T(4,128)S(1)}, f32[11,2,4,128]{3,2,1,0:T(4,128)S(1)}, u32[]{:S(2)}, u32[]{:S(2)}) collective-permute-start(f32[11,2,4,128]{3,2,1,0:T(4,128)S(1)} %get-tuple-element.7), channel_id=1, source_target_pairs={{0,1},{1,2},{2,3},{3,4},{4,5},{5,6},{6,7},{7,8},{8,9},{9,10},{10,1... | collective-permute-start | bytes 135176 | tf_op jit(solution)/shard_map/ppermute | solution.py:414
  6.6 0.7 %copy-start.3 = (f32[1,10,10]{2,0,1:T(1,128)S(1)}, f32[1,10,10]{2,0,1:T(1,128)}, u32[]{:S(2)}) copy-start(f32[1,10,10]{2,0,1:T(1,128)} %param.6) | copy-start | bytes 1204
  17.2 8.3 %collective-permute-start.2 = (f32[11,40,128]{2,1,0:T(8,128)S(1)}, f32[11,40,128]{2,1,0:T(8,128)S(1)}, u32[]{:S(2)}, u32[]{:S(2)}) collective-permute-start(f32[11,40,128]{2,1,0:T(8,128)S(1)} %reshape.18.refs_1_), channel_id=1, source_target_pairs={{16,32},{32,16},{48,64},{64,48},{80,96},{96,80},{112,128},{128,112... | collective-permute-start | bytes 675848 | tf_op jit(solution)/shard_map/ppermute | solution.py:419
  21.9 3.6 %collective-permute-start.1 = (f32[11,40,128]{2,1,0:T(8,128)S(1)}, f32[11,40,128]{2,1,0:T(8,128)S(1)}, u32[]{:S(2)}, u32[]{:S(2)}) collective-permute-start(f32[11,40,128]{2,1,0:T(8,128)S(1)} %reshape.18.refs_1_), channel_id=1, source_target_pairs={{0,16},{16,0},{32,48},{48,32},{64,80},{80,64},{96,112},{112,96},{1... | collective-permute-start | bytes 675848 | tf_op jit(solution)/shard_map/ppermute | solution.py:420
  45.9 19.0 %all-to-all-start.1 = ((f32[32,8,128]{2,1,0:T(8,128)}), f32[32,8,128]{2,1,0:T(8,128)S(1)}, u32[]{:S(2)}, u32[]{:S(2)}) async-start(f32[32,8,128]{2,1,0:T(8,128)} %reduce.2), calls=%async_computation.1 | async-start | bytes 262144 | tf_op jit(solution)/shard_map/all_to_all | solution.py:448

commit v5 on v3

--- a/solution.py
+++ b/solution.py
@@ -112,24 +112,31 @@
 
 def march_kernel(
     n_var, wide_x, wide_r, count_x,
-    place_ref, mid_ref, mate_ref, far_ref, panel_ref,
-    out_ref, now_ref, next_ref, coeff_ref, packed_ref, parts_ref,
+    place_ref, edge_ref, own_ref, mate_edge_ref, mate_ref, far_edge_ref, far_ref, panel_ref,
+    out_ref, rows_ref, now_ref, next_ref, coeff_ref, packed_ref, parts_ref,
 ):
-    n_plane = mid_ref.shape[0] - 1
-    n_theta = mid_ref.shape[-1]
+    n_plane = own_ref.shape[0] - 1
+    n_theta = own_ref.shape[-1]
     n_tile = n_theta // ROWS
-    deep = wide_r + 2 * RIM
+    edge = edge_ref.shape[2]
+    deep = wide_r + edge
     n_pair = n_var * n_var
     used = (wide_x + 2 * RIM) * deep
 
-    mate_is_low = jnp.full((RIM * deep, n_theta), place_ref[0] % 2, jnp.int32) == 1
+    mate_is_low = place_ref[0] % 2 == 1
+    starts = (jnp.where(mate_is_low, 0, RIM + wide_x), jnp.where(mate_is_low, RIM + wide_x, 0))
+    places = (
+        (RIM, edge_ref, own_ref), (starts[0], mate_edge_ref, mate_ref), (starts[1], far_edge_ref, far_ref)
+    )
 
     def turn(plane):
-        mate, far = mate_ref[plane], far_ref[plane]
-        low = jnp.where(mate_is_low, mate, far)
-        high = jnp.where(mate_is_low, far, mate)
-        blank = jnp.zeros((LANES - used, n_theta), jnp.float32)
-        return jnp.concatenate([low, mid_ref[plane], high, blank], axis=0).T
+        for start, rim, inner in places:
+            for x in range(wide_x):
+                at = (start + x) * deep
+                rows_ref[plane, pl.ds(at, edge), :] = rim[plane, x]
+                rows_ref[plane, pl.ds(at + edge, wide_r), :] = inner[plane, x]
+        rows_ref[plane, used:, :] = jnp.zeros((LANES - used, n_theta), jnp.float32)
+        return rows_ref[plane].T
 
     for plane in range(n_plane):
         turned = turn(plane)
@@ -194,16 +201,23 @@
     group = wide_x * wide_r
     per_vreg = LANES // group
     n_wide = packed_ref.shape[-1] // LANES
+    at_own = lane - (RIM * deep + RIM)
+    mine = (at_own >= 0) & (at_own < wide_x * deep) & (at_own % deep < wide_r)
+    head = lane % group < wide_r
+    even = lane % (2 * group) < group
+    even_tail = (lane + LANES - deep) % (2 * group) < wide_r
 
     def second_step(tile, largest):
-        result = advance(next_ref, tile)
+        result = [jnp.where(mine, value, 0.0) for value in advance(next_ref, tile)]
         for v in range(n_wide):
-            packed = jnp.zeros((ROWS, LANES), jnp.float32)
-            for b in range(v * per_vreg, min((v + 1) * per_vreg, n_plane)):
-                for x in range(wide_x):
-                    target = (b % per_vreg) * group + x * wide_r
-                    shift = target - ((x + RIM) * deep + RIM)
-                    packed = placed_at(lane, target, wide_r, roll_lanes(result[b], shift), packed)
+            turned = [
+                roll_lanes(result[b], (b % per_vreg) * group - (RIM * deep + RIM))
+                for b in range(v * per_vreg, min((v + 1) * per_vreg, n_plane))
+            ]
+            evens, odds = tree(turned[::2], jnp.add), tree(turned[1::2], jnp.add)
+            heads = jnp.where(even, evens, odds)
+            tails = jnp.where(even_tail, evens, odds)
+            packed = jnp.where(head, heads, roll_lanes(tails, wide_r - deep))
             packed_ref[tile, :, v * LANES : (v + 1) * LANES] = packed
             largest = jnp.maximum(largest, jnp.abs(packed))
         return largest
@@ -229,10 +243,12 @@
         keep = lane < LANES - rest * group
         return jnp.where(keep, roll_lanes(value, -rest * group), roll_lanes(other, -rest * group))
 
-    pairs = [[None] * n_wide for _ in range(ROWS)]
     zero = jnp.zeros((ROWS, LANES), jnp.float32)
+    pairs = [[(zero, zero)] * n_wide for _ in range(ROWS)]
     for s in range(RING // 2 + 1):
         for v in range(n_wide):
+            if 2 * s == RING and v * per_vreg + s >= n_plane:
+                continue
             total, error = zero, zero
             for tile in range(n_tile):
                 a_high, a_low = parts_ref[0, tile, v], parts_ref[1, tile, v]
@@ -248,7 +264,7 @@
     row = lax.broadcasted_iota(jnp.int32, (ROWS, LANES), 0)
     sums = []
     for v in range(n_wide):
-        level = [pairs[s][v] if s <= RING // 2 else (zero, zero) for s in range(ROWS)]
+        level = [pairs[s][v] for s in range(ROWS)]
         half = ROWS // 2
         while half:
             joined = []
@@ -329,15 +345,13 @@
     for s in range(RING // 2 + 1):
         left_s, right_s = turned(left, s), turned(right, s)
         term = pair_add(two_prod(left, right_s), two_prod(left_s, right))
-        share = 1.0 if s % (RING // 2) else 0.5
+        share = 1.0 if s else 0.5
         row_s = tuple(share * part[s : s + 1, :] for part in inner)
         terms.append(pair_mul(term, row_s))
     total = pair_tree(terms)
+    total = pair_tree([pair_roll(total, -b, 1) for b in range(n_plane)])
     for shift in (4, 2, 1):
         total = pair_add(total, pair_roll(total, shift, 0))
-    total = pair_add(total, pair_roll(total, -RING // 2, 1))
-    total = pair_add(total, pair_roll(total, -RING // 4, 1))
-    total = pair_tree([total, pair_roll(total, -1, 1), pair_roll(total, -2, 1)])
 
     def everywhere(part, at):
         return jnp.broadcast_to(part[:, at : at + 1], (ROWS, LANES))
@@ -376,7 +390,6 @@
     count_x = lax.axis_size("gx")
     count_r = lax.axis_size("row")
     n_vec, n_var, wide_x, wide_r, n_theta = test_vectors.shape
-    n_coeff = base_coeffs.shape[0]
     n_plane = n_vec * n_var
     at_x, at_r = lax.axis_index("gx"), lax.axis_index("row")
 
@@ -386,26 +399,31 @@
     panel = jnp.pad(panel, ((0, ROWS - n_var), (PANEL, LANES - PANEL - 2 * n_plane)))
 
     field = test_vectors.reshape((n_plane, wide_x, wide_r, n_theta))
-    turned = base_coeffs.transpose(1, 2, 0)
-    turned = jnp.pad(turned, ((0, 0), (0, 0), (0, n_theta - n_coeff)))
+    def by_cell(coeffs):
+        turned = jnp.pad(coeffs.transpose(1, 2, 0), ((0, 0), (0, 0), (0, n_theta - coeffs.shape[0])))
+        return turned[None]
+
+    edge = jnp.concatenate([field[:, :, -2 * RIM :], by_cell(base_coeffs[:, :, -2 * RIM :])], axis=0)
     ring = [(i, (i + 1) % count_r) for i in range(count_r)]
-    edge = jnp.concatenate([field[:, :, -2 * RIM :], turned[None, :, -2 * RIM :]], axis=0)
+    outer = [(i, i + 1 if i % 2 else i - 1) for i in range(1, count_x - 1)]
+    inner = [(i, i ^ 1) for i in range(count_x)]
+    sent_edge = edge
     edge = lax.ppermute(edge, "row", ring)
-    both = jnp.concatenate([field, turned[None]], axis=0)
-    both = jnp.concatenate([edge, both], axis=2)
-    both = both.reshape((n_plane + 1, wide_x * (wide_r + 2 * RIM), n_theta))
-    outer = [(i, i + 1 if i % 2 else i - 1) for i in range(1, count_x - 1)]
-    far = lax.ppermute(both, "gx", outer)
-    mate = lax.ppermute(both, "gx", [(i, i ^ 1) for i in range(count_x)])
-
+    _, coeffs = lax.optimization_barrier((sent_edge, base_coeffs))
+    own = jnp.concatenate([field, by_cell(coeffs)], axis=0)
+    far = lax.ppermute(own, "gx", outer)
+    mate = lax.ppermute(own, "gx", inner)
+    far_edge = lax.ppermute(edge, "gx", outer)
+    mate_edge = lax.ppermute(edge, "gx", inner)
     n_wide = 3
     n_tile = n_theta // ROWS
     sent = pl.pallas_call(
         lambda *refs: march_kernel(n_var, wide_x, wide_r, count_x, *refs),
         out_shape=jax.ShapeDtypeStruct((n_tile, ROWS, n_wide * LANES), jnp.float32),
-        in_specs=[pl.BlockSpec(memory_space=pltpu.SMEM)] + [VMEM] * 4,
+        in_specs=[pl.BlockSpec(memory_space=pltpu.SMEM)] + [VMEM] * 7,
         out_specs=VMEM,
         scratch_shapes=[
+            pltpu.VMEM((n_plane + 1, LANES, n_theta), jnp.float32),
             pltpu.VMEM((n_plane, n_theta + 2 * ROWS, LANES), jnp.float32),
             pltpu.VMEM((n_plane, n_theta + 2 * ROWS, LANES), jnp.float32),
             pltpu.VMEM((n_theta + ROWS, LANES), jnp.float32),
@@ -414,7 +432,7 @@
         ],
         compiler_params=PARAMS,
         name="march",
-    )(jnp.stack([at_x, at_r]), both, mate, far, panel)
+    )(jnp.stack([at_x, at_r]), edge, own, mate_edge, mate, far_edge, far, panel)
     got = lax.all_to_all(sent, "row", 0, 0, tiled=True)
     stats = pl.pallas_call(
         reduce_kernel,

time: 66.8 us -> 69.2 us (1.036)
  waiting for transfers between devices: 18 us -> 11.3 us
  starting transfers between devices: 21.3 us -> 26.6 us
  blocking collectives: 13.7 us -> 17 us
    ppermute x1, waiting for transfers between devices: 8.65 us -> 2.32 us  [body(): edge = lax.ppermute(edge, 'row', ring)]
    ppermute x2 -> x4, starting transfers between devices: 6.56 us -> 12.6 us  [the longest x1 4.14 us: body(): far_edge = lax.ppermute(edge, 'gx', outer)]
    all_to_all x1, blocking collectives: 13.7 us -> 17 us  [body(): got = lax.all_to_all(sent, 'row', 0, 0, tiled=True)]
    transpose x0 -> x1, local copies, waits for them, and re-layouts: none -> 0.74 us  [by_cell(): coeffs.transpose(1, 2, 0)]
    broadcast_in_dim x2, local copies, waits for them, and re-layouts: 0.74 us -> 0.01 us  [by_cell(): return turned[None]]
    all_to_all x1, starting transfers between devices: 9.92 us -> 9.19 us  [body(): stats = lax.all_to_all(stats, 'gx', 0, 0, tiled=True)]
    ppermute x2 -> x4, waiting for transfers between devices: 1.55 us -> 1.12 us  [the longest x1 1.11 us: body(): mate_edge = lax.ppermute(edge, 'gx', inner)]
  transfers between devices with their start and end apart: 4 -> 6, of which waited for: 3 -> 3; matrix products, arithmetic and copies ran while one was open for 2% -> 2% of each run, Pallas kernels for 2% -> 2%
where the time goes in v5:
time: 69.2 us; the launch traced here: 68.8 us
  starting transfers between devices  26.6 us (38%)
  blocking collectives  17 us (25%)
  waiting for transfers between devices  11.3 us (16%)
  Pallas kernels  9.91 us (14%)
  local copies, waits for them, and re-layouts  1.69 us (2%)
  other arithmetic  1.47 us (2%)
  between operations  0.8 us (1%)
    all_to_all x1, blocking collectives, body(): got = lax.all_to_all(sent, 'row', 0, 0, tiled=True)  17 us
    all_to_all x1, starting transfers between devices, body(): stats = lax.all_to_all(stats, 'gx', 0, 0, tiled=True)  9.19 us
    all_to_all x1, waiting for transfers between devices, body(): stats = lax.all_to_all(stats, 'gx', 0, 0, tiled=True)  7.83 us
    pallas_call x1, Pallas kernels, body(): pl.pallas_call(lambda *refs: march_kernel(n_var, wide_x, wide_r, count_x,...  6.22 us
    ppermute x1, starting transfers between devices, body(): edge = lax.ppermute(edge, 'row', ring)  4.83 us
    ppermute x1, starting transfers between devices, body(): far_edge = lax.ppermute(edge, 'gx', outer)  4.14 us
    ppermute x1, starting transfers between devices, body(): far = lax.ppermute(own, 'gx', outer)  4.05 us
    ppermute x1, starting transfers between devices, body(): mate = lax.ppermute(own, 'gx', inner)  2.5 us
  transfers between devices with their start and end apart: 6, of which 3 were waited for; matrix products, arithmetic and copies ran while one was open for 2% of the time, Pallas kernels for 2%

profile of v5, /device:TPU:1, one launch (start us, length us, event | category | flops | bytes accessed | tf_op | source)
XLA Modules:
  0.0 68.8 jit_solution(6702367584469520203)
XLA Ops:
  0.0 0.7 %slice_bitcast_fusion.2 = f32[2,4,101]{2,1,0:T(4,128)S(1)} fusion(f32[101,2,16]{0,2,1:T(8,128)} %param.5), kind=kLoop, calls=%fused_computation.14 | loop fusion | bytes 6464 | tf_op jit(solution)/shard_map/transpose | solution.py:403
  0.7 0.9 %slice.24 = f32[10,2,4,128]{3,2,1,0:T(4,128)S(1)} slice(f32[10,2,16,128]{3,2,1,0:T(8,128)} %bitcast.17), slice={[0:10], [0:2], [12:16], [0:128]} | slice | bytes 81920 | tf_op jit(solution)/shard_map/slice | solution.py:406
  1.6 0.0 copy-start.1
  1.7 4.8 %collective-permute-start = (f32[11,2,4,128]{3,2,1,0:T(4,128)S(1)}, f32[11,2,4,128]{3,2,1,0:T(4,128)S(1)}, u32[]{:S(2)}, u32[]{:S(2)}) collective-permute-start(f32[11,2,4,128]{3,2,1,0:T(4,128)S(1)} %pad_maximum_fusion.1), channel_id=1, source_target_pairs={{0,1},{1,2},{2,3},{3,4},{4,5},{5,6},{6,7},{7,8},{8,9},{9,10},{10,1... | collective-permute-start | bytes 135176 | tf_op jit(solution)/shard_map/ppermute | solution.py:411
  6.6 4.0 %collective-permute-start.4 = (f32[11,2,16,128]{3,2,1,0:T(8,128)S(1)}, f32[11,2,16,128]{3,2,1,0:T(8,128)S(1)}, u32[]{:S(2)}, u32[]{:S(2)}) collective-permute-start(f32[11,2,16,128]{3,2,1,0:T(8,128)S(1)} %pad_maximum_fusion.refs_2_), channel_id=1, source_target_pairs={{16,32},{32,16},{48,64},{64,48},{80,96},{96,80},{112,128},{128,112... | collective-permute-start | bytes 540680 | tf_op jit(solution)/shard_map/ppermute | solution.py:414
  10.6 2.5 %collective-permute-start.2 = (f32[11,2,16,128]{3,2,1,0:T(8,128)S(1)}, f32[11,2,16,128]{3,2,1,0:T(8,128)S(1)}, u32[]{:S(2)}, u32[]{:S(2)}) collective-permute-start(f32[11,2,16,128]{3,2,1,0:T(8,128)S(1)} %pad_maximum_fusion.refs_2_), channel_id=1, source_target_pairs={{0,16},{16,0},{32,48},{48,32},{64,80},{80,64},{96,112},{112,96},{1... | collective-permute-start | bytes 540680 | tf_op jit(solution)/shard_map/ppermute | solution.py:415
  13.1 0.0 copy-start.2
  13.8 0.0 copy-done.2
  13.8 0.7 abs_reduce_fusion
  14.5 0.6 fusion
  15.1 0.1 select_maximum_fusion.refs_7_
  15.2 2.3 %collective-permute-done.refs_1_ = f32[11,2,4,128]{3,2,1,0:T(4,128)S(1)} collective-permute-done((f32[11,2,4,128]{3,2,1,0:T(4,128)S(1)}, f32[11,2,4,128]{3,2,1,0:T(4,128)S(1)}, u32[]{:S(2)}, u32[]{:S(2)}) %collective-permute-start) | collective-permute-done | bytes 45088 | tf_op jit(solution)/shard_map/ppermute | solution.py:411
  17.5 4.1 %collective-permute-start.3 = (f32[11,2,4,128]{3,2,1,0:T(4,128)S(1)}, f32[11,2,4,128]{3,2,1,0:T(4,128)S(1)}, u32[]{:S(2)}, u32[]{:S(2)}) collective-permute-start(f32[11,2,4,128]{3,2,1,0:T(4,128)S(1)} %collective-permute-done.refs_1_), channel_id=1, source_target_pairs={{16,32},{32,16},{48,64},{64,48},{80,96},{96,80},{112,128},{128,112... | collective-permute-start | bytes 135176 | tf_op jit(solution)/shard_map/ppermute | solution.py:416
  21.7 1.9 %collective-permute-start.1 = (f32[11,2,4,128]{3,2,1,0:T(4,128)S(1)}, f32[11,2,4,128]{3,2,1,0:T(4,128)S(1)}, u32[]{:S(2)}, u32[]{:S(2)}) collective-permute-start(f32[11,2,4,128]{3,2,1,0:T(4,128)S(1)} %collective-permute-done.refs_1_), channel_id=1, source_target_pairs={{0,16},{16,0},{32,48},{48,32},{64,80},{80,64},{96,112},{112,96},{1... | collective-permute-start | bytes 135176 | tf_op jit(solution)/shard_map/ppermute | solution.py:417
  23.6 0.1 pad_add_fusion.refs_0_
  23.7 0.0 collective-permute-done.3.refs_5_
  23.7 1.1 %collective-permute-done.1.refs_3_ = f32[11,2,4,128]{3,2,1,0:T(4,128)S(1)} collective-permute-done((f32[11,2,4,128]{3,2,1,0:T(4,128)S(1)}, f32[11,2,4,128]{3,2,1,0:T(4,128)S(1)}, u32[]{:S(2)}, u32[]{:S(2)}) %collective-permute-start.1) | collective-permute-done | bytes 45088 | tf_op jit(solution)/shard_map/ppermute | solution.py:417
  24.8 6.2 %march.1 = f32[16,8,384]{2,1,0:T(8,128)S(1)} custom-call(s32[2]{0:T(128)S(1)} %pad_add_fusion.refs_0_, f32[11,2,4,128]{3,2,1,0:T(4,128)S(1)} %collective-permute-done.refs_1_, f32[11,2,16,128]{3,2,1,0:T(8,128)S(1)} %pad_maximum_fusion.refs_2_, f32[11,2,4,128]{3,2,1,0:T(4,128)S(1)} %collective-permute-done.1.refs_3_, ...), custom_call_target="tpu_custom_call" | custom-call | tf_op jit(solution)/shard_map/march/pallas_call | solution.py:420
  31.0 17.0 %all_to_all.10.got_ref.refs_0_ = f32[16,8,384]{2,1,0:T(8,128)S(1)} all-to-all(f32[16,8,384]{2,1,0:T(8,128)S(1)} %march.1), channel_id=1, replica_groups=mesh['gx'=32,'row'=16] {'row'}, dimensions={0} | all-to-all | bytes 393216 | tf_op jit(solution)/shard_map/all_to_all | solution.py:436
  48.0 0.9 %reduce.2 = f32[32,8,128]{2,1,0:T(8,128)} custom-call(f32[16,8,384]{2,1,0:T(8,128)S(1)} %all_to_all.10.got_ref.refs_0_), custom_call_target="tpu_custom_call" | custom-call | tf_op jit(solution)/shard_map/reduce/pallas_call | solution.py:437
  48.9 9.2 %all-to-all-start.1 = ((f32[32,8,128]{2,1,0:T(8,128)}), f32[32,8,128]{2,1,0:T(8,128)S(1)}, u32[]{:S(2)}, u32[]{:S(2)}) async-start(f32[32,8,128]{2,1,0:T(8,128)} %reduce.2), calls=%async_computation.1 | async-start | bytes 262144 | tf_op jit(solution)/shard_map/all_to_all | solution.py:445
  58.1 1.2 %relay.1.refs_1_ = f32[20,8,256]{2,1,0:T(8,128)S(1)} custom-call(f32[16,8,384]{2,1,0:T(8,128)S(1)} %all_to_all.10.got_ref.refs_0_), custom_call_target="tpu_custom_call" | custom-call | tf_op jit(solution)/shard_map/relay/pallas_call | solution.py:446
  59.4 7.8 %all-to-all-done.1.refs_0_ = f32[32,8,128]{2,1,0:T(8,128)S(1)} async-done(((f32[32,8,128]{2,1,0:T(8,128)}), f32[32,8,128]{2,1,0:T(8,128)S(1)}, u32[]{:S(2)}, u32[]{:S(2)}) %all-to-all-start.1) | async-done | bytes 131104 | tf_op jit(solution)/shard_map/all_to_all | solution.py:445
  67.2 1.6 %final.1 = f32[20,8,256]{2,1,0:T(8,128)} custom-call(f32[32,8,128]{2,1,0:T(8,128)S(1)} %all-to-all-done.1.refs_0_, f32[20,8,256]{2,1,0:T(8,128)S(1)} %relay.1.refs_1_), custom_call_target="tpu_custom_call" | custom-call | tf_op jit(solution)/shard_map/final/pallas_call | solution.py:455
  (10 shorter events, 0.1 us)
Async XLA Ops:
  0.0 6.5 %copy-start = (f32[2,5,2,16,128]{4,3,2,1,0:T(8,128)S(1)}, f32[2,5,2,16,128]{4,3,2,1,0:T(8,128)}, u32[]{:S(2)}) copy-start(f32[2,5,2,16,128]{4,3,2,1,0:T(8,128)} %param.4) | copy-start | bytes 491524
  1.6 4.9 %copy-start.1 = (f32[101,2,16]{0,2,1:T(8,128)S(1)}, f32[101,2,16]{0,2,1:T(8,128)}, u32[]{:S(2)}) copy-start(f32[101,2,16]{0,2,1:T(8,128)} %param.5) | copy-start | bytes 38788
  1.7 15.9 %collective-permute-start = (f32[11,2,4,128]{3,2,1,0:T(4,128)S(1)}, f32[11,2,4,128]{3,2,1,0:T(4,128)S(1)}, u32[]{:S(2)}, u32[]{:S(2)}) collective-permute-start(f32[11,2,4,128]{3,2,1,0:T(4,128)S(1)} %pad_maximum_fusion.1), channel_id=1, source_target_pairs={{0,1},{1,2},{2,3},{3,4},{4,5},{5,6},{6,7},{7,8},{8,9},{9,10},{10,1... | collective-permute-start | bytes 135176 | tf_op jit(solution)/shard_map/ppermute | solution.py:411
  6.6 18.2 %collective-permute-start.4 = (f32[11,2,16,128]{3,2,1,0:T(8,128)S(1)}, f32[11,2,16,128]{3,2,1,0:T(8,128)S(1)}, u32[]{:S(2)}, u32[]{:S(2)}) collective-permute-start(f32[11,2,16,128]{3,2,1,0:T(8,128)S(1)} %pad_maximum_fusion.refs_2_), channel_id=1, source_target_pairs={{16,32},{32,16},{48,64},{64,48},{80,96},{96,80},{112,128},{128,112... | collective-permute-start | bytes 540680 | tf_op jit(solution)/shard_map/ppermute | solution.py:414
  10.6 14.2 %collective-permute-start.2 = (f32[11,2,16,128]{3,2,1,0:T(8,128)S(1)}, f32[11,2,16,128]{3,2,1,0:T(8,128)S(1)}, u32[]{:S(2)}, u32[]{:S(2)}) collective-permute-start(f32[11,2,16,128]{3,2,1,0:T(8,128)S(1)} %pad_maximum_fusion.refs_2_), channel_id=1, source_target_pairs={{0,16},{16,0},{32,48},{48,32},{64,80},{80,64},{96,112},{112,96},{1... | collective-permute-start | bytes 540680 | tf_op jit(solution)/shard_map/ppermute | solution.py:415
  13.1 0.7 %copy-start.2 = (f32[1,10,10]{2,0,1:T(1,128)S(1)}, f32[1,10,10]{2,0,1:T(1,128)}, u32[]{:S(2)}) copy-start(f32[1,10,10]{2,0,1:T(1,128)} %param.6) | copy-start | bytes 1204
  17.5 6.2 %collective-permute-start.3 = (f32[11,2,4,128]{3,2,1,0:T(4,128)S(1)}, f32[11,2,4,128]{3,2,1,0:T(4,128)S(1)}, u32[]{:S(2)}, u32[]{:S(2)}) collective-permute-start(f32[11,2,4,128]{3,2,1,0:T(4,128)S(1)} %collective-permute-done.refs_1_), channel_id=1, source_target_pairs={{16,32},{32,16},{48,64},{64,48},{80,96},{96,80},{112,128},{128,112... | collective-permute-start | bytes 135176 | tf_op jit(solution)/shard_map/ppermute | solution.py:416
  21.7 3.1 %collective-permute-start.1 = (f32[11,2,4,128]{3,2,1,0:T(4,128)S(1)}, f32[11,2,4,128]{3,2,1,0:T(4,128)S(1)}, u32[]{:S(2)}, u32[]{:S(2)}) collective-permute-start(f32[11,2,4,128]{3,2,1,0:T(4,128)S(1)} %collective-permute-done.refs_1_), channel_id=1, source_target_pairs={{0,16},{16,0},{32,48},{48,32},{64,80},{80,64},{96,112},{112,96},{1... | collective-permute-start | bytes 135176 | tf_op jit(solution)/shard_map/ppermute | solution.py:417
  48.9 18.3 %all-to-all-start.1 = ((f32[32,8,128]{2,1,0:T(8,128)}), f32[32,8,128]{2,1,0:T(8,128)S(1)}, u32[]{:S(2)}, u32[]{:S(2)}) async-start(f32[32,8,128]{2,1,0:T(8,128)} %reduce.2), calls=%async_computation.1 | async-start | bytes 262144 | tf_op jit(solution)/shard_map/all_to_all | solution.py:445

commit v6 on v4

--- a/solution.py
+++ b/solution.py
@@ -283,14 +283,13 @@
         out_ref[tile, :, last:] = jnp.where(lane < HIGH, packed_ref[tile, :, last:], stats)
 
 
-def prepare_kernel(field_ref, coeff_ref, edge_ref, turned_ref):
-    n_plane, _, wide_r, _ = field_ref.shape
+def prepare_kernel(tail_ref, coeff_ref, edge_ref, turned_ref):
+    n_plane = tail_ref.shape[0]
     n_coeff = coeff_ref.shape[-1]
-    start = wide_r - edge_ref.shape[2]
-    edge_ref[:n_plane] = field_ref[:, :, start:, :]
+    edge_ref[:n_plane] = tail_ref[...]
     turned_ref[...] = jnp.zeros_like(turned_ref)
     turned_ref[:, :, :n_coeff] = coeff_ref[...]
-    edge_ref[n_plane] = turned_ref[:, start:, :]
+    edge_ref[n_plane] = turned_ref[:, turned_ref.shape[1] - edge_ref.shape[2] :, :]
 
 
 def reduce_kernel(got_ref, out_ref):
@@ -409,7 +408,7 @@
         out_specs=(VMEM, VMEM),
         compiler_params=PARAMS,
         name="prepare",
-    )(field, base_coeffs.transpose(1, 2, 0))
+    )(field[:, :, wide_r - 2 * RIM :], base_coeffs.transpose(1, 2, 0))
     ring = [(i, (i + 1) % count_r) for i in range(count_r)]
     edge = lax.ppermute(edge, "row", ring)
     both = jnp.concatenate([field, turned[None]], axis=0)

time: 66.9 us -> 66 us (0.987)
  local copies, waits for them, and re-layouts: 1.69 us -> 1 us
    unnamed x8 -> x6, local copies, waits for them, and re-layouts: 1.66 us -> 0.01 us
    slice x0 -> x1, local copies, waits for them, and re-layouts: none -> 0.97 us  [body(): field[:, :, wide_r - 2 * RIM:]]
where the time goes in v6:
time: 66 us; the launch traced here: 65.7 us
  starting transfers between devices  21.3 us (32%)
  waiting for transfers between devices  17.9 us (27%)
  blocking collectives  13.7 us (21%)
  Pallas kernels  9.44 us (14%)
  other arithmetic  1.55 us (2%)
  local copies, waits for them, and re-layouts  1 us (2%)
  between operations  0.75 us (1%)
    all_to_all x1, blocking collectives, body(): got = lax.all_to_all(sent, 'row', 0, 0, tiled=True)  13.7 us
    all_to_all x1, starting transfers between devices, body(): stats = lax.all_to_all(stats, 'gx', 0, 0, tiled=True)  9.92 us
    ppermute x1, waiting for transfers between devices, body(): edge = lax.ppermute(edge, 'row', ring)  8.51 us
    all_to_all x1, waiting for transfers between devices, body(): stats = lax.all_to_all(stats, 'gx', 0, 0, tiled=True)  7.83 us
    pallas_call x1, Pallas kernels, body(): pl.pallas_call(lambda *refs: march_kernel(n_var, wide_x, wide_r, count_x,...  5.74 us
    ppermute x1, starting transfers between devices, body(): edge = lax.ppermute(edge, 'row', ring)  4.83 us
    ppermute x1, starting transfers between devices, body(): far = lax.ppermute(both, 'gx', outer)  4.63 us
    ppermute x1, starting transfers between devices, body(): mate = lax.ppermute(both, 'gx', [(i, i ^ 1) for i in range(count_x)])  1.92 us
  transfers between devices with their start and end apart: 4, of which 3 were waited for; matrix products, arithmetic and copies ran while one was open for 2% of the time, Pallas kernels for 2%

profile of v6, /device:TPU:1, one launch (start us, length us, event | category | flops | bytes accessed | tf_op | source)
XLA Modules:
  0.0 65.7 jit_solution(3583298449901831116)
XLA Ops:
  0.0 0.0 copy-start.2
  0.0 0.0 copy-start
  0.0 0.0 copy-start.1
  0.0 1.0 %slice.20.tail_ref = f32[10,2,4,128]{3,2,1,0:T(4,128)S(1)} slice(f32[10,2,16,128]{3,2,1,0:T(8,128)} %bitcast.14), slice={[0:10], [0:2], [12:16], [0:128]} | slice | bytes 81920 | tf_op jit(solution)/shard_map/slice | solution.py:411
  1.0 0.0 copy-done
  1.0 4.8 %collective-permute-start = (f32[11,2,4,128]{3,2,1,0:T(4,128)S(1)}, f32[11,2,4,128]{3,2,1,0:T(4,128)S(1)}, u32[]{:S(2)}, u32[]{:S(2)}) collective-permute-start(f32[11,2,4,128]{3,2,1,0:T(4,128)S(1)} %get-tuple-element.7), channel_id=1, source_target_pairs={{0,1},{1,2},{2,3},{3,4},{4,5},{5,6},{6,7},{7,8},{8,9},{9,10},{10,1... | collective-permute-start | bytes 135176 | tf_op jit(solution)/shard_map/ppermute | solution.py:413
  6.5 0.0 copy-done.2
  6.5 0.7 %abs_reduce_fusion = f32[]{:T(128)} fusion(f32[1,10,10]{2,0,1:T(1,128)S(1)} %copy-done.2), kind=kLoop, calls=%fused_computation.5 | loop fusion | flops 199 | bytes 404 | tf_op jit(solution)/shard_map/reduce_max | solution.py:395
  7.2 0.7 %fusion = f32[1,10,10]{2,1,0:T(8,128)S(1)} fusion(f32[1,10,10]{2,0,1:T(1,128)S(1)} %copy-done.2, f32[]{:T(128)} %abs_reduce_fusion, pred[]{:T(512)S(6)} %eq.3), kind=kLoop, calls=%fused_computation.2 | loop fusion | flops 200 | bytes 805 | tf_op jit(solution)/shard_map/jit(_where)/select_n | solution.py:396
  7.9 8.5 %collective-permute-done = f32[11,2,4,128]{3,2,1,0:T(4,128)S(1)} collective-permute-done((f32[11,2,4,128]{3,2,1,0:T(4,128)S(1)}, f32[11,2,4,128]{3,2,1,0:T(4,128)S(1)}, u32[]{:S(2)}, u32[]{:S(2)}) %collective-permute-start) | collective-permute-done | bytes 45088 | tf_op jit(solution)/shard_map/ppermute | solution.py:413
  16.4 0.0 copy-done.1
  16.5 4.6 %collective-permute-start.2 = (f32[11,40,128]{2,1,0:T(8,128)S(1)}, f32[11,40,128]{2,1,0:T(8,128)S(1)}, u32[]{:S(2)}, u32[]{:S(2)}) collective-permute-start(f32[11,40,128]{2,1,0:T(8,128)S(1)} %reshape.18.refs_1_), channel_id=1, source_target_pairs={{16,32},{32,16},{48,64},{64,48},{80,96},{96,80},{112,128},{128,112... | collective-permute-start | bytes 675848 | tf_op jit(solution)/shard_map/ppermute | solution.py:418
  21.1 1.9 %collective-permute-start.1 = (f32[11,40,128]{2,1,0:T(8,128)S(1)}, f32[11,40,128]{2,1,0:T(8,128)S(1)}, u32[]{:S(2)}, u32[]{:S(2)}) collective-permute-start(f32[11,40,128]{2,1,0:T(8,128)S(1)} %reshape.18.refs_1_), channel_id=1, source_target_pairs={{0,16},{16,0},{32,48},{48,32},{64,80},{80,64},{96,112},{112,96},{1... | collective-permute-start | bytes 675848 | tf_op jit(solution)/shard_map/ppermute | solution.py:419
  23.0 0.1 pad_add_fusion.refs_0_
  23.1 0.1 select_maximum_fusion.refs_4_
  23.2 1.6 %collective-permute-done.2.refs_3_ = f32[11,40,128]{2,1,0:T(8,128)S(1)} collective-permute-done((f32[11,40,128]{2,1,0:T(8,128)S(1)}, f32[11,40,128]{2,1,0:T(8,128)S(1)}, u32[]{:S(2)}, u32[]{:S(2)}) %collective-permute-start.2) | collective-permute-done | bytes 225312 | tf_op jit(solution)/shard_map/ppermute | solution.py:418
  24.7 0.0 collective-permute-done.1.refs_2_
  24.7 5.7 %march.1 = f32[16,8,384]{2,1,0:T(8,128)S(1)} custom-call(s32[2]{0:T(128)S(1)} %pad_add_fusion.refs_0_, f32[11,40,128]{2,1,0:T(8,128)S(1)} %reshape.18.refs_1_, f32[11,40,128]{2,1,0:T(8,128)S(1)} %collective-permute-done.1.refs_2_, f32[11,40,128]{2,1,0:T(8,128)S(1)} %collective-permute-done.2.refs_3_, f32[8,128]{1,0:T(8,128)S(1)} %select_maximum_fusion.refs_4_), custom_call_target="tpu_custom_call" | custom-call | tf_op jit(solution)/shard_map/march/pallas_call | solution.py:423
  30.5 13.7 %all_to_all.10.got_ref.refs_0_ = f32[16,8,384]{2,1,0:T(8,128)S(1)} all-to-all(f32[16,8,384]{2,1,0:T(8,128)S(1)} %march.1), channel_id=1, replica_groups=mesh['gx'=32,'row'=16] {'row'}, dimensions={0} | all-to-all | bytes 393216 | tf_op jit(solution)/shard_map/all_to_all | solution.py:438
  44.2 0.9 %reduce.2 = f32[32,8,128]{2,1,0:T(8,128)} custom-call(f32[16,8,384]{2,1,0:T(8,128)S(1)} %all_to_all.10.got_ref.refs_0_), custom_call_target="tpu_custom_call" | custom-call | tf_op jit(solution)/shard_map/reduce/pallas_call | solution.py:439
  45.1 9.9 %all-to-all-start.1 = ((f32[32,8,128]{2,1,0:T(8,128)}), f32[32,8,128]{2,1,0:T(8,128)S(1)}, u32[]{:S(2)}, u32[]{:S(2)}) async-start(f32[32,8,128]{2,1,0:T(8,128)} %reduce.2), calls=%async_computation.1 | async-start | bytes 262144 | tf_op jit(solution)/shard_map/all_to_all | solution.py:447
  55.1 1.2 %relay.1.refs_1_ = f32[20,8,256]{2,1,0:T(8,128)S(1)} custom-call(f32[16,8,384]{2,1,0:T(8,128)S(1)} %all_to_all.10.got_ref.refs_0_), custom_call_target="tpu_custom_call" | custom-call | tf_op jit(solution)/shard_map/relay/pallas_call | solution.py:448
  56.3 7.8 %all-to-all-done.1.refs_0_ = f32[32,8,128]{2,1,0:T(8,128)S(1)} async-done(((f32[32,8,128]{2,1,0:T(8,128)}), f32[32,8,128]{2,1,0:T(8,128)S(1)}, u32[]{:S(2)}, u32[]{:S(2)}) %all-to-all-start.1) | async-done | bytes 131104 | tf_op jit(solution)/shard_map/all_to_all | solution.py:447
  64.1 1.6 %final.1 = f32[20,8,256]{2,1,0:T(8,128)} custom-call(f32[32,8,128]{2,1,0:T(8,128)S(1)} %all-to-all-done.1.refs_0_, f32[20,8,256]{2,1,0:T(8,128)S(1)} %relay.1.refs_1_), custom_call_target="tpu_custom_call" | custom-call | tf_op jit(solution)/shard_map/final/pallas_call | solution.py:457
  (4 shorter events, 0.1 us)
Async XLA Ops:
  0.0 6.5 %copy-start.2 = (f32[1,10,10]{2,0,1:T(1,128)S(1)}, f32[1,10,10]{2,0,1:T(1,128)}, u32[]{:S(2)}) copy-start(f32[1,10,10]{2,0,1:T(1,128)} %param.6) | copy-start | bytes 1204
  0.0 1.0 %copy-start = (f32[101,2,16]{0,2,1:T(8,128)S(1)}, f32[101,2,16]{0,2,1:T(8,128)}, u32[]{:S(2)}) copy-start(f32[101,2,16]{0,2,1:T(8,128)} %param.5) | copy-start | bytes 38788
  0.0 16.4 %copy-start.1 = (f32[2,5,2,16,128]{4,3,2,1,0:T(8,128)S(1)}, f32[2,5,2,16,128]{4,3,2,1,0:T(8,128)}, u32[]{:S(2)}) copy-start(f32[2,5,2,16,128]{4,3,2,1,0:T(8,128)} %param.4) | copy-start | bytes 491524
  1.0 15.4 %collective-permute-start = (f32[11,2,4,128]{3,2,1,0:T(4,128)S(1)}, f32[11,2,4,128]{3,2,1,0:T(4,128)S(1)}, u32[]{:S(2)}, u32[]{:S(2)}) collective-permute-start(f32[11,2,4,128]{3,2,1,0:T(4,128)S(1)} %get-tuple-element.7), channel_id=1, source_target_pairs={{0,1},{1,2},{2,3},{3,4},{4,5},{5,6},{6,7},{7,8},{8,9},{9,10},{10,1... | collective-permute-start | bytes 135176 | tf_op jit(solution)/shard_map/ppermute | solution.py:413
  16.5 8.3 %collective-permute-start.2 = (f32[11,40,128]{2,1,0:T(8,128)S(1)}, f32[11,40,128]{2,1,0:T(8,128)S(1)}, u32[]{:S(2)}, u32[]{:S(2)}) collective-permute-start(f32[11,40,128]{2,1,0:T(8,128)S(1)} %reshape.18.refs_1_), channel_id=1, source_target_pairs={{16,32},{32,16},{48,64},{64,48},{80,96},{96,80},{112,128},{128,112... | collective-permute-start | bytes 675848 | tf_op jit(solution)/shard_map/ppermute | solution.py:418
  21.1 3.6 %collective-permute-start.1 = (f32[11,40,128]{2,1,0:T(8,128)S(1)}, f32[11,40,128]{2,1,0:T(8,128)S(1)}, u32[]{:S(2)}, u32[]{:S(2)}) collective-permute-start(f32[11,40,128]{2,1,0:T(8,128)S(1)} %reshape.18.refs_1_), channel_id=1, source_target_pairs={{0,16},{16,0},{32,48},{48,32},{64,80},{80,64},{96,112},{112,96},{1... | collective-permute-start | bytes 675848 | tf_op jit(solution)/shard_map/ppermute | solution.py:419
  45.1 19.0 %all-to-all-start.1 = ((f32[32,8,128]{2,1,0:T(8,128)}), f32[32,8,128]{2,1,0:T(8,128)S(1)}, u32[]{:S(2)}, u32[]{:S(2)}) async-start(f32[32,8,128]{2,1,0:T(8,128)} %reduce.2), calls=%async_computation.1 | async-start | bytes 262144 | tf_op jit(solution)/shard_map/all_to_all | solution.py:447

commit v7 on v6

--- a/solution.py
+++ b/solution.py
@@ -392,11 +392,6 @@
     n_plane = n_vec * n_var
     at_x, at_r = lax.axis_index("gx"), lax.axis_index("row")
 
-    panel = panel_set[0] / jnp.max(jnp.abs(panel_set[0]))
-    panel = jnp.where(at_x * count_r + at_r == owner_index[0], panel, 0.0)
-    panel = jnp.concatenate([panel[:n_var], panel[n_var:]], axis=1)
-    panel = jnp.pad(panel, ((0, ROWS - n_var), (PANEL, LANES - PANEL - 2 * n_plane)))
-
     field = test_vectors.reshape((n_plane, wide_x, wide_r, n_theta))
     edge, turned = pl.pallas_call(
         prepare_kernel,
@@ -411,12 +406,18 @@
     )(field[:, :, wide_r - 2 * RIM :], base_coeffs.transpose(1, 2, 0))
     ring = [(i, (i + 1) % count_r) for i in range(count_r)]
     edge = lax.ppermute(edge, "row", ring)
+    edge, candidate = lax.optimization_barrier((edge, panel_set[0]))
     both = jnp.concatenate([field, turned[None]], axis=0)
     both = jnp.concatenate([edge, both], axis=2)
     both = both.reshape((n_plane + 1, wide_x * (wide_r + 2 * RIM), n_theta))
     outer = [(i, i + 1 if i % 2 else i - 1) for i in range(1, count_x - 1)]
     far = lax.ppermute(both, "gx", outer)
     mate = lax.ppermute(both, "gx", [(i, i ^ 1) for i in range(count_x)])
+
+    panel = candidate / jnp.max(jnp.abs(candidate))
+    panel = jnp.where(at_x * count_r + at_r == owner_index[0], panel, 0.0)
+    panel = jnp.concatenate([panel[:n_var], panel[n_var:]], axis=1)
+    panel = jnp.pad(panel, ((0, ROWS - n_var), (PANEL, LANES - PANEL - 2 * n_plane)))
 
     n_wide = 3
     n_tile = n_theta // ROWS

time: 66 us -> 66 us (level)
    ppermute x1, waiting for transfers between devices: 8.51 us -> 9.79 us  [body(): edge = lax.ppermute(edge, 'row', ring)]
    ppermute x1, waiting for transfers between devices: 1.55 us -> 0.37 us  [body(): far = lax.ppermute(both, 'gx', outer)]
where the time goes in v7:
time: 66 us; the launch traced here: 65.7 us
  starting transfers between devices  21.9 us (33%)
  waiting for transfers between devices  18 us (27%)
  blocking collectives  13.2 us (20%)
  Pallas kernels  9.44 us (14%)
  other arithmetic  1.43 us (2%)
  local copies, waits for them, and re-layouts  1 us (2%)
  between operations  0.77 us (1%)
    all_to_all x1, blocking collectives, body(): got = lax.all_to_all(sent, 'row', 0, 0, tiled=True)  13.2 us
    all_to_all x1, starting transfers between devices, body(): stats = lax.all_to_all(stats, 'gx', 0, 0, tiled=True)  10.5 us
    ppermute x1, waiting for transfers between devices, body(): edge = lax.ppermute(edge, 'row', ring)  9.79 us
    all_to_all x1, waiting for transfers between devices, body(): stats = lax.all_to_all(stats, 'gx', 0, 0, tiled=True)  7.83 us
    pallas_call x1, Pallas kernels, body(): pl.pallas_call(lambda *refs: march_kernel(n_var, wide_x, wide_r, count_x,...  5.74 us
    ppermute x1, starting transfers between devices, body(): edge = lax.ppermute(edge, 'row', ring)  4.83 us
    ppermute x1, starting transfers between devices, body(): far = lax.ppermute(both, 'gx', outer)  4.63 us
    ppermute x1, starting transfers between devices, body(): mate = lax.ppermute(both, 'gx', [(i, i ^ 1) for i in range(count_x)])  1.92 us
  transfers between devices with their start and end apart: 4, of which 3 were waited for; matrix products, arithmetic and copies ran while one was open for 2% of the time, Pallas kernels for 2%

profile of v7, /device:TPU:1, one launch (start us, length us, event | category | flops | bytes accessed | tf_op | source)
XLA Modules:
  0.0 65.7 jit_solution(4415251750638367839)
XLA Ops:
  0.0 0.0 copy-start.2
  0.0 0.0 copy-start
  0.0 0.0 copy-start.1
  0.0 1.0 %slice.12.tail_ref = f32[10,2,4,128]{3,2,1,0:T(4,128)S(1)} slice(f32[10,2,16,128]{3,2,1,0:T(8,128)} %bitcast.13), slice={[0:10], [0:2], [12:16], [0:128]} | slice | bytes 81920 | tf_op jit(solution)/shard_map/slice | solution.py:406
  1.0 0.0 copy-done
  1.0 4.8 %collective-permute-start = (f32[11,2,4,128]{3,2,1,0:T(4,128)S(1)}, f32[11,2,4,128]{3,2,1,0:T(4,128)S(1)}, u32[]{:S(2)}, u32[]{:S(2)}) collective-permute-start(f32[11,2,4,128]{3,2,1,0:T(4,128)S(1)} %get-tuple-element.9), channel_id=1, source_target_pairs={{0,1},{1,2},{2,3},{3,4},{4,5},{5,6},{6,7},{7,8},{8,9},{9,10},{10,1... | collective-permute-start | bytes 135176 | tf_op jit(solution)/shard_map/ppermute | solution.py:408
  5.8 0.1 pad_add_fusion.refs_0_
  6.6 0.0 copy-done.2
  6.6 9.8 %collective-permute-done = f32[11,2,4,128]{3,2,1,0:T(4,128)S(1)} collective-permute-done((f32[11,2,4,128]{3,2,1,0:T(4,128)S(1)}, f32[11,2,4,128]{3,2,1,0:T(4,128)S(1)}, u32[]{:S(2)}, u32[]{:S(2)}) %collective-permute-start) | collective-permute-done | bytes 45088 | tf_op jit(solution)/shard_map/ppermute | solution.py:408
  16.4 0.0 copy-done.1
  16.5 4.6 %collective-permute-start.2 = (f32[11,40,128]{2,1,0:T(8,128)S(1)}, f32[11,40,128]{2,1,0:T(8,128)S(1)}, u32[]{:S(2)}, u32[]{:S(2)}) collective-permute-start(f32[11,40,128]{2,1,0:T(8,128)S(1)} %reshape.10.refs_1_), channel_id=1, source_target_pairs={{16,32},{32,16},{48,64},{64,48},{80,96},{96,80},{112,128},{128,112... | collective-permute-start | bytes 675848 | tf_op jit(solution)/shard_map/ppermute | solution.py:414
  21.1 1.9 %collective-permute-start.1 = (f32[11,40,128]{2,1,0:T(8,128)S(1)}, f32[11,40,128]{2,1,0:T(8,128)S(1)}, u32[]{:S(2)}, u32[]{:S(2)}) collective-permute-start(f32[11,40,128]{2,1,0:T(8,128)S(1)} %reshape.10.refs_1_), channel_id=1, source_target_pairs={{0,16},{16,0},{32,48},{48,32},{64,80},{80,64},{96,112},{112,96},{1... | collective-permute-start | bytes 675848 | tf_op jit(solution)/shard_map/ppermute | solution.py:415
  23.0 0.6 abs_reduce_fusion
  23.6 0.6 divide_select_fusion
  24.3 0.1 select_maximum_fusion.refs_4_
  24.4 0.4 collective-permute-done.2.refs_3_
  24.7 0.0 collective-permute-done.1.refs_2_
  24.7 5.7 %march.1 = f32[16,8,384]{2,1,0:T(8,128)S(1)} custom-call(s32[2]{0:T(128)S(1)} %pad_add_fusion.refs_0_, f32[11,40,128]{2,1,0:T(8,128)S(1)} %reshape.10.refs_1_, f32[11,40,128]{2,1,0:T(8,128)S(1)} %collective-permute-done.1.refs_2_, f32[11,40,128]{2,1,0:T(8,128)S(1)} %collective-permute-done.2.refs_3_, f32[8,128]{1,0:T(8,128)S(1)} %select_maximum_fusion.refs_4_), custom_call_target="tpu_custom_call" | custom-call | tf_op jit(solution)/shard_map/march/pallas_call | solution.py:424
  30.5 13.2 %all_to_all.10.got_ref.refs_0_ = f32[16,8,384]{2,1,0:T(8,128)S(1)} all-to-all(f32[16,8,384]{2,1,0:T(8,128)S(1)} %march.1), channel_id=1, replica_groups=mesh['gx'=32,'row'=16] {'row'}, dimensions={0} | all-to-all | bytes 393216 | tf_op jit(solution)/shard_map/all_to_all | solution.py:439
  43.7 0.9 %reduce.1 = f32[32,8,128]{2,1,0:T(8,128)} custom-call(f32[16,8,384]{2,1,0:T(8,128)S(1)} %all_to_all.10.got_ref.refs_0_), custom_call_target="tpu_custom_call" | custom-call | tf_op jit(solution)/shard_map/reduce/pallas_call | solution.py:440
  44.6 10.5 %all-to-all-start.1 = ((f32[32,8,128]{2,1,0:T(8,128)}), f32[32,8,128]{2,1,0:T(8,128)S(1)}, u32[]{:S(2)}, u32[]{:S(2)}) async-start(f32[32,8,128]{2,1,0:T(8,128)} %reduce.1), calls=%async_computation.1 | async-start | bytes 262144 | tf_op jit(solution)/shard_map/all_to_all | solution.py:448
  55.1 1.2 %relay.1.refs_1_ = f32[20,8,256]{2,1,0:T(8,128)S(1)} custom-call(f32[16,8,384]{2,1,0:T(8,128)S(1)} %all_to_all.10.got_ref.refs_0_), custom_call_target="tpu_custom_call" | custom-call | tf_op jit(solution)/shard_map/relay/pallas_call | solution.py:449
  56.3 7.8 %all-to-all-done.1.refs_0_ = f32[32,8,128]{2,1,0:T(8,128)S(1)} async-done(((f32[32,8,128]{2,1,0:T(8,128)}), f32[32,8,128]{2,1,0:T(8,128)S(1)}, u32[]{:S(2)}, u32[]{:S(2)}) %all-to-all-start.1) | async-done | bytes 131104 | tf_op jit(solution)/shard_map/all_to_all | solution.py:448
  64.1 1.6 %final.1 = f32[20,8,256]{2,1,0:T(8,128)} custom-call(f32[32,8,128]{2,1,0:T(8,128)S(1)} %all-to-all-done.1.refs_0_, f32[20,8,256]{2,1,0:T(8,128)S(1)} %relay.1.refs_1_), custom_call_target="tpu_custom_call" | custom-call | tf_op jit(solution)/shard_map/final/pallas_call | solution.py:458
  (5 shorter events, 0.1 us)
Async XLA Ops:
  0.0 6.6 %copy-start.2 = (f32[1,10,10]{2,0,1:T(1,128)S(1)}, f32[1,10,10]{2,0,1:T(1,128)}, u32[]{:S(2)}) copy-start(f32[1,10,10]{2,0,1:T(1,128)} %param.6) | copy-start | bytes 1204
  0.0 1.0 %copy-start = (f32[101,2,16]{0,2,1:T(8,128)S(1)}, f32[101,2,16]{0,2,1:T(8,128)}, u32[]{:S(2)}) copy-start(f32[101,2,16]{0,2,1:T(8,128)} %param.5) | copy-start | bytes 38788
  0.0 16.4 %copy-start.1 = (f32[2,5,2,16,128]{4,3,2,1,0:T(8,128)S(1)}, f32[2,5,2,16,128]{4,3,2,1,0:T(8,128)}, u32[]{:S(2)}) copy-start(f32[2,5,2,16,128]{4,3,2,1,0:T(8,128)} %param.4) | copy-start | bytes 491524
  1.0 15.4 %collective-permute-start = (f32[11,2,4,128]{3,2,1,0:T(4,128)S(1)}, f32[11,2,4,128]{3,2,1,0:T(4,128)S(1)}, u32[]{:S(2)}, u32[]{:S(2)}) collective-permute-start(f32[11,2,4,128]{3,2,1,0:T(4,128)S(1)} %get-tuple-element.9), channel_id=1, source_target_pairs={{0,1},{1,2},{2,3},{3,4},{4,5},{5,6},{6,7},{7,8},{8,9},{9,10},{10,1... | collective-permute-start | bytes 135176 | tf_op jit(solution)/shard_map/ppermute | solution.py:408
  16.5 8.3 %collective-permute-start.2 = (f32[11,40,128]{2,1,0:T(8,128)S(1)}, f32[11,40,128]{2,1,0:T(8,128)S(1)}, u32[]{:S(2)}, u32[]{:S(2)}) collective-permute-start(f32[11,40,128]{2,1,0:T(8,128)S(1)} %reshape.10.refs_1_), channel_id=1, source_target_pairs={{16,32},{32,16},{48,64},{64,48},{80,96},{96,80},{112,128},{128,112... | collective-permute-start | bytes 675848 | tf_op jit(solution)/shard_map/ppermute | solution.py:414
  21.1 3.6 %collective-permute-start.1 = (f32[11,40,128]{2,1,0:T(8,128)S(1)}, f32[11,40,128]{2,1,0:T(8,128)S(1)}, u32[]{:S(2)}, u32[]{:S(2)}) collective-permute-start(f32[11,40,128]{2,1,0:T(8,128)S(1)} %reshape.10.refs_1_), channel_id=1, source_target_pairs={{0,16},{16,0},{32,48},{48,32},{64,80},{80,64},{96,112},{112,96},{1... | collective-permute-start | bytes 675848 | tf_op jit(solution)/shard_map/ppermute | solution.py:415
  44.6 19.6 %all-to-all-start.1 = ((f32[32,8,128]{2,1,0:T(8,128)}), f32[32,8,128]{2,1,0:T(8,128)S(1)}, u32[]{:S(2)}, u32[]{:S(2)}) async-start(f32[32,8,128]{2,1,0:T(8,128)} %reduce.1), calls=%async_computation.1 | async-start | bytes 262144 | tf_op jit(solution)/shard_map/all_to_all | solution.py:448

commit v8 on v7

--- a/solution.py
+++ b/solution.py
@@ -8,7 +8,7 @@
 from jax.sharding import PartitionSpec as P
 
 STEPS = 2
-UNROLL = 2
+UNROLL = 4
 RIM = 2
 LANES = 128
 ROWS = 8
@@ -180,16 +180,9 @@
                 result[k + i] = local
         return result
 
-    def first_step(tile, carry):
-        result = advance(now_ref, tile)
+    def keep(tile, result):
         for b in range(n_plane):
             next_ref[b, pl.ds(ROWS + tile * ROWS, ROWS), :] = jnp.where(inside, result[b], 0.0)
-        return carry
-
-    lax.fori_loop(0, n_tile, first_step, 0, unroll=UNROLL)
-    for b in range(n_plane):
-        next_ref[b, ROWS - 1 : ROWS, :] = next_ref[b, ROWS + n_theta - 1 : ROWS + n_theta, :]
-        next_ref[b, ROWS + n_theta : ROWS + n_theta + 1, :] = next_ref[b, ROWS : ROWS + 1, :]
 
     group = wide_x * wide_r
     per_vreg = LANES // group
@@ -199,8 +192,7 @@
         start = (x + RIM) * deep + RIM
         mine.append((lane >= start) & (lane < start + wide_r))
 
-    def second_step(tile, largest):
-        result = advance(next_ref, tile)
+    def pack(tile, result, largest):
         for v in range(n_wide):
             pieces = []
             for b in range(v * per_vreg, min((v + 1) * per_vreg, n_plane)):
@@ -212,7 +204,22 @@
             largest = jnp.maximum(largest, jnp.abs(packed))
         return largest
 
-    largest = lax.fori_loop(0, n_tile, second_step, jnp.zeros((ROWS, LANES), jnp.float32), unroll=UNROLL)
+    for tile in (n_tile - 2, n_tile - 1, 0, 1):
+        keep(tile, advance(now_ref, tile))
+    for b in range(n_plane):
+        next_ref[b, ROWS - 1 : ROWS, :] = next_ref[b, ROWS + n_theta - 1 : ROWS + n_theta, :]
+        next_ref[b, ROWS + n_theta : ROWS + n_theta + 1, :] = next_ref[b, ROWS : ROWS + 1, :]
+
+    def both_steps(tile, largest):
+        ahead = advance(now_ref, tile + 2)
+        largest = pack(tile, advance(next_ref, tile), largest)
+        keep(tile + 2, ahead)
+        return largest
+
+    largest = jnp.zeros((ROWS, LANES), jnp.float32)
+    largest = lax.fori_loop(0, n_tile - 4, both_steps, largest, unroll=UNROLL)
+    for tile in range(n_tile - 4, n_tile):
+        largest = pack(tile, advance(next_ref, tile), largest)
     largest = jnp.max(largest, axis=1, keepdims=True)
     largest = jnp.max(largest, axis=0, keepdims=True)
     inverse = safe_inverse(jnp.broadcast_to(largest, (ROWS, LANES)))

time: 66 us -> 65.5 us (level)
  no operation moved by 1% of the time
where the time goes in v8:
time: 65.5 us; the launch traced here: 65.2 us
  starting transfers between devices  21.9 us (33%)
  waiting for transfers between devices  18 us (27%)
  blocking collectives  13.2 us (20%)
  Pallas kernels  8.96 us (14%)
  other arithmetic  1.43 us (2%)
  local copies, waits for them, and re-layouts  1 us (2%)
  between operations  0.77 us (1%)
    all_to_all x1, blocking collectives, body(): got = lax.all_to_all(sent, 'row', 0, 0, tiled=True)  13.2 us
    all_to_all x1, starting transfers between devices, body(): stats = lax.all_to_all(stats, 'gx', 0, 0, tiled=True)  10.5 us
    ppermute x1, waiting for transfers between devices, body(): edge = lax.ppermute(edge, 'row', ring)  9.79 us
    all_to_all x1, waiting for transfers between devices, body(): stats = lax.all_to_all(stats, 'gx', 0, 0, tiled=True)  7.83 us
    pallas_call x1, Pallas kernels, body(): pl.pallas_call(lambda *refs: march_kernel(n_var, wide_x, wide_r, count_x,...  5.26 us
    ppermute x1, starting transfers between devices, body(): edge = lax.ppermute(edge, 'row', ring)  4.83 us
    ppermute x1, starting transfers between devices, body(): far = lax.ppermute(both, 'gx', outer)  4.63 us
    ppermute x1, starting transfers between devices, body(): mate = lax.ppermute(both, 'gx', [(i, i ^ 1) for i in range(count_x)])  1.92 us
  transfers between devices with their start and end apart: 4, of which 3 were waited for; matrix products, arithmetic and copies ran while one was open for 2% of the time, Pallas kernels for 2%

profile of v8, /device:TPU:1, one launch (start us, length us, event | category | flops | bytes accessed | tf_op | source)
XLA Modules:
  0.0 65.2 jit_solution(8863242555871976145)
XLA Ops:
  0.0 0.0 copy-start.2
  0.0 0.0 copy-start
  0.0 0.0 copy-start.1
  0.0 1.0 %slice.12.tail_ref = f32[10,2,4,128]{3,2,1,0:T(4,128)S(1)} slice(f32[10,2,16,128]{3,2,1,0:T(8,128)} %bitcast.13), slice={[0:10], [0:2], [12:16], [0:128]} | slice | bytes 81920 | tf_op jit(solution)/shard_map/slice | solution.py:413
  1.0 0.0 copy-done
  1.0 4.8 %collective-permute-start = (f32[11,2,4,128]{3,2,1,0:T(4,128)S(1)}, f32[11,2,4,128]{3,2,1,0:T(4,128)S(1)}, u32[]{:S(2)}, u32[]{:S(2)}) collective-permute-start(f32[11,2,4,128]{3,2,1,0:T(4,128)S(1)} %get-tuple-element.9), channel_id=1, source_target_pairs={{0,1},{1,2},{2,3},{3,4},{4,5},{5,6},{6,7},{7,8},{8,9},{9,10},{10,1... | collective-permute-start | bytes 135176 | tf_op jit(solution)/shard_map/ppermute | solution.py:415
  5.8 0.1 pad_add_fusion.refs_0_
  6.6 0.0 copy-done.2
  6.6 9.8 %collective-permute-done = f32[11,2,4,128]{3,2,1,0:T(4,128)S(1)} collective-permute-done((f32[11,2,4,128]{3,2,1,0:T(4,128)S(1)}, f32[11,2,4,128]{3,2,1,0:T(4,128)S(1)}, u32[]{:S(2)}, u32[]{:S(2)}) %collective-permute-start) | collective-permute-done | bytes 45088 | tf_op jit(solution)/shard_map/ppermute | solution.py:415
  16.4 0.0 copy-done.1
  16.5 4.6 %collective-permute-start.2 = (f32[11,40,128]{2,1,0:T(8,128)S(1)}, f32[11,40,128]{2,1,0:T(8,128)S(1)}, u32[]{:S(2)}, u32[]{:S(2)}) collective-permute-start(f32[11,40,128]{2,1,0:T(8,128)S(1)} %reshape.10.refs_1_), channel_id=1, source_target_pairs={{16,32},{32,16},{48,64},{64,48},{80,96},{96,80},{112,128},{128,112... | collective-permute-start | bytes 675848 | tf_op jit(solution)/shard_map/ppermute | solution.py:421
  21.1 1.9 %collective-permute-start.1 = (f32[11,40,128]{2,1,0:T(8,128)S(1)}, f32[11,40,128]{2,1,0:T(8,128)S(1)}, u32[]{:S(2)}, u32[]{:S(2)}) collective-permute-start(f32[11,40,128]{2,1,0:T(8,128)S(1)} %reshape.10.refs_1_), channel_id=1, source_target_pairs={{0,16},{16,0},{32,48},{48,32},{64,80},{80,64},{96,112},{112,96},{1... | collective-permute-start | bytes 675848 | tf_op jit(solution)/shard_map/ppermute | solution.py:422
  23.0 0.6 abs_reduce_fusion
  23.6 0.6 divide_select_fusion
  24.3 0.1 select_maximum_fusion.refs_4_
  24.4 0.4 collective-permute-done.2.refs_3_
  24.7 0.0 collective-permute-done.1.refs_2_
  24.7 5.3 %march.1 = f32[16,8,384]{2,1,0:T(8,128)S(1)} custom-call(s32[2]{0:T(128)S(1)} %pad_add_fusion.refs_0_, f32[11,40,128]{2,1,0:T(8,128)S(1)} %reshape.10.refs_1_, f32[11,40,128]{2,1,0:T(8,128)S(1)} %collective-permute-done.1.refs_2_, f32[11,40,128]{2,1,0:T(8,128)S(1)} %collective-permute-done.2.refs_3_, f32[8,128]{1,0:T(8,128)S(1)} %select_maximum_fusion.refs_4_), custom_call_target="tpu_custom_call" | custom-call | tf_op jit(solution)/shard_map/march/pallas_call | solution.py:431
  30.0 13.2 %all_to_all.10.got_ref.refs_0_ = f32[16,8,384]{2,1,0:T(8,128)S(1)} all-to-all(f32[16,8,384]{2,1,0:T(8,128)S(1)} %march.1), channel_id=1, replica_groups=mesh['gx'=32,'row'=16] {'row'}, dimensions={0} | all-to-all | bytes 393216 | tf_op jit(solution)/shard_map/all_to_all | solution.py:446
  43.2 0.9 %reduce.1 = f32[32,8,128]{2,1,0:T(8,128)} custom-call(f32[16,8,384]{2,1,0:T(8,128)S(1)} %all_to_all.10.got_ref.refs_0_), custom_call_target="tpu_custom_call" | custom-call | tf_op jit(solution)/shard_map/reduce/pallas_call | solution.py:447
  44.1 10.5 %all-to-all-start.1 = ((f32[32,8,128]{2,1,0:T(8,128)}), f32[32,8,128]{2,1,0:T(8,128)S(1)}, u32[]{:S(2)}, u32[]{:S(2)}) async-start(f32[32,8,128]{2,1,0:T(8,128)} %reduce.1), calls=%async_computation.1 | async-start | bytes 262144 | tf_op jit(solution)/shard_map/all_to_all | solution.py:455
  54.6 1.2 %relay.1.refs_1_ = f32[20,8,256]{2,1,0:T(8,128)S(1)} custom-call(f32[16,8,384]{2,1,0:T(8,128)S(1)} %all_to_all.10.got_ref.refs_0_), custom_call_target="tpu_custom_call" | custom-call | tf_op jit(solution)/shard_map/relay/pallas_call | solution.py:456
  55.8 7.8 %all-to-all-done.1.refs_0_ = f32[32,8,128]{2,1,0:T(8,128)S(1)} async-done(((f32[32,8,128]{2,1,0:T(8,128)}), f32[32,8,128]{2,1,0:T(8,128)S(1)}, u32[]{:S(2)}, u32[]{:S(2)}) %all-to-all-start.1) | async-done | bytes 131104 | tf_op jit(solution)/shard_map/all_to_all | solution.py:455
  63.7 1.6 %final.1 = f32[20,8,256]{2,1,0:T(8,128)} custom-call(f32[32,8,128]{2,1,0:T(8,128)S(1)} %all-to-all-done.1.refs_0_, f32[20,8,256]{2,1,0:T(8,128)S(1)} %relay.1.refs_1_), custom_call_target="tpu_custom_call" | custom-call | tf_op jit(solution)/shard_map/final/pallas_call | solution.py:465
  (5 shorter events, 0.1 us)
Async XLA Ops:
  0.0 6.6 %copy-start.2 = (f32[1,10,10]{2,0,1:T(1,128)S(1)}, f32[1,10,10]{2,0,1:T(1,128)}, u32[]{:S(2)}) copy-start(f32[1,10,10]{2,0,1:T(1,128)} %param.6) | copy-start | bytes 1204
  0.0 1.0 %copy-start = (f32[101,2,16]{0,2,1:T(8,128)S(1)}, f32[101,2,16]{0,2,1:T(8,128)}, u32[]{:S(2)}) copy-start(f32[101,2,16]{0,2,1:T(8,128)} %param.5) | copy-start | bytes 38788
  0.0 16.4 %copy-start.1 = (f32[2,5,2,16,128]{4,3,2,1,0:T(8,128)S(1)}, f32[2,5,2,16,128]{4,3,2,1,0:T(8,128)}, u32[]{:S(2)}) copy-start(f32[2,5,2,16,128]{4,3,2,1,0:T(8,128)} %param.4) | copy-start | bytes 491524
  1.0 15.4 %collective-permute-start = (f32[11,2,4,128]{3,2,1,0:T(4,128)S(1)}, f32[11,2,4,128]{3,2,1,0:T(4,128)S(1)}, u32[]{:S(2)}, u32[]{:S(2)}) collective-permute-start(f32[11,2,4,128]{3,2,1,0:T(4,128)S(1)} %get-tuple-element.9), channel_id=1, source_target_pairs={{0,1},{1,2},{2,3},{3,4},{4,5},{5,6},{6,7},{7,8},{8,9},{9,10},{10,1... | collective-permute-start | bytes 135176 | tf_op jit(solution)/shard_map/ppermute | solution.py:415
  16.5 8.3 %collective-permute-start.2 = (f32[11,40,128]{2,1,0:T(8,128)S(1)}, f32[11,40,128]{2,1,0:T(8,128)S(1)}, u32[]{:S(2)}, u32[]{:S(2)}) collective-permute-start(f32[11,40,128]{2,1,0:T(8,128)S(1)} %reshape.10.refs_1_), channel_id=1, source_target_pairs={{16,32},{32,16},{48,64},{64,48},{80,96},{96,80},{112,128},{128,112... | collective-permute-start | bytes 675848 | tf_op jit(solution)/shard_map/ppermute | solution.py:421
  21.1 3.6 %collective-permute-start.1 = (f32[11,40,128]{2,1,0:T(8,128)S(1)}, f32[11,40,128]{2,1,0:T(8,128)S(1)}, u32[]{:S(2)}, u32[]{:S(2)}) collective-permute-start(f32[11,40,128]{2,1,0:T(8,128)S(1)} %reshape.10.refs_1_), channel_id=1, source_target_pairs={{0,16},{16,0},{32,48},{48,32},{64,80},{80,64},{96,112},{112,96},{1... | collective-permute-start | bytes 675848 | tf_op jit(solution)/shard_map/ppermute | solution.py:422
  44.1 19.6 %all-to-all-start.1 = ((f32[32,8,128]{2,1,0:T(8,128)}), f32[32,8,128]{2,1,0:T(8,128)S(1)}, u32[]{:S(2)}, u32[]{:S(2)}) async-start(f32[32,8,128]{2,1,0:T(8,128)} %reduce.1), calls=%async_computation.1 | async-start | bytes 262144 | tf_op jit(solution)/shard_map/all_to_all | solution.py:455

commit v9 on v8

--- a/solution.py
+++ b/solution.py
@@ -8,7 +8,7 @@
 from jax.sharding import PartitionSpec as P
 
 STEPS = 2
-UNROLL = 4
+UNROLL = 12
 RIM = 2
 LANES = 128
 ROWS = 8

time: 65.5 us -> 65.4 us (level)
  no operation moved by 1% of the time
where the time goes in v9:
time: 65.4 us; the launch traced here: 65.1 us
  starting transfers between devices  21.9 us (33%)
  waiting for transfers between devices  18 us (28%)
  blocking collectives  13.2 us (20%)
  Pallas kernels  8.82 us (13%)
  other arithmetic  1.43 us (2%)
  local copies, waits for them, and re-layouts  1 us (2%)
  between operations  0.77 us (1%)
    all_to_all x1, blocking collectives, body(): got = lax.all_to_all(sent, 'row', 0, 0, tiled=True)  13.2 us
    all_to_all x1, starting transfers between devices, body(): stats = lax.all_to_all(stats, 'gx', 0, 0, tiled=True)  10.5 us
    ppermute x1, waiting for transfers between devices, body(): edge = lax.ppermute(edge, 'row', ring)  9.79 us
    all_to_all x1, waiting for transfers between devices, body(): stats = lax.all_to_all(stats, 'gx', 0, 0, tiled=True)  7.83 us
    pallas_call x1, Pallas kernels, body(): pl.pallas_call(lambda *refs: march_kernel(n_var, wide_x, wide_r, count_x,...  5.11 us
    ppermute x1, starting transfers between devices, body(): edge = lax.ppermute(edge, 'row', ring)  4.83 us
    ppermute x1, starting transfers between devices, body(): far = lax.ppermute(both, 'gx', outer)  4.63 us
    ppermute x1, starting transfers between devices, body(): mate = lax.ppermute(both, 'gx', [(i, i ^ 1) for i in range(count_x)])  1.92 us
  transfers between devices with their start and end apart: 4, of which 3 were waited for; matrix products, arithmetic and copies ran while one was open for 2% of the time, Pallas kernels for 2%

profile of v9, /device:TPU:1, one launch (start us, length us, event | category | flops | bytes accessed | tf_op | source)
XLA Modules:
  0.0 65.1 jit_solution(437777506967865040)
XLA Ops:
  0.0 0.0 copy-start.2
  0.0 0.0 copy-start
  0.0 0.0 copy-start.1
  0.0 1.0 %slice.12.tail_ref = f32[10,2,4,128]{3,2,1,0:T(4,128)S(1)} slice(f32[10,2,16,128]{3,2,1,0:T(8,128)} %bitcast.13), slice={[0:10], [0:2], [12:16], [0:128]} | slice | bytes 81920 | tf_op jit(solution)/shard_map/slice | solution.py:413
  1.0 0.0 copy-done
  1.0 4.8 %collective-permute-start = (f32[11,2,4,128]{3,2,1,0:T(4,128)S(1)}, f32[11,2,4,128]{3,2,1,0:T(4,128)S(1)}, u32[]{:S(2)}, u32[]{:S(2)}) collective-permute-start(f32[11,2,4,128]{3,2,1,0:T(4,128)S(1)} %get-tuple-element.9), channel_id=1, source_target_pairs={{0,1},{1,2},{2,3},{3,4},{4,5},{5,6},{6,7},{7,8},{8,9},{9,10},{10,1... | collective-permute-start | bytes 135176 | tf_op jit(solution)/shard_map/ppermute | solution.py:415
  5.8 0.1 pad_add_fusion.refs_0_
  6.6 0.0 copy-done.2
  6.6 9.8 %collective-permute-done = f32[11,2,4,128]{3,2,1,0:T(4,128)S(1)} collective-permute-done((f32[11,2,4,128]{3,2,1,0:T(4,128)S(1)}, f32[11,2,4,128]{3,2,1,0:T(4,128)S(1)}, u32[]{:S(2)}, u32[]{:S(2)}) %collective-permute-start) | collective-permute-done | bytes 45088 | tf_op jit(solution)/shard_map/ppermute | solution.py:415
  16.4 0.0 copy-done.1
  16.5 4.6 %collective-permute-start.2 = (f32[11,40,128]{2,1,0:T(8,128)S(1)}, f32[11,40,128]{2,1,0:T(8,128)S(1)}, u32[]{:S(2)}, u32[]{:S(2)}) collective-permute-start(f32[11,40,128]{2,1,0:T(8,128)S(1)} %reshape.10.refs_1_), channel_id=1, source_target_pairs={{16,32},{32,16},{48,64},{64,48},{80,96},{96,80},{112,128},{128,112... | collective-permute-start | bytes 675848 | tf_op jit(solution)/shard_map/ppermute | solution.py:421
  21.1 1.9 %collective-permute-start.1 = (f32[11,40,128]{2,1,0:T(8,128)S(1)}, f32[11,40,128]{2,1,0:T(8,128)S(1)}, u32[]{:S(2)}, u32[]{:S(2)}) collective-permute-start(f32[11,40,128]{2,1,0:T(8,128)S(1)} %reshape.10.refs_1_), channel_id=1, source_target_pairs={{0,16},{16,0},{32,48},{48,32},{64,80},{80,64},{96,112},{112,96},{1... | collective-permute-start | bytes 675848 | tf_op jit(solution)/shard_map/ppermute | solution.py:422
  23.0 0.6 abs_reduce_fusion
  23.6 0.6 divide_select_fusion
  24.3 0.1 select_maximum_fusion.refs_4_
  24.4 0.4 collective-permute-done.2.refs_3_
  24.7 0.0 collective-permute-done.1.refs_2_
  24.7 5.1 %march.1 = f32[16,8,384]{2,1,0:T(8,128)S(1)} custom-call(s32[2]{0:T(128)S(1)} %pad_add_fusion.refs_0_, f32[11,40,128]{2,1,0:T(8,128)S(1)} %reshape.10.refs_1_, f32[11,40,128]{2,1,0:T(8,128)S(1)} %collective-permute-done.1.refs_2_, f32[11,40,128]{2,1,0:T(8,128)S(1)} %collective-permute-done.2.refs_3_, f32[8,128]{1,0:T(8,128)S(1)} %select_maximum_fusion.refs_4_), custom_call_target="tpu_custom_call" | custom-call | tf_op jit(solution)/shard_map/march/pallas_call | solution.py:431
  29.9 13.2 %all_to_all.10.got_ref.refs_0_ = f32[16,8,384]{2,1,0:T(8,128)S(1)} all-to-all(f32[16,8,384]{2,1,0:T(8,128)S(1)} %march.1), channel_id=1, replica_groups=mesh['gx'=32,'row'=16] {'row'}, dimensions={0} | all-to-all | bytes 393216 | tf_op jit(solution)/shard_map/all_to_all | solution.py:446
  43.0 0.9 %reduce.1 = f32[32,8,128]{2,1,0:T(8,128)} custom-call(f32[16,8,384]{2,1,0:T(8,128)S(1)} %all_to_all.10.got_ref.refs_0_), custom_call_target="tpu_custom_call" | custom-call | tf_op jit(solution)/shard_map/reduce/pallas_call | solution.py:447
  43.9 10.5 %all-to-all-start.1 = ((f32[32,8,128]{2,1,0:T(8,128)}), f32[32,8,128]{2,1,0:T(8,128)S(1)}, u32[]{:S(2)}, u32[]{:S(2)}) async-start(f32[32,8,128]{2,1,0:T(8,128)} %reduce.1), calls=%async_computation.1 | async-start | bytes 262144 | tf_op jit(solution)/shard_map/all_to_all | solution.py:455
  54.4 1.2 %relay.1.refs_1_ = f32[20,8,256]{2,1,0:T(8,128)S(1)} custom-call(f32[16,8,384]{2,1,0:T(8,128)S(1)} %all_to_all.10.got_ref.refs_0_), custom_call_target="tpu_custom_call" | custom-call | tf_op jit(solution)/shard_map/relay/pallas_call | solution.py:456
  55.7 7.8 %all-to-all-done.1.refs_0_ = f32[32,8,128]{2,1,0:T(8,128)S(1)} async-done(((f32[32,8,128]{2,1,0:T(8,128)}), f32[32,8,128]{2,1,0:T(8,128)S(1)}, u32[]{:S(2)}, u32[]{:S(2)}) %all-to-all-start.1) | async-done | bytes 131104 | tf_op jit(solution)/shard_map/all_to_all | solution.py:455
  63.5 1.6 %final.1 = f32[20,8,256]{2,1,0:T(8,128)} custom-call(f32[32,8,128]{2,1,0:T(8,128)S(1)} %all-to-all-done.1.refs_0_, f32[20,8,256]{2,1,0:T(8,128)S(1)} %relay.1.refs_1_), custom_call_target="tpu_custom_call" | custom-call | tf_op jit(solution)/shard_map/final/pallas_call | solution.py:465
  (5 shorter events, 0.1 us)
Async XLA Ops:
  0.0 6.6 %copy-start.2 = (f32[1,10,10]{2,0,1:T(1,128)S(1)}, f32[1,10,10]{2,0,1:T(1,128)}, u32[]{:S(2)}) copy-start(f32[1,10,10]{2,0,1:T(1,128)} %param.6) | copy-start | bytes 1204
  0.0 1.0 %copy-start = (f32[101,2,16]{0,2,1:T(8,128)S(1)}, f32[101,2,16]{0,2,1:T(8,128)}, u32[]{:S(2)}) copy-start(f32[101,2,16]{0,2,1:T(8,128)} %param.5) | copy-start | bytes 38788
  0.0 16.4 %copy-start.1 = (f32[2,5,2,16,128]{4,3,2,1,0:T(8,128)S(1)}, f32[2,5,2,16,128]{4,3,2,1,0:T(8,128)}, u32[]{:S(2)}) copy-start(f32[2,5,2,16,128]{4,3,2,1,0:T(8,128)} %param.4) | copy-start | bytes 491524
  1.0 15.4 %collective-permute-start = (f32[11,2,4,128]{3,2,1,0:T(4,128)S(1)}, f32[11,2,4,128]{3,2,1,0:T(4,128)S(1)}, u32[]{:S(2)}, u32[]{:S(2)}) collective-permute-start(f32[11,2,4,128]{3,2,1,0:T(4,128)S(1)} %get-tuple-element.9), channel_id=1, source_target_pairs={{0,1},{1,2},{2,3},{3,4},{4,5},{5,6},{6,7},{7,8},{8,9},{9,10},{10,1... | collective-permute-start | bytes 135176 | tf_op jit(solution)/shard_map/ppermute | solution.py:415
  16.5 8.3 %collective-permute-start.2 = (f32[11,40,128]{2,1,0:T(8,128)S(1)}, f32[11,40,128]{2,1,0:T(8,128)S(1)}, u32[]{:S(2)}, u32[]{:S(2)}) collective-permute-start(f32[11,40,128]{2,1,0:T(8,128)S(1)} %reshape.10.refs_1_), channel_id=1, source_target_pairs={{16,32},{32,16},{48,64},{64,48},{80,96},{96,80},{112,128},{128,112... | collective-permute-start | bytes 675848 | tf_op jit(solution)/shard_map/ppermute | solution.py:421
  21.1 3.6 %collective-permute-start.1 = (f32[11,40,128]{2,1,0:T(8,128)S(1)}, f32[11,40,128]{2,1,0:T(8,128)S(1)}, u32[]{:S(2)}, u32[]{:S(2)}) collective-permute-start(f32[11,40,128]{2,1,0:T(8,128)S(1)} %reshape.10.refs_1_), channel_id=1, source_target_pairs={{0,16},{16,0},{32,48},{48,32},{64,80},{80,64},{96,112},{112,96},{1... | collective-permute-start | bytes 675848 | tf_op jit(solution)/shard_map/ppermute | solution.py:422
  43.9 19.6 %all-to-all-start.1 = ((f32[32,8,128]{2,1,0:T(8,128)}), f32[32,8,128]{2,1,0:T(8,128)S(1)}, u32[]{:S(2)}, u32[]{:S(2)}) async-start(f32[32,8,128]{2,1,0:T(8,128)} %reduce.1), calls=%async_computation.1 | async-start | bytes 262144 | tf_op jit(solution)/shard_map/all_to_all | solution.py:455

commit v10 on v9

--- a/solution.py
+++ b/solution.py
@@ -303,8 +303,10 @@
     count, _, wide = got_ref.shape
     pair, size, panel = merge([got_ref[n, :, wide - LANES :] for n in range(count)])
     tile = pack_stats(pair, size, panel)
+    half = ROWS // 2
+    folded = jnp.where(lanes_of(tile.shape) < HIGH, roll_lanes(tile, HIGH), pltpu.roll(tile, half, 0))
     for n in range(out_ref.shape[0]):
-        out_ref[n] = tile
+        out_ref[n] = folded[:half]
 
 
 def relay_kernel(n_plane, wide_x, wide_r, got_ref, out_ref):
@@ -327,7 +329,11 @@
 
 def final_kernel(n_var, wide_x, scale, got_ref, cells_ref, out_ref, weight_ref):
     n_plane = 2 * n_var
-    tiles = [got_ref[n] for n in range(got_ref.shape[0])]
+    upper = lax.broadcasted_iota(jnp.int32, (ROWS, LANES), 0) < ROWS // 2
+    tiles = []
+    for n in range(got_ref.shape[0]):
+        twice = jnp.concatenate([got_ref[n], got_ref[n]], axis=0)
+        tiles.append(jnp.where(upper, roll_lanes(twice, HIGH), twice))
     pair, size, tile = merge(tiles)
     lane = lanes_of((ROWS, LANES))
     row = lax.broadcasted_iota(jnp.int32, (ROWS, LANES), 0)
@@ -446,7 +452,7 @@
     got = lax.all_to_all(sent, "row", 0, 0, tiled=True)
     stats = pl.pallas_call(
         reduce_kernel,
-        out_shape=jax.ShapeDtypeStruct((count_x, ROWS, LANES), jnp.float32),
+        out_shape=jax.ShapeDtypeStruct((count_x, ROWS // 2, LANES), jnp.float32),
         in_specs=[VMEM],
         out_specs=VMEM,
         compiler_params=PARAMS,

time: 65.4 us -> 64.5 us (0.986)
  waiting for transfers between devices: 18 us -> 17 us
    all_to_all x1, waiting for transfers between devices: 7.83 us -> 6.84 us  [body(): stats = lax.all_to_all(stats, 'gx', 0, 0, tiled=True)]
where the time goes in v10:
time: 64.5 us; the launch traced here: 64.2 us
  starting transfers between devices  21.9 us (34%)
  waiting for transfers between devices  17 us (26%)
  blocking collectives  13.2 us (20%)
  Pallas kernels  8.94 us (14%)
  other arithmetic  1.43 us (2%)
  local copies, waits for them, and re-layouts  1 us (2%)
  between operations  0.77 us (1%)
    all_to_all x1, blocking collectives, body(): got = lax.all_to_all(sent, 'row', 0, 0, tiled=True)  13.2 us
    all_to_all x1, starting transfers between devices, body(): stats = lax.all_to_all(stats, 'gx', 0, 0, tiled=True)  10.5 us
    ppermute x1, waiting for transfers between devices, body(): edge = lax.ppermute(edge, 'row', ring)  9.79 us
    all_to_all x1, waiting for transfers between devices, body(): stats = lax.all_to_all(stats, 'gx', 0, 0, tiled=True)  6.84 us
    pallas_call x1, Pallas kernels, body(): pl.pallas_call(lambda *refs: march_kernel(n_var, wide_x, wide_r, count_x,...  5.11 us
    ppermute x1, starting transfers between devices, body(): edge = lax.ppermute(edge, 'row', ring)  4.83 us
    ppermute x1, starting transfers between devices, body(): far = lax.ppermute(both, 'gx', outer)  4.63 us
    ppermute x1, starting transfers between devices, body(): mate = lax.ppermute(both, 'gx', [(i, i ^ 1) for i in range(count_x)])  1.92 us
  transfers between devices with their start and end apart: 4, of which 3 were waited for; matrix products, arithmetic and copies ran while one was open for 2% of the time, Pallas kernels for 2%

profile of v10, /device:TPU:1, one launch (start us, length us, event | category | flops | bytes accessed | tf_op | source)
XLA Modules:
  0.0 64.2 jit_solution(1819897655212004776)
XLA Ops:
  0.0 0.0 copy-start.2
  0.0 0.0 copy-start
  0.0 0.0 copy-start.1
  0.0 1.0 %slice.12.tail_ref = f32[10,2,4,128]{3,2,1,0:T(4,128)S(1)} slice(f32[10,2,16,128]{3,2,1,0:T(8,128)} %bitcast.13), slice={[0:10], [0:2], [12:16], [0:128]} | slice | bytes 81920 | tf_op jit(solution)/shard_map/slice | solution.py:419
  1.0 0.0 copy-done
  1.0 4.8 %collective-permute-start = (f32[11,2,4,128]{3,2,1,0:T(4,128)S(1)}, f32[11,2,4,128]{3,2,1,0:T(4,128)S(1)}, u32[]{:S(2)}, u32[]{:S(2)}) collective-permute-start(f32[11,2,4,128]{3,2,1,0:T(4,128)S(1)} %get-tuple-element.9), channel_id=1, source_target_pairs={{0,1},{1,2},{2,3},{3,4},{4,5},{5,6},{6,7},{7,8},{8,9},{9,10},{10,1... | collective-permute-start | bytes 135176 | tf_op jit(solution)/shard_map/ppermute | solution.py:421
  5.8 0.1 pad_add_fusion.refs_0_
  6.6 0.0 copy-done.2
  6.6 9.8 %collective-permute-done = f32[11,2,4,128]{3,2,1,0:T(4,128)S(1)} collective-permute-done((f32[11,2,4,128]{3,2,1,0:T(4,128)S(1)}, f32[11,2,4,128]{3,2,1,0:T(4,128)S(1)}, u32[]{:S(2)}, u32[]{:S(2)}) %collective-permute-start) | collective-permute-done | bytes 45088 | tf_op jit(solution)/shard_map/ppermute | solution.py:421
  16.4 0.0 copy-done.1
  16.5 4.6 %collective-permute-start.2 = (f32[11,40,128]{2,1,0:T(8,128)S(1)}, f32[11,40,128]{2,1,0:T(8,128)S(1)}, u32[]{:S(2)}, u32[]{:S(2)}) collective-permute-start(f32[11,40,128]{2,1,0:T(8,128)S(1)} %reshape.10.refs_1_), channel_id=1, source_target_pairs={{16,32},{32,16},{48,64},{64,48},{80,96},{96,80},{112,128},{128,112... | collective-permute-start | bytes 675848 | tf_op jit(solution)/shard_map/ppermute | solution.py:427
  21.1 1.9 %collective-permute-start.1 = (f32[11,40,128]{2,1,0:T(8,128)S(1)}, f32[11,40,128]{2,1,0:T(8,128)S(1)}, u32[]{:S(2)}, u32[]{:S(2)}) collective-permute-start(f32[11,40,128]{2,1,0:T(8,128)S(1)} %reshape.10.refs_1_), channel_id=1, source_target_pairs={{0,16},{16,0},{32,48},{48,32},{64,80},{80,64},{96,112},{112,96},{1... | collective-permute-start | bytes 675848 | tf_op jit(solution)/shard_map/ppermute | solution.py:428
  23.0 0.6 abs_reduce_fusion
  23.6 0.6 %divide_select_fusion = f32[10,10]{1,0:T(8,128)S(1)} fusion(f32[10,10]{1,0:T(8,128)S(1)} %bitcast.16, f32[]{:T(128)} %abs_reduce_fusion, pred[]{:T(512)S(6)} %eq.3), kind=kLoop, calls=%fused_computation.2 | loop fusion | flops 200 | bytes 805 | tf_op jit(solution)/shard_map/jit(_where)/select_n | solution.py:431
  24.3 0.1 select_maximum_fusion.refs_4_
  24.4 0.4 collective-permute-done.2.refs_3_
  24.7 0.0 collective-permute-done.1.refs_2_
  24.7 5.1 %march.1 = f32[16,8,384]{2,1,0:T(8,128)S(1)} custom-call(s32[2]{0:T(128)S(1)} %pad_add_fusion.refs_0_, f32[11,40,128]{2,1,0:T(8,128)S(1)} %reshape.10.refs_1_, f32[11,40,128]{2,1,0:T(8,128)S(1)} %collective-permute-done.1.refs_2_, f32[11,40,128]{2,1,0:T(8,128)S(1)} %collective-permute-done.2.refs_3_, f32[8,128]{1,0:T(8,128)S(1)} %select_maximum_fusion.refs_4_), custom_call_target="tpu_custom_call" | custom-call | tf_op jit(solution)/shard_map/march/pallas_call | solution.py:437
  29.9 13.2 %all_to_all.10.got_ref.refs_0_ = f32[16,8,384]{2,1,0:T(8,128)S(1)} all-to-all(f32[16,8,384]{2,1,0:T(8,128)S(1)} %march.1), channel_id=1, replica_groups=mesh['gx'=32,'row'=16] {'row'}, dimensions={0} | all-to-all | bytes 393216 | tf_op jit(solution)/shard_map/all_to_all | solution.py:452
  43.0 0.9 %reduce.1 = f32[32,4,128]{2,1,0:T(4,128)} custom-call(f32[16,8,384]{2,1,0:T(8,128)S(1)} %all_to_all.10.got_ref.refs_0_), custom_call_target="tpu_custom_call" | custom-call | tf_op jit(solution)/shard_map/reduce/pallas_call | solution.py:453
  44.0 10.5 %all-to-all-start.1 = ((f32[32,4,128]{2,1,0:T(4,128)}), f32[32,4,128]{2,1,0:T(4,128)S(1)}, u32[]{:S(2)}, u32[]{:S(2)}) async-start(f32[32,4,128]{2,1,0:T(4,128)} %reduce.1), calls=%async_computation.1 | async-start | bytes 131072 | tf_op jit(solution)/shard_map/all_to_all | solution.py:461
  54.5 1.2 %relay.1.refs_1_ = f32[20,8,256]{2,1,0:T(8,128)S(1)} custom-call(f32[16,8,384]{2,1,0:T(8,128)S(1)} %all_to_all.10.got_ref.refs_0_), custom_call_target="tpu_custom_call" | custom-call | tf_op jit(solution)/shard_map/relay/pallas_call | solution.py:462
  55.7 6.8 %all-to-all-done.1.refs_0_ = f32[32,4,128]{2,1,0:T(4,128)S(1)} async-done(((f32[32,4,128]{2,1,0:T(4,128)}), f32[32,4,128]{2,1,0:T(4,128)S(1)}, u32[]{:S(2)}, u32[]{:S(2)}) %all-to-all-start.1) | async-done | bytes 65568 | tf_op jit(solution)/shard_map/all_to_all | solution.py:461
  62.6 1.6 %final.1 = f32[20,8,256]{2,1,0:T(8,128)} custom-call(f32[32,4,128]{2,1,0:T(4,128)S(1)} %all-to-all-done.1.refs_0_, f32[20,8,256]{2,1,0:T(8,128)S(1)} %relay.1.refs_1_), custom_call_target="tpu_custom_call" | custom-call | tf_op jit(solution)/shard_map/final/pallas_call | solution.py:471
  (5 shorter events, 0.1 us)
Async XLA Ops:
  0.0 6.6 %copy-start.2 = (f32[1,10,10]{2,0,1:T(1,128)S(1)}, f32[1,10,10]{2,0,1:T(1,128)}, u32[]{:S(2)}) copy-start(f32[1,10,10]{2,0,1:T(1,128)} %param.6) | copy-start | bytes 1204
  0.0 1.0 %copy-start = (f32[101,2,16]{0,2,1:T(8,128)S(1)}, f32[101,2,16]{0,2,1:T(8,128)}, u32[]{:S(2)}) copy-start(f32[101,2,16]{0,2,1:T(8,128)} %param.5) | copy-start | bytes 38788
  0.0 16.4 %copy-start.1 = (f32[2,5,2,16,128]{4,3,2,1,0:T(8,128)S(1)}, f32[2,5,2,16,128]{4,3,2,1,0:T(8,128)}, u32[]{:S(2)}) copy-start(f32[2,5,2,16,128]{4,3,2,1,0:T(8,128)} %param.4) | copy-start | bytes 491524
  1.0 15.4 %collective-permute-start = (f32[11,2,4,128]{3,2,1,0:T(4,128)S(1)}, f32[11,2,4,128]{3,2,1,0:T(4,128)S(1)}, u32[]{:S(2)}, u32[]{:S(2)}) collective-permute-start(f32[11,2,4,128]{3,2,1,0:T(4,128)S(1)} %get-tuple-element.9), channel_id=1, source_target_pairs={{0,1},{1,2},{2,3},{3,4},{4,5},{5,6},{6,7},{7,8},{8,9},{9,10},{10,1... | collective-permute-start | bytes 135176 | tf_op jit(solution)/shard_map/ppermute | solution.py:421
  16.5 8.3 %collective-permute-start.2 = (f32[11,40,128]{2,1,0:T(8,128)S(1)}, f32[11,40,128]{2,1,0:T(8,128)S(1)}, u32[]{:S(2)}, u32[]{:S(2)}) collective-permute-start(f32[11,40,128]{2,1,0:T(8,128)S(1)} %reshape.10.refs_1_), channel_id=1, source_target_pairs={{16,32},{32,16},{48,64},{64,48},{80,96},{96,80},{112,128},{128,112... | collective-permute-start | bytes 675848 | tf_op jit(solution)/shard_map/ppermute | solution.py:427
  21.1 3.6 %collective-permute-start.1 = (f32[11,40,128]{2,1,0:T(8,128)S(1)}, f32[11,40,128]{2,1,0:T(8,128)S(1)}, u32[]{:S(2)}, u32[]{:S(2)}) collective-permute-start(f32[11,40,128]{2,1,0:T(8,128)S(1)} %reshape.10.refs_1_), channel_id=1, source_target_pairs={{0,16},{16,0},{32,48},{48,32},{64,80},{80,64},{96,112},{112,96},{1... | collective-permute-start | bytes 675848 | tf_op jit(solution)/shard_map/ppermute | solution.py:428
  44.0 18.6 %all-to-all-start.1 = ((f32[32,4,128]{2,1,0:T(4,128)}), f32[32,4,128]{2,1,0:T(4,128)S(1)}, u32[]{:S(2)}, u32[]{:S(2)}) async-start(f32[32,4,128]{2,1,0:T(4,128)} %reduce.1), calls=%async_computation.1 | async-start | bytes 131072 | tf_op jit(solution)/shard_map/all_to_all | solution.py:461
